TPU v7x, 32 devices: a whole 2x2x4 slice. The times are simulated.
32 devices in a mesh: rep: 2 (over y), ep: 4 (over z), node: 2 (over x), sub: 2 (over core).
Axes of the slice: x: 2, y: 2, z: 4, core: 2. Of those that a mesh axis runs over, the one named last changes fastest.
Arguments:
- tokens: bfloat16 [1024, 7168], P(('rep', 'ep', 'node'), 'sub'), parts along dimension 0, may hold values from -6 to 6
- routes: int32 [1024, 2], P(('rep', 'ep', 'node')), parts along dimension 0, may hold values from 0 to 3, all different within a row; in each aligned block of 64 rows (0 to 63, 64 to 127, ...) at most 40 rows name the same one
- tenant: int32 [1024], P(('rep', 'ep', 'node')), parts along dimension 0, may hold values from 0 to 7
- expert_place: int32 [4], replicated, may hold values from 0 to 3, each once
- router_weight: bfloat16 [7168, 4], P('sub'), may hold values from -0.0625 to 0.0625
- adapter_down: bfloat16 [7168, 128], P('sub'), may hold values from -0.0625 to 0.0625
- adapter_up: bfloat16 [128, 4], replicated, may hold values from -1.5 to 1.5
- gate_weight: bfloat16 [4, 7168, 1024], P('ep', 'sub', 'node'), may hold values from -0.0625 to 0.0625
- up_weight: bfloat16 [4, 7168, 1024], P('ep', 'sub', 'node'), may hold values from -0.0625 to 0.0625
- down_weight: bfloat16 [4, 2, 1024, 3584], P('ep', 'sub', None, 'node'), may hold values from -0.1875 to 0.1875
Outputs:
- mixed: bfloat16 [1024, 7168], P(('rep', 'ep', 'node'), 'sub'), parts along dimension 0
There are 2 independent parts, one for each index of `rep`. A program takes and returns all parts, laid end to end along the dimension named above; an argument that names none is the same for every part. Nothing has to cross between parts.
Inputs may be any that keep to these rules, and one draw needn't show every extreme that they name: `routes`: each row names 2 different experts. Within the rows of one device (aligned blocks of 64 rows) no expert is named by more than 40 rows, a bound that some block reaches. `expert_place`: A permutation: each index of ep holds exactly one expert.
All inputs are finite; a program needn't handle non-finite values.
Results may differ from a plain program's by a relative error of at most 0.0057.
Values may be sent and summed in bfloat16 or wider, within the bound.
No kernel may reach another device: no remote copies, remote signals or barrier semaphores. Data moves between devices by JAX's collectives and lax.ppermute only.
A program may use at most 128 MiB of HBM per device.

v0:
```python
import jax
import jax.numpy as jnp
from jax import lax
from jax.sharding import PartitionSpec as P

RANK = 16


route_scale = 2.5


def body(
    tokens,
    routes,
    tenant,
    expert_place,
    router_weight,
    adapter_down,
    adapter_up,
    gate_weight,
    up_weight,
    down_weight,
):
    tok_rows, half_width = tokens.shape
    topk = routes.shape[1]
    experts = router_weight.shape[1]
    ep_count = lax.axis_size("ep")
    node_count = lax.axis_size("node")
    capacity = 5 * tok_rows * topk // (4 * ep_count)
    hidden_dev = gate_weight.shape[2]
    out_width = down_weight.shape[3]
    base = jnp.dot(tokens, router_weight, preferred_element_type=jnp.float32)
    lowrank = jnp.dot(tokens, adapter_down, preferred_element_type=jnp.float32)
    column_owner = lax.broadcasted_iota(jnp.int32, (1, adapter_down.shape[1]), 1) // RANK
    lowrank = jnp.where(column_owner == tenant[:, None], lowrank, jnp.float32(0.0))
    partial_logits = base + jnp.dot(
        lowrank, adapter_up.astype(jnp.float32), precision=lax.Precision.HIGHEST
    )
    logits = lax.psum(partial_logits, "sub")
    flat = routes.reshape(-1)
    onehot = (flat[:, None] == lax.broadcasted_iota(jnp.int32, (1, experts), 1)).astype(jnp.int32)
    picked = jnp.sum(onehot.astype(jnp.float32) * jnp.repeat(logits, topk, axis=0), axis=1).reshape(
        tok_rows, topk
    )
    score = jax.nn.sigmoid(picked)
    weight = route_scale * score / jnp.sum(score, axis=1, keepdims=True)
    rank = jnp.sum((jnp.cumsum(onehot, axis=0) - 1) * onehot, axis=1)
    slot = jnp.sum(onehot * expert_place[None, :], axis=1)
    position = slot * capacity + rank
    group_rows = ep_count * capacity
    placing = (position[None, :] == lax.broadcasted_iota(jnp.int32, (group_rows, 1), 0)).astype(
        jnp.bfloat16
    )
    repeated = jnp.repeat(tokens, topk, axis=0)
    outgoing = jnp.dot(placing, repeated, preferred_element_type=jnp.float32).astype(jnp.bfloat16)
    outgoing = outgoing.reshape(ep_count, capacity, half_width)
    spread = jnp.broadcast_to(outgoing[:, None], (ep_count, node_count, capacity, half_width))
    spread = spread.reshape(ep_count * node_count, capacity, half_width)
    arrived = lax.all_to_all(spread, ("ep", "node"), split_axis=0, concat_axis=0, tiled=True)
    flat_rows = arrived.reshape(-1, half_width)
    gate = jnp.dot(flat_rows, gate_weight[0], preferred_element_type=jnp.float32)
    up = jnp.dot(flat_rows, up_weight[0], preferred_element_type=jnp.float32)
    partial_value = jnp.concatenate([gate, up], axis=1)
    total = lax.psum(partial_value, "sub")
    hidden = (jax.nn.silu(total[:, :hidden_dev]) * total[:, hidden_dev:]).astype(jnp.bfloat16)
    down_local = down_weight[0, 0]
    folded = jnp.dot(
        lax.all_gather(hidden, "node", axis=1, tiled=True),
        down_local,
        preferred_element_type=jnp.float32,
    )
    expert_out = folded.astype(jnp.bfloat16).reshape(ep_count, node_count, capacity, out_width)
    columns = lax.all_to_all(expert_out, "node", split_axis=1, concat_axis=3, tiled=True)
    returned = columns.reshape(ep_count, capacity, half_width)
    back = lax.all_to_all(returned, "ep", split_axis=0, concat_axis=0, tiled=True).reshape(
        group_rows, half_width
    )
    chosen = jnp.dot(placing.T, back, preferred_element_type=jnp.float32)
    mixed = jnp.sum(chosen.reshape(tok_rows, topk, half_width) * weight[:, :, None], axis=1)
    return mixed.astype(jnp.bfloat16)


def solution(mesh):
    placed = (
        P(("rep", "ep", "node"), "sub"),
        P(("rep", "ep", "node"), None),
        P(("rep", "ep", "node")),
        P(),
        P("sub", None),
        P("sub", None),
        P(),
        P("ep", "sub", "node"),
        P("ep", "sub", "node"),
        P("ep", "sub", None, "node"),
    )
    return jax.shard_map(
        body, mesh=mesh, in_specs=placed, out_specs=P(("rep", "ep", "node"), "sub"), check_vma=False
    )
```

profile of v0, /device:TPU:0, one launch (start us, length us, event | category | flops | bytes accessed | tf_op | source)
XLA Modules:
  0.0 169.0 jit_solution(13380539462013915515)
XLA Ops:
  6.5 0.0 copy-start
  6.5 0.0 copy-start.5
  6.5 0.0 all-reduce.2.cloned.1.call-start
  6.5 0.9 copy.26
  7.4 0.1 eq.67
  7.5 0.1 fusion.14
  7.6 1.5 broadcast_in_dim.22
  9.1 0.3 reshape.125
  9.5 0.2 reduce_window_sum.11
  9.7 0.0 copy-done.5
  9.7 0.2 select_reduce_fusion.1
  9.9 0.4 convolution_convert_fusion
  10.3 0.2 broadcast_in_dim.24
  10.5 0.0 copy-start.7
  10.5 59.9 %all_to_all.25 = bf16[8,40,3584]{2,1,0:T(8,128)(2,1)S(1)} all-to-all(bf16[8,40,3584]{2,1,0:T(8,128)(2,1)S(1)} %bitcast.37), channel_id=1, replica_groups=mesh['rep'=2,'ep'=4,'node'=2,'sub'=2] {'ep','node'}, dimensions={0} | all-to-all | bytes 4587520 | tf_op jit(solution)/shard_map/all_to_all | solution.py:59
  70.4 0.0 copy-done.7
  70.4 0.0 copy-start.8
  70.4 1.3 fusion.2
  71.7 0.7 copy-done.8
  72.4 1.3 fusion.4
  73.7 1.2 pad_maximum_fusion
  74.9 0.0 all-reduce.2.cloned.1.call-update
  75.0 19.1 %all-reduce.2.cloned.1.call-done = f32[320,1024]{1,0:T(8,128)} async-done(((f32[320,1024]{1,0:T(8,128)}), f32[320,1024]{1,0:T(8,128)}) %all-reduce.2.cloned.1.call-update) | async-done | bytes 1310736 | tf_op jit(solution)/shard_map/psum | solution.py:64
  94.0 1.5 fusion.10
  95.5 10.6 %all_gather.3 = bf16[320,1024]{1,0:T(8,128)(2,1)S(1)} all-gather(bf16[320,512]{1,0:T(8,128)(2,1)S(1)} %fusion.10), channel_id=1, replica_groups=mesh['rep'=2,'ep'=4,'node'=2,'sub'=2] {'node'}, dimensions={1}, use_global_device_ids=true | all-gather | bytes 983040 | tf_op jit(solution)/shard_map/all_gather | solution.py:68
  106.1 3.4 %fusion.6 = bf16[320,1792]{1,0:T(8,128)(2,1)S(1)} fusion(bf16[320,1024]{1,0:T(8,128)(2,1)S(1)} %all_gather.3, bf16[1,1,1024,1792]{3,2,1,0:T(8,128)(2,1)} %param.19), kind=kOutput, calls=%fused_computation.8 | convolution fusion | flops 1174978560 | bytes 5472256 | tf_op jit(solution)/shard_map/dot_general | solution.py:67
  109.5 0.1 copy.28
  109.6 17.1 %all_to_all.26 = bf16[4,2,40,1792]{3,2,0,1:T(8,128)(2,1)S(1)} all-to-all(bf16[4,2,40,1792]{3,2,0,1:T(8,128)(2,1)S(1)} %copy.28), channel_id=1, replica_groups=mesh['rep'=2,'ep'=4,'node'=2,'sub'=2] {'node'}, dimensions={1} | all-to-all | bytes 2293760 | tf_op jit(solution)/shard_map/all_to_all | solution.py:73
  126.7 1.2 copy.29
  127.9 0.0 copy-start.1
  127.9 0.0 copy-start.2
  127.9 0.0 copy-start.6
  127.9 1.6 reshape.129
  129.5 4.9 %all-to-all-start.2 = ((bf16[4,40,3584]{2,1,0:T(8,128)(2,1)}), bf16[4,40,3584]{2,1,0:T(8,128)(2,1)S(1)}, u32[]{:S(2)}, u32[]{:S(2)}) async-start(bf16[4,40,3584]{2,1,0:T(8,128)(2,1)} %reshape.129), calls=%async_computation.2 | async-start | bytes 2293760 | tf_op jit(solution)/shard_map/all_to_all | solution.py:75
  134.4 0.1 add.37
  134.5 0.1 copy.27
  134.6 0.0 copy-done.1
  134.6 0.0 copy-done.2
  134.6 0.2 fusion.17
  134.8 0.0 copy-done
  134.8 0.0 copy-done.6
  134.8 0.3 convolution_select_fusion
  135.2 0.0 copy-done.4
  135.2 0.1 convolution_add_fusion
  135.3 2.5 %psum.15 = f32[64,4]{0,1:T(4,128)S(1)} all-reduce(f32[64,4]{0,1:T(4,128)S(1)} %convolution_add_fusion), channel_id=1, replica_groups=mesh['rep'=2,'ep'=4,'node'=2,'sub'=2] {'sub'}, use_global_device_ids=true, to_apply=%region_4.5 | all-reduce | flops 256 | bytes 2048 | tf_op jit(solution)/shard_map/psum | solution.py:39
  137.8 0.0 copy-done.3
  137.9 23.0 %all-to-all-done.2 = bf16[4,40,3584]{2,1,0:T(8,128)(2,1)S(1)} async-done(((bf16[4,40,3584]{2,1,0:T(8,128)(2,1)}), bf16[4,40,3584]{2,1,0:T(8,128)(2,1)S(1)}, u32[]{:S(2)}, u32[]{:S(2)}) %all-to-all-start.2) | async-done | bytes 1146912 | tf_op jit(solution)/shard_map/all_to_all | solution.py:75
  160.9 1.2 fusion.9
  (7 shorter events, 0.1 us)
Async XLA Ops:
  6.5 128.3 %copy-start = (bf16[3584,128]{1,0:T(8,128)(2,1)S(1)}, bf16[3584,128]{1,0:T(8,128)(2,1)}, u32[]{:S(2)}) copy-start(bf16[3584,128]{1,0:T(8,128)(2,1)} %param.15) | copy-start | bytes 2752516
  6.5 3.1 %copy-start.5 = (s32[4]{0:T(128)S(1)}, s32[4]{0:T(128)}, u32[]{:S(2)}) copy-start(s32[4]{0:T(128)} %param.13) | copy-start | bytes 52
  6.5 87.5 %all-reduce.2.cloned.1.call-start = ((), (), s32[]{:S(2)}) async-start(), calls=%async_computation.3 | async-start | bytes 2621440 | tf_op jit(solution)/shard_map/psum | solution.py:64
  10.5 59.9 %copy-start.7 = (bf16[1,3584,512]{2,1,0:T(8,128)(2,1)S(1)}, bf16[1,3584,512]{2,1,0:T(8,128)(2,1)}, u32[]{:S(2)}) copy-start(bf16[1,3584,512]{2,1,0:T(8,128)(2,1)} %param.18) | copy-start | bytes 11010052
  70.4 2.0 %copy-start.8 = (bf16[1,3584,512]{2,1,0:T(8,128)(2,1)S(1)}, bf16[1,3584,512]{2,1,0:T(8,128)(2,1)}, u32[]{:S(2)}) copy-start(bf16[1,3584,512]{2,1,0:T(8,128)(2,1)} %param.17) | copy-start | bytes 11010052
  127.9 6.8 %copy-start.1 = (bf16[64,3584]{1,0:T(8,128)(2,1)S(1)}, bf16[64,3584]{1,0:T(8,128)(2,1)}, u32[]{:S(2)}) copy-start(bf16[64,3584]{1,0:T(8,128)(2,1)} %param.10) | copy-start | bytes 1376260
  127.9 6.7 %copy-start.2 = (bf16[3584,4]{0,1:T(4,128)(2,1)S(1)}, bf16[3584,4]{0,1:T(4,128)(2,1)}, u32[]{:S(2)}) copy-start(bf16[3584,4]{0,1:T(4,128)(2,1)} %param.14) | copy-start | bytes 86020
  127.9 7.0 %copy-start.6 = (s32[64]{0:T(128)S(1)}, s32[64]{0:T(128)}, u32[]{:S(2)}) copy-start(s32[64]{0:T(128)} %param.12) | copy-start | bytes 772
  129.5 5.7 %copy-start.4 = (bf16[128,4]{0,1:T(4,128)(2,1)S(1)}, bf16[128,4]{0,1:T(4,128)(2,1)}, u32[]{:S(2)}) copy-start(bf16[128,4]{0,1:T(4,128)(2,1)} %param.16) | copy-start | bytes 3076
  129.5 8.3 %copy-start.3 = (s32[64,2]{0,1:T(2,128)S(1)}, s32[64,2]{0,1:T(2,128)}, u32[]{:S(2)}) copy-start(s32[64,2]{0,1:T(2,128)} %param.11) | copy-start | bytes 1540
  129.5 31.4 %all-to-all-start.2 = ((bf16[4,40,3584]{2,1,0:T(8,128)(2,1)}), bf16[4,40,3584]{2,1,0:T(8,128)(2,1)S(1)}, u32[]{:S(2)}, u32[]{:S(2)}) async-start(bf16[4,40,3584]{2,1,0:T(8,128)(2,1)} %reshape.129), calls=%async_computation.2 | async-start | bytes 2293760 | tf_op jit(solution)/shard_map/all_to_all | solution.py:75
Sparse Core Ops, SparseCore 0:
  75.1 18.9 all-reduce.1
where the time goes:
time: 169 us
  blocking collectives  90 us (53%)
  waiting for transfers between devices  42.1 us (25%)
  between operations  13.5 us (8%)
  matrix products  8.41 us (5%)
  local copies, waits for them, and re-layouts  6.77 us (4%)
  starting transfers between devices  4.93 us (3%)
  other arithmetic  3.17 us (2%)
    all_to_all x1, blocking collectives, body(): lax.all_to_all(spread, ('ep', 'node'), split_axis=0, concat_axis=0, tiled...  59.9 us
    all_to_all x1, waiting for transfers between devices, body(): lax.all_to_all(returned, 'ep', split_axis=0, concat_axis=0, tiled=True)  23 us
    psum x1, waiting for transfers between devices, body(): total = lax.psum(partial_value, 'sub')  19.1 us
    all_to_all x1, blocking collectives, body(): lax.all_to_all(expert_out, 'node', split_axis=1, concat_axis=3, tiled=True)  17.1 us
    all_gather x1, blocking collectives, body(): lax.all_gather(hidden, 'node', axis=1, tiled=True)  10.6 us
    all_to_all x1, starting transfers between devices, body(): lax.all_to_all(returned, 'ep', split_axis=0, concat_axis=0, tiled=True)  4.92 us
    dot_general x1, matrix products, body(): jnp.dot(lax.all_gather(hidden, 'node', axis=1, tiled=True), down_local, p...  3.39 us
  transfers between devices with their start and end apart: 2, of which 2 were waited for; matrix products, arithmetic and copies ran while one was open for 1% of the time, Pallas kernels for 0%

commit v1 on v0

v1 whole, which is shorter than its diff:
```python
import jax
import jax.numpy as jnp
from jax import lax
from jax.sharding import PartitionSpec as P

RANK = 16
ROUTE_SCALE = 2.5
f32 = jnp.float32
bf16 = jnp.bfloat16


def partner(index, step):
    return index ^ step


def swap(value, axis, step):
    count = lax.axis_size(axis)
    return lax.ppermute(value, axis, [(i, partner(i, step)) for i in range(count)])


def in_index_order(parts, index):
    parts = list(parts)
    bit = 1
    while bit < len(parts):
        flip = (index & bit) != 0
        parts = [jnp.where(flip, parts[j ^ bit], parts[j]) for j in range(len(parts))]
        bit *= 2
    return parts


def after(value, *others):
    return lax.optimization_barrier((value,) + others)[0]


def body(
    tokens,
    routes,
    tenant,
    expert_place,
    router_weight,
    adapter_down,
    adapter_up,
    gate_weight,
    up_weight,
    down_weight,
):
    tok_rows, half_width = tokens.shape
    topk = routes.shape[1]
    experts = router_weight.shape[1]
    eps = lax.axis_size("ep")
    nodes = lax.axis_size("node")
    cap = 5 * tok_rows * topk // (4 * eps)
    hidden_dev = gate_weight.shape[2]
    out_width = down_weight.shape[3]
    ep_me = lax.axis_index("ep")
    node_me = lax.axis_index("node")

    expert_of_block = jnp.argmax(
        expert_place[None, :] == (jnp.arange(eps, dtype=jnp.int32) ^ ep_me)[:, None], axis=1
    ).astype(jnp.int32)
    routes_t = routes.T
    named = jnp.any(routes_t[None] == expert_of_block[:, None, None], axis=1)
    earlier = (
        lax.broadcasted_iota(jnp.int32, (tok_rows, tok_rows), 0)
        < lax.broadcasted_iota(jnp.int32, (tok_rows, tok_rows), 1)
    ).astype(bf16)
    before = jnp.dot(named.astype(bf16), earlier, preferred_element_type=f32)
    place = jnp.where(named, before, f32(-1.0))
    row = lax.broadcasted_iota(jnp.int32, (1, cap, 1), 1).astype(f32)
    placing = (place[:, None, :] == row).astype(bf16).reshape(eps * cap, tok_rows)
    outgoing = jnp.dot(placing, tokens, preferred_element_type=f32).astype(bf16)
    outgoing = outgoing.reshape(eps, cap, half_width)

    order = list(range(eps))
    mine = [outgoing[0]] + [None] * (eps - 1)
    for k in order[1:]:
        mine[k] = swap(outgoing[k], "ep", k)
    blocks = []
    for k in order:
        blocks.append([mine[k]] + [swap(mine[k], "node", j) for j in range(1, nodes)])

    gate_w, up_w, down_w = gate_weight[0], up_weight[0], down_weight[0, 0]
    chunks = CHUNKS(eps)
    returned = [None] * eps
    for chunk in chunks:
        rows = jnp.concatenate([blocks[k][j] for j in range(nodes) for k in chunk], axis=0)
        gate = jnp.dot(rows, gate_w, preferred_element_type=f32)
        up = jnp.dot(rows, up_w, preferred_element_type=f32)
        theirs = swap(jnp.concatenate([gate.astype(bf16), up.astype(bf16)], axis=1), "sub", 1)
        gate = gate + theirs[:, :hidden_dev].astype(f32)
        up = up + theirs[:, hidden_dev:].astype(f32)
        hidden = (jax.nn.silu(gate) * up).astype(bf16)
        groups = hidden.reshape(nodes, len(chunk) * cap, hidden_dev)
        by_node = [hidden]
        for i in range(1, nodes):
            got = swap(groups, "node", i)
            by_node.append(jnp.concatenate([got[j ^ i] for j in range(nodes)], axis=0))
        full = jnp.concatenate(in_index_order(by_node, node_me), axis=1)
        out = jnp.dot(full, down_w, preferred_element_type=f32).astype(bf16)
        out = out.reshape(nodes, len(chunk), cap, out_width)
        for i, k in enumerate(chunk):
            part = out[:, i]
            returned[k] = part if k == 0 else swap(part, "ep", k)

    base = jnp.dot(tokens, router_weight, preferred_element_type=f32)
    lowrank = jnp.dot(tokens, adapter_down, preferred_element_type=f32)
    column_owner = lax.broadcasted_iota(jnp.int32, (1, adapter_down.shape[1]), 1) // RANK
    lowrank = jnp.where(column_owner == tenant[:, None], lowrank, f32(0.0))
    logits = base + jnp.dot(lowrank, adapter_up.astype(f32), precision=lax.Precision.HIGHEST)
    logits = logits + swap(logits, "sub", 1)
    score = jax.nn.sigmoid(logits).T
    chosen = jnp.any(
        routes_t[None] == lax.broadcasted_iota(jnp.int32, (experts, 1, 1), 0), axis=1
    )
    score = jnp.where(chosen, score, f32(0.0))
    weight = ROUTE_SCALE * score / jnp.sum(score, axis=0, keepdims=True)
    to_block = expert_of_block[:, None] == jnp.arange(experts, dtype=jnp.int32)[None, :]
    weight = jnp.sum(jnp.where(to_block[:, :, None], weight[None], f32(0.0)), axis=1)
    info = jnp.stack([place, weight])
    infos = [info] + [swap(info, "node", j) for j in range(1, nodes)]

    back = jnp.stack(returned, axis=1).reshape(nodes, eps * cap, out_width)
    mixed = []
    for j in range(nodes):
        hit = infos[j][0][:, None, :] == row
        weighted = jnp.where(hit, infos[j][1][:, None, :], f32(0.0)).reshape(eps * cap, tok_rows)
        high = weighted.astype(bf16)
        low = (weighted - high.astype(f32)).astype(bf16)
        dims = (((0,), (0,)), ((), ()))
        total = lax.dot_general(high, back[j], dims, preferred_element_type=f32)
        total = total + lax.dot_general(low, back[j], dims, preferred_element_type=f32)
        part = total.astype(bf16)
        mixed.append(part if j == 0 else swap(part, "node", j))
    return jnp.concatenate(in_index_order(mixed, node_me), axis=1)


def CHUNKS(eps):
    return [list(range(eps))]


def solution(mesh):
    placed = (
        P(("rep", "ep", "node"), "sub"),
        P(("rep", "ep", "node"), None),
        P(("rep", "ep", "node")),
        P(),
        P("sub", None),
        P("sub", None),
        P(),
        P("ep", "sub", "node"),
        P("ep", "sub", "node"),
        P("ep", "sub", None, "node"),
    )
    return jax.shard_map(
        body, mesh=mesh, in_specs=placed, out_specs=P(("rep", "ep", "node"), "sub"), check_vma=False
    )
```

time: 169 us -> 95.3 us (0.56)
  the two profiles are of different devices: /device:TPU:0 before, /device:TPU:8 now
where the time goes in v1:
time: 95.3 us; the launch traced here: 95.1 us
  waiting for transfers between devices  63.2 us (66%)
  starting transfers between devices  16.9 us (18%)
  matrix products  9.37 us (10%)
  other arithmetic  4.1 us (4%)
  local copies, waits for them, and re-layouts  1.22 us (1%)
    ppermute x15, waiting for transfers between devices, swap(): lax.ppermute(value, axis, [(i, partner(i, step)) for i in range(count)])  63.2 us
    ppermute x15, starting transfers between devices, swap(): lax.ppermute(value, axis, [(i, partner(i, step)) for i in range(count)])  16.9 us
    dot_general x1, matrix products, body(): out = jnp.dot(full, down_w, preferred_element_type=f32).astype(bf16)  3.39 us
  transfers between devices with their start and end apart: 15, of which 10 were waited for; matrix products, arithmetic and copies ran while one was open for 4% of the time, Pallas kernels for 0%

profile of v1, /device:TPU:8, one launch (start us, length us, event | category | flops | bytes accessed | tf_op | source)
XLA Modules:
  0.0 95.1 jit_solution(13852134816825838755)
XLA Ops:
  0.0 1.5 %iota_reduce_fusion = (pred[4]{0:T(512)(128)(4,1)}, s32[4]{0:T(128)S(1)}) fusion(s32[4]{0:T(128)} %param.13, s32[4]{0:T(128)S(1)} %iota_xor_fusion), kind=kLoop, calls=%fused_computation.59 | loop fusion | flops 100 | bytes 52 | tf_op jit(solution)/shard_map/body/reduce | solution.py:58
  1.5 0.8 compare_reduce_fusion
  2.3 0.1 convolution_select_fusion.1
  2.4 0.1 eq.166
  2.5 0.1 bitcast_compare_fusion
  2.6 1.5 %convolution_convert_fusion = bf16[160,3584]{1,0:T(8,128)(2,1)S(1)} fusion(pred[160,64]{1,0:T(32,128)(4,1)S(1)} %bitcast_compare_fusion, bf16[64,3584]{1,0:T(8,128)(2,1)} %param.10), kind=kOutput, calls=%fused_computation | convolution fusion | flops 73973760 | bytes 1615872 | tf_op jit(solution)/shard_map/dot_general | solution.py:71
  4.1 0.1 fusion.20
  4.2 3.0 %collective-permute-start.3 = (bf16[40,3584]{1,0:T(8,128)(2,1)S(1)}, bf16[40,3584]{1,0:T(8,128)(2,1)S(1)}, u32[]{:S(2)}, u32[]{:S(2)}) collective-permute-start(bf16[40,3584]{1,0:T(8,128)(2,1)S(1)} %get-tuple-element.20), channel_id=1, source_target_pairs={{0,8},{4,12},{8,0},{12,4},{1,9},{5,13},{9,1},{13,5},{2,10},{6,14},... | collective-permute-start | bytes 860168 | tf_op jit(solution)/shard_map/ppermute | solution.py:18
  7.3 0.4 collective-permute-start.4
  7.7 1.5 %collective-permute-start.5 = (bf16[40,3584]{1,0:T(8,128)(2,1)S(1)}, bf16[40,3584]{1,0:T(8,128)(2,1)S(1)}, u32[]{:S(2)}, u32[]{:S(2)}) collective-permute-start(bf16[40,3584]{1,0:T(8,128)(2,1)S(1)} %get-tuple-element.17), channel_id=1, source_target_pairs={{0,2},{2,0},{1,3},{3,1},{4,6},{6,4},{5,7},{7,5},{8,10},{10,8},{9,1... | collective-permute-start | bytes 860168 | tf_op jit(solution)/shard_map/ppermute | solution.py:18
  9.2 0.3 convolution_select_fusion
  9.6 0.2 fusion.23
  9.8 0.1 convolution_add_fusion.2
  9.9 6.1 %collective-permute-done.2 = bf16[40,3584]{1,0:T(8,128)(2,1)S(1)} collective-permute-done((bf16[40,3584]{1,0:T(8,128)(2,1)S(1)}, bf16[40,3584]{1,0:T(8,128)(2,1)S(1)}, u32[]{:S(2)}, u32[]{:S(2)}) %collective-permute-start.2) | collective-permute-done | bytes 286752 | tf_op jit(solution)/shard_map/ppermute | solution.py:18
  16.0 1.7 %collective-permute-start.6 = (bf16[40,3584]{1,0:T(8,128)(2,1)S(1)}, bf16[40,3584]{1,0:T(8,128)(2,1)S(1)}, u32[]{:S(2)}, u32[]{:S(2)}) collective-permute-start(bf16[40,3584]{1,0:T(8,128)(2,1)S(1)} %collective-permute-done.2), channel_id=1, source_target_pairs={{0,2},{2,0},{1,3},{3,1},{4,6},{6,4},{5,7},{7,5},{8,10},{10,8},{9,1... | collective-permute-start | bytes 860168 | tf_op jit(solution)/shard_map/ppermute | solution.py:18
  17.7 9.2 %collective-permute-done.3 = bf16[40,3584]{1,0:T(8,128)(2,1)S(1)} collective-permute-done((bf16[40,3584]{1,0:T(8,128)(2,1)S(1)}, bf16[40,3584]{1,0:T(8,128)(2,1)S(1)}, u32[]{:S(2)}, u32[]{:S(2)}) %collective-permute-start.3) | collective-permute-done | bytes 286752 | tf_op jit(solution)/shard_map/ppermute | solution.py:18
  26.8 1.5 %collective-permute-start.7 = (bf16[40,3584]{1,0:T(8,128)(2,1)S(1)}, bf16[40,3584]{1,0:T(8,128)(2,1)S(1)}, u32[]{:S(2)}, u32[]{:S(2)}) collective-permute-start(bf16[40,3584]{1,0:T(8,128)(2,1)S(1)} %collective-permute-done.3), channel_id=1, source_target_pairs={{0,2},{2,0},{1,3},{3,1},{4,6},{6,4},{5,7},{7,5},{8,10},{10,8},{9,1... | collective-permute-start | bytes 860168 | tf_op jit(solution)/shard_map/ppermute | solution.py:18
  28.3 4.1 %collective-permute-done.4 = bf16[40,3584]{1,0:T(8,128)(2,1)S(1)} collective-permute-done((bf16[40,3584]{1,0:T(8,128)(2,1)S(1)}, bf16[40,3584]{1,0:T(8,128)(2,1)S(1)}, u32[]{:S(2)}, u32[]{:S(2)}) %collective-permute-start.4) | collective-permute-done | bytes 286752 | tf_op jit(solution)/shard_map/ppermute | solution.py:18
  32.5 1.5 %collective-permute-start.8 = (bf16[40,3584]{1,0:T(8,128)(2,1)S(1)}, bf16[40,3584]{1,0:T(8,128)(2,1)S(1)}, u32[]{:S(2)}, u32[]{:S(2)}) collective-permute-start(bf16[40,3584]{1,0:T(8,128)(2,1)S(1)} %collective-permute-done.4), channel_id=1, source_target_pairs={{0,2},{2,0},{1,3},{3,1},{4,6},{6,4},{5,7},{7,5},{8,10},{10,8},{9,1... | collective-permute-start | bytes 860168 | tf_op jit(solution)/shard_map/ppermute | solution.py:18
  34.1 5.8 %collective-permute-done.8 = bf16[40,3584]{1,0:T(8,128)(2,1)S(1)} collective-permute-done((bf16[40,3584]{1,0:T(8,128)(2,1)S(1)}, bf16[40,3584]{1,0:T(8,128)(2,1)S(1)}, u32[]{:S(2)}, u32[]{:S(2)}) %collective-permute-start.8) | collective-permute-done | bytes 286752 | tf_op jit(solution)/shard_map/ppermute | solution.py:18
  39.9 1.3 %fusion.21 = (bf16[320,512]{1,0:T(8,128)(2,1)S(1)}, f32[320,512]{1,0:T(8,128)S(1)}) fusion(bf16[320,3584]{1,0:T(8,128)(2,1)S(1)} %constant_dynamic-update-slice_fusion, bf16[1,3584,512]{2,1,0:T(8,128)(2,1)S(1)} %copy-done.5), kind=kOutput, calls=%fused_computation.70 | convolution fusion | flops 1174568960 | bytes 6946816 | tf_op jit(solution)/shard_map/dot_general | solution.py:88
  41.3 0.7 copy-done.6
  42.0 1.3 %fusion.22 = (bf16[320,512]{1,0:T(8,128)(2,1)S(1)}, f32[320,512]{1,0:T(8,128)S(1)}) fusion(bf16[320,3584]{1,0:T(8,128)(2,1)S(1)} %constant_dynamic-update-slice_fusion, bf16[1,3584,512]{2,1,0:T(8,128)(2,1)S(1)} %copy-done.6), kind=kOutput, calls=%fused_computation.71 | convolution fusion | flops 1174568960 | bytes 6946816 | tf_op jit(solution)/shard_map/dot_general | solution.py:87
  43.6 0.1 select_reduce_fusion
  43.7 1.9 %collective-permute-done.9 = bf16[320,1024]{1,0:T(8,128)(2,1)S(1)} collective-permute-done((bf16[320,1024]{1,0:T(8,128)(2,1)S(1)}, bf16[320,1024]{1,0:T(8,128)(2,1)S(1)}, u32[]{:S(2)}, u32[]{:S(2)}) %collective-permute-start.9) | collective-permute-done | bytes 655392 | tf_op jit(solution)/shard_map/ppermute | solution.py:18
  45.6 0.3 multiply_convert_fusion
  45.8 1.6 %collective-permute-start.10 = (bf16[2,160,512]{2,1,0:T(8,128)(2,1)S(1)}, bf16[2,160,512]{2,1,0:T(8,128)(2,1)S(1)}, u32[]{:S(2)}, u32[]{:S(2)}) collective-permute-start(bf16[2,160,512]{2,1,0:T(8,128)(2,1)S(1)} %bitcast.77), channel_id=1, source_target_pairs={{0,2},{2,0},{1,3},{3,1},{4,6},{6,4},{5,7},{7,5},{8,10},{10,8},{9,1... | collective-permute-start | bytes 983048 | tf_op jit(solution)/shard_map/ppermute | solution.py:18
  47.4 0.5 collective-permute-start.1
  47.9 7.8 %collective-permute-done.1 = f32[2,4,64]{2,1,0:T(4,128)S(1)} collective-permute-done((f32[2,4,64]{2,1,0:T(4,128)S(1)}, f32[2,4,64]{2,1,0:T(4,128)S(1)}, u32[]{:S(2)}, u32[]{:S(2)}) %collective-permute-start.1) | collective-permute-done | bytes 2080 | tf_op jit(solution)/shard_map/ppermute | solution.py:18
  55.8 0.1 broadcast_select_fusion.1
  55.9 3.4 %fusion.6 = bf16[320,1792]{1,0:T(8,128)(2,1)S(1)} fusion(bf16[1,1,1024,1792]{3,2,1,0:T(8,128)(2,1)} %param.19, bf16[320,512]{1,0:T(8,128)(2,1)S(1)} %get-tuple-element.23, bf16[320,512]{1,0:T(8,128)(2,1)S(1)} %get-tuple-element.22), kind=kOutput, calls=%fused_computation.7 | convolution fusion | flops 1176289280 | bytes 5472256 | tf_op jit(solution)/shard_map/dot_general | solution.py:99
  59.3 0.1 slice_bitcast_fusion.3
  59.4 3.0 %collective-permute-start.12 = (bf16[2,40,1792]{2,1,0:T(8,128)(2,1)S(1)}, bf16[2,40,1792]{2,1,0:T(8,128)(2,1)S(1)}, u32[]{:S(2)}, u32[]{:S(2)}) collective-permute-start(bf16[2,40,1792]{2,1,0:T(8,128)(2,1)S(1)} %get-tuple-element.16), channel_id=1, source_target_pairs={{0,8},{4,12},{8,0},{12,4},{1,9},{5,13},{9,1},{13,5},{2,10},{6,14},... | collective-permute-start | bytes 860168 | tf_op jit(solution)/shard_map/ppermute | solution.py:18
  62.5 0.5 collective-permute-start.13
  62.9 0.1 select_convert_fusion.1
  63.0 0.1 fusion.14
  63.1 7.3 %collective-permute-done.11 = bf16[2,40,1792]{2,1,0:T(8,128)(2,1)S(1)} collective-permute-done((bf16[2,40,1792]{2,1,0:T(8,128)(2,1)S(1)}, bf16[2,40,1792]{2,1,0:T(8,128)(2,1)S(1)}, u32[]{:S(2)}, u32[]{:S(2)}) %collective-permute-start.11) | collective-permute-done | bytes 286752 | tf_op jit(solution)/shard_map/ppermute | solution.py:18
  70.4 11.7 %collective-permute-done.12 = bf16[2,40,1792]{2,1,0:T(8,128)(2,1)S(1)} collective-permute-done((bf16[2,40,1792]{2,1,0:T(8,128)(2,1)S(1)}, bf16[2,40,1792]{2,1,0:T(8,128)(2,1)S(1)}, u32[]{:S(2)}, u32[]{:S(2)}) %collective-permute-start.12) | collective-permute-done | bytes 286752 | tf_op jit(solution)/shard_map/ppermute | solution.py:18
  82.0 5.1 %collective-permute-done.13 = bf16[2,40,1792]{2,1,0:T(8,128)(2,1)S(1)} collective-permute-done((bf16[2,40,1792]{2,1,0:T(8,128)(2,1)S(1)}, bf16[2,40,1792]{2,1,0:T(8,128)(2,1)S(1)}, u32[]{:S(2)}, u32[]{:S(2)}) %collective-permute-start.13) | collective-permute-done | bytes 286752 | tf_op jit(solution)/shard_map/ppermute | solution.py:18
  87.1 0.1 pad_maximum_fusion
  87.3 0.1 fusion.19
  87.4 0.3 fusion.24
  87.6 0.3 fusion.9
  87.9 1.6 %collective-permute-start.14 = (bf16[64,1792]{1,0:T(8,128)(2,1)S(1)}, bf16[64,1792]{1,0:T(8,128)(2,1)S(1)}, u32[]{:S(2)}, u32[]{:S(2)}) collective-permute-start(bf16[64,1792]{1,0:T(8,128)(2,1)S(1)} %fusion.9), channel_id=1, source_target_pairs={{0,2},{2,0},{1,3},{3,1},{4,6},{6,4},{5,7},{7,5},{8,10},{10,8},{9,1... | collective-permute-start | bytes 688136 | tf_op jit(solution)/shard_map/ppermute | solution.py:18
  89.5 0.3 fusion.25
  89.7 4.3 %collective-permute-done.14 = bf16[64,1792]{1,0:T(8,128)(2,1)S(1)} collective-permute-done((bf16[64,1792]{1,0:T(8,128)(2,1)S(1)}, bf16[64,1792]{1,0:T(8,128)(2,1)S(1)}, u32[]{:S(2)}, u32[]{:S(2)}) %collective-permute-start.14) | collective-permute-done | bytes 229408 | tf_op jit(solution)/shard_map/ppermute | solution.py:18
  94.0 0.3 broadcast_select_fusion.3
  94.3 0.8 pad_maximum_fusion.2
  (40 shorter events, 0.6 us)
Async XLA Ops:
  0.0 9.2 %copy-start = (bf16[3584,128]{1,0:T(8,128)(2,1)S(1)}, bf16[3584,128]{1,0:T(8,128)(2,1)}, u32[]{:S(2)}) copy-start(bf16[3584,128]{1,0:T(8,128)(2,1)} %param.15) | copy-start | bytes 2752516
  0.0 9.2 %copy-start.1 = (bf16[64,3584]{1,0:T(8,128)(2,1)S(1)}, bf16[64,3584]{1,0:T(8,128)(2,1)}, u32[]{:S(2)}) copy-start(bf16[64,3584]{1,0:T(8,128)(2,1)} %param.10) | copy-start | bytes 1376260
  0.0 9.2 %copy-start.4 = (s32[64]{0:T(128)S(1)}, s32[64]{0:T(128)}, u32[]{:S(2)}) copy-start(s32[64]{0:T(128)} %param.12) | copy-start | bytes 772
  4.0 5.5 %copy-start.2 = (bf16[3584,4]{0,1:T(4,128)(2,1)S(1)}, bf16[3584,4]{0,1:T(4,128)(2,1)}, u32[]{:S(2)}) copy-start(bf16[3584,4]{0,1:T(4,128)(2,1)} %param.14) | copy-start | bytes 86020
  4.0 5.7 %copy-start.3 = (bf16[128,4]{0,1:T(4,128)(2,1)S(1)}, bf16[128,4]{0,1:T(4,128)(2,1)}, u32[]{:S(2)}) copy-start(bf16[128,4]{0,1:T(4,128)(2,1)} %param.16) | copy-start | bytes 3076
  4.2 11.8 %collective-permute-start.2 = (bf16[40,3584]{1,0:T(8,128)(2,1)S(1)}, bf16[40,3584]{1,0:T(8,128)(2,1)S(1)}, u32[]{:S(2)}, u32[]{:S(2)}) collective-permute-start(bf16[40,3584]{1,0:T(8,128)(2,1)S(1)} %get-tuple-element.21), channel_id=1, source_target_pairs={{0,4},{4,0},{8,12},{12,8},{1,5},{5,1},{9,13},{13,9},{2,6},{6,2},{1... | collective-permute-start | bytes 860168 | tf_op jit(solution)/shard_map/ppermute | solution.py:18
  4.2 22.6 %collective-permute-start.3 = (bf16[40,3584]{1,0:T(8,128)(2,1)S(1)}, bf16[40,3584]{1,0:T(8,128)(2,1)S(1)}, u32[]{:S(2)}, u32[]{:S(2)}) collective-permute-start(bf16[40,3584]{1,0:T(8,128)(2,1)S(1)} %get-tuple-element.20), channel_id=1, source_target_pairs={{0,8},{4,12},{8,0},{12,4},{1,9},{5,13},{9,1},{13,5},{2,10},{6,14},... | collective-permute-start | bytes 860168 | tf_op jit(solution)/shard_map/ppermute | solution.py:18
  7.3 25.2 %collective-permute-start.4 = (bf16[40,3584]{1,0:T(8,128)(2,1)S(1)}, bf16[40,3584]{1,0:T(8,128)(2,1)S(1)}, u32[]{:S(2)}, u32[]{:S(2)}) collective-permute-start(bf16[40,3584]{1,0:T(8,128)(2,1)S(1)} %get-tuple-element.19), channel_id=1, source_target_pairs={{0,12},{4,8},{8,4},{12,0},{1,13},{5,9},{9,5},{13,1},{2,14},{6,10},... | collective-permute-start | bytes 860168 | tf_op jit(solution)/shard_map/ppermute | solution.py:18
  7.7 26.3 %collective-permute-start.5 = (bf16[40,3584]{1,0:T(8,128)(2,1)S(1)}, bf16[40,3584]{1,0:T(8,128)(2,1)S(1)}, u32[]{:S(2)}, u32[]{:S(2)}) collective-permute-start(bf16[40,3584]{1,0:T(8,128)(2,1)S(1)} %get-tuple-element.17), channel_id=1, source_target_pairs={{0,2},{2,0},{1,3},{3,1},{4,6},{6,4},{5,7},{7,5},{8,10},{10,8},{9,1... | collective-permute-start | bytes 860168 | tf_op jit(solution)/shard_map/ppermute | solution.py:18
  9.5 30.4 %copy-start.5 = (bf16[1,3584,512]{2,1,0:T(8,128)(2,1)S(1)}, bf16[1,3584,512]{2,1,0:T(8,128)(2,1)}, u32[]{:S(2)}) copy-start(bf16[1,3584,512]{2,1,0:T(8,128)(2,1)} %param.18) | copy-start | bytes 11010052
  9.9 33.6 %collective-permute-start = (f32[64,4]{0,1:T(4,128)S(1)}, f32[64,4]{0,1:T(4,128)S(1)}, u32[]{:S(2)}, u32[]{:S(2)}) collective-permute-start(f32[64,4]{0,1:T(4,128)S(1)} %convolution_add_fusion.2), channel_id=1, source_target_pairs={{0,1},{1,0},{2,3},{3,2},{4,5},{5,4},{6,7},{7,6},{8,9},{9,8},{10,11... | collective-permute-start | bytes 3080 | tf_op jit(solution)/shard_map/ppermute | solution.py:18
  16.0 18.0 %collective-permute-start.6 = (bf16[40,3584]{1,0:T(8,128)(2,1)S(1)}, bf16[40,3584]{1,0:T(8,128)(2,1)S(1)}, u32[]{:S(2)}, u32[]{:S(2)}) collective-permute-start(bf16[40,3584]{1,0:T(8,128)(2,1)S(1)} %collective-permute-done.2), channel_id=1, source_target_pairs={{0,2},{2,0},{1,3},{3,1},{4,6},{6,4},{5,7},{7,5},{8,10},{10,8},{9,1... | collective-permute-start | bytes 860168 | tf_op jit(solution)/shard_map/ppermute | solution.py:18
  26.8 7.2 %collective-permute-start.7 = (bf16[40,3584]{1,0:T(8,128)(2,1)S(1)}, bf16[40,3584]{1,0:T(8,128)(2,1)S(1)}, u32[]{:S(2)}, u32[]{:S(2)}) collective-permute-start(bf16[40,3584]{1,0:T(8,128)(2,1)S(1)} %collective-permute-done.3), channel_id=1, source_target_pairs={{0,2},{2,0},{1,3},{3,1},{4,6},{6,4},{5,7},{7,5},{8,10},{10,8},{9,1... | collective-permute-start | bytes 860168 | tf_op jit(solution)/shard_map/ppermute | solution.py:18
  32.5 7.4 %collective-permute-start.8 = (bf16[40,3584]{1,0:T(8,128)(2,1)S(1)}, bf16[40,3584]{1,0:T(8,128)(2,1)S(1)}, u32[]{:S(2)}, u32[]{:S(2)}) collective-permute-start(bf16[40,3584]{1,0:T(8,128)(2,1)S(1)} %collective-permute-done.4), channel_id=1, source_target_pairs={{0,2},{2,0},{1,3},{3,1},{4,6},{6,4},{5,7},{7,5},{8,10},{10,8},{9,1... | collective-permute-start | bytes 860168 | tf_op jit(solution)/shard_map/ppermute | solution.py:18
  39.9 2.0 %copy-start.6 = (bf16[1,3584,512]{2,1,0:T(8,128)(2,1)S(1)}, bf16[1,3584,512]{2,1,0:T(8,128)(2,1)}, u32[]{:S(2)}) copy-start(bf16[1,3584,512]{2,1,0:T(8,128)(2,1)} %param.17) | copy-start | bytes 11010052
  43.4 2.2 %collective-permute-start.9 = (bf16[320,1024]{1,0:T(8,128)(2,1)S(1)}, bf16[320,1024]{1,0:T(8,128)(2,1)S(1)}, u32[]{:S(2)}, u32[]{:S(2)}) collective-permute-start(bf16[320,1024]{1,0:T(8,128)(2,1)S(1)} %pad_maximum_fusion.1), channel_id=1, source_target_pairs={{0,1},{1,0},{2,3},{3,2},{4,5},{5,4},{6,7},{7,6},{8,9},{9,8},{10,11... | collective-permute-start | bytes 1966088 | tf_op jit(solution)/shard_map/ppermute | solution.py:18
  45.8 9.9 %collective-permute-start.10 = (bf16[2,160,512]{2,1,0:T(8,128)(2,1)S(1)}, bf16[2,160,512]{2,1,0:T(8,128)(2,1)S(1)}, u32[]{:S(2)}, u32[]{:S(2)}) collective-permute-start(bf16[2,160,512]{2,1,0:T(8,128)(2,1)S(1)} %bitcast.77), channel_id=1, source_target_pairs={{0,2},{2,0},{1,3},{3,1},{4,6},{6,4},{5,7},{7,5},{8,10},{10,8},{9,1... | collective-permute-start | bytes 983048 | tf_op jit(solution)/shard_map/ppermute | solution.py:18
  47.4 8.3 %collective-permute-start.1 = (f32[2,4,64]{2,1,0:T(4,128)S(1)}, f32[2,4,64]{2,1,0:T(4,128)S(1)}, u32[]{:S(2)}, u32[]{:S(2)}) collective-permute-start(f32[2,4,64]{2,1,0:T(4,128)S(1)} %pad_maximum_fusion.4), channel_id=1, source_target_pairs={{0,2},{2,0},{1,3},{3,1},{4,6},{6,4},{5,7},{7,5},{8,10},{10,8},{9,1... | collective-permute-start | bytes 6152 | tf_op jit(solution)/shard_map/ppermute | solution.py:18
  59.4 11.0 %collective-permute-start.11 = (bf16[2,40,1792]{2,1,0:T(8,128)(2,1)S(1)}, bf16[2,40,1792]{2,1,0:T(8,128)(2,1)S(1)}, u32[]{:S(2)}, u32[]{:S(2)}) collective-permute-start(bf16[2,40,1792]{2,1,0:T(8,128)(2,1)S(1)} %get-tuple-element.14), channel_id=1, source_target_pairs={{0,4},{4,0},{8,12},{12,8},{1,5},{5,1},{9,13},{13,9},{2,6},{6,2},{1... | collective-permute-start | bytes 860168 | tf_op jit(solution)/shard_map/ppermute | solution.py:18
  59.4 22.6 %collective-permute-start.12 = (bf16[2,40,1792]{2,1,0:T(8,128)(2,1)S(1)}, bf16[2,40,1792]{2,1,0:T(8,128)(2,1)S(1)}, u32[]{:S(2)}, u32[]{:S(2)}) collective-permute-start(bf16[2,40,1792]{2,1,0:T(8,128)(2,1)S(1)} %get-tuple-element.16), channel_id=1, source_target_pairs={{0,8},{4,12},{8,0},{12,4},{1,9},{5,13},{9,1},{13,5},{2,10},{6,14},... | collective-permute-start | bytes 860168 | tf_op jit(solution)/shard_map/ppermute | solution.py:18
  62.5 24.7 %collective-permute-start.13 = (bf16[2,40,1792]{2,1,0:T(8,128)(2,1)S(1)}, bf16[2,40,1792]{2,1,0:T(8,128)(2,1)S(1)}, u32[]{:S(2)}, u32[]{:S(2)}) collective-permute-start(bf16[2,40,1792]{2,1,0:T(8,128)(2,1)S(1)} %get-tuple-element.15), channel_id=1, source_target_pairs={{0,12},{4,8},{8,4},{12,0},{1,13},{5,9},{9,5},{13,1},{2,14},{6,10},... | collective-permute-start | bytes 860168 | tf_op jit(solution)/shard_map/ppermute | solution.py:18
  87.9 6.1 %collective-permute-start.14 = (bf16[64,1792]{1,0:T(8,128)(2,1)S(1)}, bf16[64,1792]{1,0:T(8,128)(2,1)S(1)}, u32[]{:S(2)}, u32[]{:S(2)}) collective-permute-start(bf16[64,1792]{1,0:T(8,128)(2,1)S(1)} %fusion.9), channel_id=1, source_target_pairs={{0,2},{2,0},{1,3},{3,1},{4,6},{6,4},{5,7},{7,5},{8,10},{10,8},{9,1... | collective-permute-start | bytes 688136 | tf_op jit(solution)/shard_map/ppermute | solution.py:18

commit v2 on v0

v2 whole, which is shorter than its diff:
```python
import functools

import jax
import jax.numpy as jnp
from jax import lax
from jax.experimental import pallas as pl
from jax.experimental.pallas import tpu as pltpu
from jax.sharding import PartitionSpec as P

RANK = 16
ROUTE_SCALE = 2.5
VMEM_LIMIT = 24 * 1024 * 1024
f32 = jnp.float32
bf16 = jnp.bfloat16


def partner(index, step):
    return index ^ step


def swap(value, axis, step):
    count = lax.axis_size(axis)
    return lax.ppermute(value, axis, [(i, partner(i, step)) for i in range(count)])


def send(value, ep_step, node_step):
    if not ep_step and not node_step:
        return value
    if not node_step:
        return swap(value, "ep", ep_step)
    if not ep_step:
        return swap(value, "node", node_step)
    eps, nodes = lax.axis_size("ep"), lax.axis_size("node")
    pairs = [
        (i * nodes + j, partner(i, ep_step) * nodes + partner(j, node_step))
        for i in range(eps)
        for j in range(nodes)
    ]
    return lax.ppermute(value, ("ep", "node"), pairs)


def regroup(rows, step, size):
    count = rows.shape[0] // size
    return jnp.concatenate([rows[(j ^ step) * size : (j ^ step) * size + size] for j in range(count)])


WHOLE = pl.BlockSpec(memory_space=pltpu.VMEM)
ANY = pl.BlockSpec(memory_space=pl.ANY)
IN_HBM = pl.BlockSpec(memory_space=pltpu.HBM)


def call(kernel, out_shape, in_specs, scratch=(), aliases=None):
    return pl.pallas_call(
        kernel,
        out_shape=out_shape,
        in_specs=in_specs,
        out_specs=[ANY if i in (aliases or {}).values() else WHOLE for i in range(len(out_shape))],
        scratch_shapes=list(scratch),
        input_output_aliases=aliases or {},
        compiler_params=pltpu.CompilerParams(vmem_limit_bytes=VMEM_LIMIT),
        cost_estimate=pl.CostEstimate(flops=0, bytes_accessed=0, transcendentals=0),
    )


def in_hbm(value):
    return pltpu.with_memory_space_constraint(value, pltpu.HBM)


def pack_rows(expert_place, routes_t, tokens, order, cap, behind=()):
    experts = expert_place.shape[0]
    topk, tok_rows = routes_t.shape
    width = tokens.shape[1]

    def kernel(where_hbm, routes_hbm, tokens_hbm, *refs):
        place_ref, *refs = refs[len(behind) :]
        block_refs, (where_ref, routes_ref, tokens_ref, sems) = refs[: len(order)], refs[len(order) :]
        pairs = [(where_hbm, where_ref), (routes_hbm, routes_ref), (tokens_hbm, tokens_ref)]
        copies = [pltpu.make_async_copy(a, b, sems.at[i]) for i, (a, b) in enumerate(pairs)]
        for copy in copies:
            copy.start()
        copies[0].wait()
        copies[1].wait()
        named_by = routes_ref[...]
        where = where_ref[...] ^ lax.axis_index("ep")
        relative = jnp.zeros_like(named_by)
        for e in range(experts):
            relative = jnp.where(named_by == e, where[:, e : e + 1], relative)
        block = lax.broadcasted_iota(jnp.int32, (experts, tok_rows), 0)
        named = functools.reduce(
            jnp.logical_or, [relative[k : k + 1] == block for k in range(topk)]
        )
        earlier = lax.broadcasted_iota(jnp.int32, (tok_rows, tok_rows), 0) < (
            lax.broadcasted_iota(jnp.int32, (tok_rows, tok_rows), 1)
        )
        before = jnp.dot(
            jnp.where(named, f32(1.0), f32(0.0)).astype(bf16),
            jnp.where(earlier, f32(1.0), f32(0.0)).astype(bf16),
            preferred_element_type=f32,
        )
        place = jnp.where(named, before, f32(-1.0))
        place_ref[...] = place
        row = lax.broadcasted_iota(jnp.int32, (cap, tok_rows), 0).astype(f32)
        copies[2].wait()
        for block_ref, k in zip(block_refs, order):
            placing = jnp.where(place[k : k + 1] == row, f32(1.0), f32(0.0)).astype(bf16)
            block_ref[...] = jnp.dot(
                placing, tokens_ref[...], preferred_element_type=f32
            ).astype(bf16)

    shapes = [jax.ShapeDtypeStruct((experts, tok_rows), f32)]
    shapes += [jax.ShapeDtypeStruct((cap, width), bf16)] * len(order)
    scratch = [
        pltpu.VMEM((1, experts), jnp.int32),
        pltpu.VMEM((topk, tok_rows), jnp.int32),
        pltpu.VMEM((tok_rows, width), bf16),
        pltpu.SemaphoreType.DMA((3,)),
    ]
    return call(kernel, shapes, [IN_HBM] * 3 + [ANY] * len(behind), scratch)(
        in_hbm(expert_place.reshape(1, experts)), in_hbm(routes_t), in_hbm(tokens), *behind
    )


def hold(held, behind):
    count = len(behind)
    shapes = [jax.ShapeDtypeStruct(a.shape, a.dtype) for a in held]
    aliases = {count + i: i for i in range(len(held))}
    specs = [ANY] * (count + len(held))
    return call(lambda *refs: None, shapes, specs, aliases=aliases)(*behind, *held)


def load(arrays, behind):
    count = len(arrays)

    def kernel(*refs):
        fetch(refs[:count], refs[count + len(behind) : -1], refs[-1])

    shapes = [pltpu.VMEM(a.shape, a.dtype) for a in arrays]
    specs = [IN_HBM] * count + [ANY] * len(behind)
    return call(kernel, shapes, specs, [pltpu.SemaphoreType.DMA((count,))])(
        *[in_hbm(a) for a in arrays], *behind
    )


def as_column(row, size):
    same = lax.broadcasted_iota(jnp.int32, (size, size), 0) == (
        lax.broadcasted_iota(jnp.int32, (size, size), 1)
    )
    return jnp.sum(jnp.where(same, row, jnp.zeros_like(row)), axis=1, keepdims=True)


def fetch(sources, places, sems):
    copies = [pltpu.make_async_copy(a, b, sems.at[i]) for i, (a, b) in enumerate(zip(sources, places))]
    for copy in copies:
        copy.start()
    for copy in copies:
        copy.wait()


def partial_logits(tokens, tenant, router_weight, adapter_down, adapter_up, behind):
    tok_rows = tokens.shape[0]
    ranks, experts = adapter_up.shape
    given = [tokens, adapter_down, router_weight.T, adapter_up.T, tenant.reshape(1, tok_rows)]

    def kernel(*refs):
        out_ref, *held, sems = refs[len(given) + len(behind) :]
        fetch(refs[: len(given)], held, sems)
        tokens_ref, down_ref, router_ref, up_ref, tenant_ref = held
        lowrank = jnp.dot(tokens_ref[...], down_ref[...], preferred_element_type=f32)
        owner = (lax.broadcasted_iota(jnp.int32, (tok_rows, ranks), 1) // RANK).astype(f32)
        tenants = as_column(tenant_ref[...].astype(f32), tok_rows)
        lowrank = jnp.where(owner == tenants, lowrank, f32(0.0))
        across = (((1,), (1,)), ((), ()))
        base = lax.dot_general(
            router_ref[...], tokens_ref[...], across, preferred_element_type=f32
        )
        out_ref[...] = base + lax.dot_general(
            up_ref[...].astype(f32),
            lowrank,
            across,
            precision=lax.Precision.HIGHEST,
            preferred_element_type=f32,
        )

    shapes = [jax.ShapeDtypeStruct((experts, tok_rows), f32)]
    specs = [IN_HBM] * len(given) + [ANY] * len(behind)
    scratch = [pltpu.VMEM(a.shape, a.dtype) for a in given]
    scratch.append(pltpu.SemaphoreType.DMA((len(given),)))
    return call(kernel, shapes, specs, scratch)(*[in_hbm(a) for a in given], *behind)[0]


def route_info(parts, place, expert_place, routes_t):
    _, experts, tok_rows = parts.shape
    topk = routes_t.shape[0]
    given = [expert_place.reshape(1, experts), routes_t]

    def kernel(parts_ref, place_ref, where_hbm, routes_hbm, out_ref, where_ref, routes_ref, sems):
        fetch([where_hbm, routes_hbm], [where_ref, routes_ref], sems)
        score = jax.nn.sigmoid(functools.reduce(jnp.add, [parts_ref[i] for i in range(parts.shape[0])]))
        expert = lax.broadcasted_iota(jnp.int32, (experts, tok_rows), 0)
        chosen = functools.reduce(
            jnp.logical_or, [routes_ref[k : k + 1, :] == expert for k in range(topk)]
        )
        score = jnp.where(chosen, score, f32(0.0))
        weight = ROUTE_SCALE * score / jnp.sum(score, axis=0, keepdims=True)
        slot = where_ref[...] ^ lax.axis_index("ep")
        for r in range(experts):
            here = jnp.zeros((1, tok_rows), f32)
            for e in range(experts):
                here = jnp.where(slot[:, e : e + 1] == r, weight[e : e + 1], here)
            out_ref[0, :, r : r + 1] = as_column(place_ref[r : r + 1, :], tok_rows)
            out_ref[1, :, r : r + 1] = as_column(here, tok_rows)

    shapes = [jax.ShapeDtypeStruct((2, tok_rows, experts), f32)]
    scratch = [pltpu.VMEM(a.shape, a.dtype) for a in given]
    scratch.append(pltpu.SemaphoreType.DMA((len(given),)))
    return call(kernel, shapes, [WHOLE] * 2 + [IN_HBM] * 2, scratch)(
        parts, place, *[in_hbm(a) for a in given]
    )[0]


def activate(own, both):
    count, wide = own.shape

    def kernel(own_ref, both_ref, out_ref):
        total = own_ref[...] + both_ref[1 - lax.axis_index("sub")].astype(f32)
        gate, up = total[:, : wide // 2], total[:, wide // 2 :]
        out_ref[...] = (jax.nn.silu(gate) * up).astype(bf16)

    shapes = [jax.ShapeDtypeStruct((count, wide // 2), bf16)]
    return call(kernel, shapes, [WHOLE] * 2)(own, both)[0]


def dots(rows, weights, kinds, behind):
    count, wide = rows.shape[0], weights[0].shape[1]

    def kernel(rows_ref, *refs):
        for i in range(len(weights)):
            value = jnp.dot(rows_ref[...], refs[i][...], preferred_element_type=f32)
            for out in refs[len(weights) + len(behind) :]:
                out[:, i * wide : (i + 1) * wide] = value.astype(out.dtype)

    shapes = [jax.ShapeDtypeStruct((count, len(weights) * wide), kind) for kind in kinds]
    specs = [WHOLE] * (1 + len(weights)) + [ANY] * len(behind)
    return call(kernel, shapes, specs)(rows, *weights, *behind)


def project(by_node, weight, behind):
    nodes = len(by_node)
    count, part = by_node[0].shape

    def kernel(*refs):
        hidden_refs, weight_ref, out_ref = refs[:nodes], refs[nodes], refs[-1]
        node_me = lax.axis_index("node")
        total = None
        for i in range(nodes):
            node = node_me ^ i
            hidden = hidden_refs[i][...] if by_node[i].ndim == 2 else hidden_refs[i][node]
            at = pl.ds(pl.multiple_of(node * part, part), part)
            value = jnp.dot(hidden, weight_ref[at, :], preferred_element_type=f32)
            total = value if total is None else total + value
        out_ref[...] = total.astype(bf16)

    shapes = [jax.ShapeDtypeStruct((count, weight.shape[1]), bf16)]
    specs = [WHOLE] * (nodes + 1) + [ANY] * len(behind)
    return call(kernel, shapes, specs)(*by_node, weight, *behind)[0]


def weighted_sum(info, pieces):
    tok_rows = info.shape[1]
    total = None
    for k, value in pieces:
        row = lax.broadcasted_iota(jnp.int32, (tok_rows, value.shape[0]), 1).astype(f32)
        factor = jnp.where(info[0, :, k : k + 1] == row, info[1, :, k : k + 1], f32(0.0))
        high = factor.astype(bf16)
        low = (factor - high.astype(f32)).astype(bf16)
        for part in (high, low):
            product = jnp.dot(part, value, preferred_element_type=f32)
            total = product if total is None else total + product
    return total


def combine_early(info, order, pieces):
    width = pieces[0].shape[-1]
    tok_rows = info.shape[1]

    def kernel(info_ref, *refs):
        for piece, out in zip(refs, refs[len(pieces) :]):
            out[...] = weighted_sum(info_ref[...], [(k, piece[i]) for i, k in enumerate(order)])

    shapes = [jax.ShapeDtypeStruct((tok_rows, width), f32)] * len(pieces)
    return call(kernel, shapes, [WHOLE] * (1 + len(pieces)))(info, *pieces)


def combine_late(info, early, pieces):
    nodes = len(early)
    order = [k for k, _ in pieces[0]]
    flat = [rows for part in pieces for _, rows in part]
    tok_rows, width = early[0].shape

    def kernel(info_ref, *refs):
        early_refs, late_refs, out_ref = refs[:nodes], refs[nodes:-1], refs[-1]
        node_me = lax.axis_index("node")
        for j in range(nodes):
            mine = [(k, late_refs[j * len(order) + i][...]) for i, k in enumerate(order)]
            value = (early_refs[j][...] + weighted_sum(info_ref[...], mine)).astype(bf16)
            for at in range(nodes):

                @pl.when(node_me ^ j == at)
                def _(value=value, at=at):
                    out_ref[:, at * width : (at + 1) * width] = value

    shapes = [jax.ShapeDtypeStruct((tok_rows, nodes * width), bf16)]
    return call(kernel, shapes, [WHOLE] * (1 + nodes + len(flat)))(info, *early, *flat)[0]


def body(
    tokens,
    routes,
    tenant,
    expert_place,
    router_weight,
    adapter_down,
    adapter_up,
    gate_weight,
    up_weight,
    down_weight,
):
    tok_rows, half_width = tokens.shape
    topk = routes.shape[1]
    eps = lax.axis_size("ep")
    nodes = lax.axis_size("node")
    cap = 5 * tok_rows * topk // (4 * eps)
    out_width = down_weight.shape[3]

    quarter = max(1, eps // 4)
    near = range(1, 2 * quarter)
    middle = range(2 * quarter, 3 * quarter)
    far = range(3 * quarter, eps)
    others = range(1, nodes)
    routes_t = routes.T
    place, *first_out = pack_rows(expert_place, routes_t, tokens, [*middle], cap)
    _, *later_out = pack_rows(expert_place, routes_t, tokens, [0, *near, *far], cap, first_out)
    outgoing = dict(zip([*middle, 0, *near, *far], first_out + later_out))

    blocks = [[outgoing[k]] + [None] * (nodes - 1) for k in range(eps)]
    for k in [*middle, *near]:
        blocks[k][0] = swap(outgoing[k], "ep", k)
    for k in [0, *near]:
        blocks[k][1:] = [swap(outgoing[k], "node", j) for j in others]
    gate_w, up_w, down_w = load(
        [gate_weight[0], up_weight[0], down_weight[0, 0]], [outgoing[0]]
    )
    for k, rows in zip(middle, hold([blocks[k][0] for k in middle], [gate_w, blocks[1][0]])):
        blocks[k] = [rows] + [swap(rows, "node", j) for j in others]
    crossed = [blocks[k][j] for k in near for j in others]
    crossed = hold(crossed + [outgoing[k] for k in far], [blocks[middle[-1]][0]])
    for i, k in enumerate(near):
        for j in others:
            blocks[k][j] = swap(crossed[i * len(others) + j - 1], "ep", k)
    for i, k in enumerate(far):
        blocks[k][0] = swap(crossed[len(near) * len(others) + i], "ep", k)

    def gate_up(chunk, behind):
        rows = [blocks[k][j] for j in range(nodes) for k in chunk]
        own, sent = dots(jnp.concatenate(rows, axis=0), [gate_w, up_w], [f32, bf16], behind)
        return activate(own, lax.all_gather(sent, "sub"))

    def down(chunk, hidden, gather=False, behind=()):
        size = len(chunk) * cap
        by_node = [hidden]
        for i in others:
            sent = regroup(hidden, i, size)
            if gather:
                by_node.append(lax.all_gather(sent, "node"))
            else:
                by_node.append(swap(sent, "node", i))
        out = project(by_node, down_w, behind)
        return out.reshape(nodes, len(chunk), cap, out_width)

    logits = partial_logits(
        tokens, tenant, router_weight, adapter_down, adapter_up, crossed[:1]
    )
    info = route_info(lax.all_gather(logits, "sub"), place, expert_place, routes_t)

    early_chunk, late_chunk = [0, *middle], [*near, *far]
    hidden = gate_up(early_chunk, [info])
    for k in far:
        for j in others:
            blocks[k][j] = swap(blocks[k][0], "node", j)
    early_out = down(early_chunk, hidden, behind=[blocks[k][j] for k in near for j in others])
    hidden = gate_up(late_chunk, [early_out])
    late_out = down(late_chunk, hidden, True)

    back = [early_out[:, 0]]
    back += [swap(early_out[:, i], "ep", k) for i, k in enumerate(early_chunk) if k]
    late = [
        [(k, send(late_out[j, i], k, j)) for i, k in enumerate(late_chunk)] for j in range(nodes)
    ]
    across = [jnp.stack([part[j] for part in back]) for j in range(nodes)]
    across[1:] = hold(across[1:], [late_out])
    across[1:] = [swap(across[j], "node", j) for j in others]
    return combine_late(info, combine_early(info, early_chunk, across), late)


def solution(mesh):
    placed = (
        P(("rep", "ep", "node"), "sub"),
        P(("rep", "ep", "node"), None),
        P(("rep", "ep", "node")),
        P(),
        P("sub", None),
        P("sub", None),
        P(),
        P("ep", "sub", "node"),
        P("ep", "sub", "node"),
        P("ep", "sub", None, "node"),
    )
    return jax.shard_map(
        body, mesh=mesh, in_specs=placed, out_specs=P(("rep", "ep", "node"), "sub"), check_vma=False
    )
```

time: 169 us -> 76.9 us (0.46)
  blocking collectives: 90 us -> 13.2 us
  Pallas kernels: 0 us -> 17.2 us
  waiting for transfers between devices: 42.1 us -> 25.2 us
  starting transfers between devices: 4.93 us -> 20.4 us
  between operations: 13.5 us -> 0.21 us
  matrix products: 8.41 us -> 0 us
  local copies, waits for them, and re-layouts: 6.77 us -> 0.13 us
  other arithmetic: 3.17 us -> 0.27 us
    all_to_all x2 -> x0, blocking collectives: 77 us -> none  [the longest x1 59.9 us: body(): lax.all_to_all(spread, ('ep', 'node'), split_axis=0, concat_axis=0, tiled...]
    ppermute x0 -> x15, waiting for transfers between devices: none -> 25.2 us  [the longest x13 19.4 us: swap(): lax.ppermute(value, axis, [(i, partner(i, step)) for i in range(count)])]
    all_to_all x1 -> x0, waiting for transfers between devices: 23 us -> none  [body(): lax.all_to_all(returned, 'ep', split_axis=0, concat_axis=0, tiled=True)]
    ppermute x0 -> x15, starting transfers between devices: none -> 20.4 us  [the longest x13 16.9 us: swap(): lax.ppermute(value, axis, [(i, partner(i, step)) for i in range(count)])]
    psum x1 -> x0, waiting for transfers between devices: 19.1 us -> none  [body(): total = lax.psum(partial_value, 'sub')]
    pallas_call x0 -> x16, Pallas kernels: none -> 17.2 us  [the longest x1 4.23 us: load(): call(kernel, shapes, specs, [pltpu.SemaphoreType.DMA((count,))])]
    dot_general x8 -> x0, matrix products: 8.41 us -> none  [the longest x1 3.39 us: body(): jnp.dot(lax.all_gather(hidden, 'node', axis=1, tiled=True), down_local, p...]
    all_to_all x1 -> x0, starting transfers between devices: 4.92 us -> none  [body(): lax.all_to_all(returned, 'ep', split_axis=0, concat_axis=0, tiled=True)]
  transfers between devices with their start and end apart: 2 -> 15, of which waited for: 2 -> 9; matrix products, arithmetic and copies ran while one was open for 1% -> 0% of each run, Pallas kernels for 0% -> 16%
where the time goes in v2:
time: 76.9 us; the launch traced here: 76.7 us
  waiting for transfers between devices  25.2 us (33%)
  starting transfers between devices  20.4 us (27%)
  Pallas kernels  17.2 us (22%)
  blocking collectives  13.2 us (17%)
    ppermute x13, waiting for transfers between devices, swap(): lax.ppermute(value, axis, [(i, partner(i, step)) for i in range(count)])  19.4 us
    ppermute x13, starting transfers between devices, swap(): lax.ppermute(value, axis, [(i, partner(i, step)) for i in range(count)])  16.9 us
    all_gather x1, blocking collectives, down(): by_node.append(lax.all_gather(sent, 'node'))  6.92 us
    ppermute x2, waiting for transfers between devices, send(): return lax.ppermute(value, ('ep', 'node'), pairs)  5.88 us
    all_gather x2, blocking collectives, gate_up(): return activate(own, lax.all_gather(sent, 'sub'))  4.55 us
    pallas_call x1, Pallas kernels, load(): call(kernel, shapes, specs, [pltpu.SemaphoreType.DMA((count,))])  4.23 us
    ppermute x2, starting transfers between devices, send(): return lax.ppermute(value, ('ep', 'node'), pairs)  3.46 us
    pallas_call x2, Pallas kernels, pack_rows(): call(kernel, shapes, [IN_HBM] * 3 + [ANY] * len(behind), scratch)  2.98 us
  transfers between devices with their start and end apart: 15, of which 9 were waited for; matrix products, arithmetic and copies ran while one was open for 0% of the time, Pallas kernels for 16%

profile of v2, /device:TPU:0, one launch (start us, length us, event | category | flops | bytes accessed | tf_op | source)
XLA Modules:
  0.0 76.7 jit_solution(6571016976163854969)
XLA Ops:
  0.0 1.3 %shard_map.100 = (f32[4,64]{1,0:T(4,128)S(1)}, bf16[40,3584]{1,0:T(8,128)(2,1)S(1)}) custom-call(s32[1,4]{1,0:T(1,128)} %bitcast.44, s32[2,64]{1,0:T(2,128)} %bitcast.41, bf16[64,3584]{1,0:T(8,128)(2,1)} %refs_0_.1), custom_call_target="tpu_custom_call" | custom-call | tf_op jit(solution)/shard_map/pallas_call | solution.py:118
  1.3 1.7 %shard_map.101 = (f32[4,64]{1,0:T(4,128)}, bf16[40,3584]{1,0:T(8,128)(2,1)S(1)}, bf16[40,3584]{1,0:T(8,128)(2,1)S(1)}, bf16[40,3584]{1,0:T(8,128)(2,1)S(1)}) custom-call(s32[1,4]{1,0:T(1,128)} %bitcast.45, s32[2,64]{1,0:T(2,128)} %bitcast.42, bf16[64,3584]{1,0:T(8,128)(2,1)} %refs_0_.1, bf16[40,3584]{1,0:T(8,128)(2,1)S(1)} %get-tuple-element.21.refs_0_), custom_call_target="tpu_custom_call" | custom-call | tf_op jit(solution)/shard_map/pallas_call | solution.py:118
  3.0 3.1 %collective-permute-start = (bf16[40,3584]{1,0:T(8,128)(2,1)S(1)}, bf16[40,3584]{1,0:T(8,128)(2,1)S(1)}, u32[]{:S(2)}, u32[]{:S(2)}) collective-permute-start(bf16[40,3584]{1,0:T(8,128)(2,1)S(1)} %get-tuple-element.24), channel_id=1, source_target_pairs={{0,4},{4,0},{8,12},{12,8},{1,5},{5,1},{9,13},{13,9},{2,6},{6,2},{1... | collective-permute-start | bytes 860168 | tf_op jit(solution)/shard_map/ppermute | solution.py:23
  6.1 2.6 %collective-permute-start.1 = (bf16[40,3584]{1,0:T(8,128)(2,1)S(1)}, bf16[40,3584]{1,0:T(8,128)(2,1)S(1)}, u32[]{:S(2)}, u32[]{:S(2)}) collective-permute-start(bf16[40,3584]{1,0:T(8,128)(2,1)S(1)} %get-tuple-element.21.refs_0_), channel_id=1, source_target_pairs={{0,8},{4,12},{8,0},{12,4},{1,9},{5,13},{9,1},{13,5},{2,10},{6,14},... | collective-permute-start | bytes 860168 | tf_op jit(solution)/shard_map/ppermute | solution.py:23
  8.7 1.5 %collective-permute-start.2 = (bf16[40,3584]{1,0:T(8,128)(2,1)S(1)}, bf16[40,3584]{1,0:T(8,128)(2,1)S(1)}, u32[]{:S(2)}, u32[]{:S(2)}) collective-permute-start(bf16[40,3584]{1,0:T(8,128)(2,1)S(1)} %get-tuple-element.24), channel_id=1, source_target_pairs={{0,2},{2,0},{1,3},{3,1},{4,6},{6,4},{5,7},{7,5},{8,10},{10,8},{9,1... | collective-permute-start | bytes 860168 | tf_op jit(solution)/shard_map/ppermute | solution.py:23
  10.2 0.5 collective-permute-start.3
  10.7 4.2 %shard_map.102 = (bf16[3584,512]{1,0:T(8,128)(2,1)S(1)}, bf16[3584,512]{1,0:T(8,128)(2,1)S(1)}, bf16[1024,1792]{1,0:T(8,128)(2,1)S(1)}) custom-call(bf16[3584,512]{1,0:T(8,128)(2,1)} %bitcast.37, bf16[3584,512]{1,0:T(8,128)(2,1)} %bitcast.38, bf16[1024,1792]{1,0:T(8,128)(2,1)} %bitcast.39, bf16[40,3584]{1,0:T(8,128)(2,1)S(1)} %get-tuple-element.22.refs_3_), custom_call_target="tpu_custom_call" | custom-call | tf_op jit(solution)/shard_map/pallas_call | solution.py:139
  14.9 4.0 %collective-permute-done.refs_1_ = bf16[40,3584]{1,0:T(8,128)(2,1)S(1)} collective-permute-done((bf16[40,3584]{1,0:T(8,128)(2,1)S(1)}, bf16[40,3584]{1,0:T(8,128)(2,1)S(1)}, u32[]{:S(2)}, u32[]{:S(2)}) %collective-permute-start) | collective-permute-done | bytes 286752 | tf_op jit(solution)/shard_map/ppermute | solution.py:23
  18.9 2.5 %collective-permute-done.1.refs_2_ = bf16[40,3584]{1,0:T(8,128)(2,1)S(1)} collective-permute-done((bf16[40,3584]{1,0:T(8,128)(2,1)S(1)}, bf16[40,3584]{1,0:T(8,128)(2,1)S(1)}, u32[]{:S(2)}, u32[]{:S(2)}) %collective-permute-start.1) | collective-permute-done | bytes 286752 | tf_op jit(solution)/shard_map/ppermute | solution.py:23
  21.5 1.5 %collective-permute-start.4 = (bf16[40,3584]{1,0:T(8,128)(2,1)S(1)}, bf16[40,3584]{1,0:T(8,128)(2,1)S(1)}, u32[]{:S(2)}, u32[]{:S(2)}) collective-permute-start(bf16[40,3584]{1,0:T(8,128)(2,1)S(1)} %shard_map.103.refs_0_), channel_id=1, source_target_pairs={{0,2},{2,0},{1,3},{3,1},{4,6},{6,4},{5,7},{7,5},{8,10},{10,8},{9,1... | collective-permute-start | bytes 860168 | tf_op jit(solution)/shard_map/ppermute | solution.py:23
  23.0 0.0 collective-permute-done.2.refs_1_
  23.0 0.5 collective-permute-start.6
  23.4 2.1 %collective-permute-start.8 = (bf16[40,3584]{1,0:T(8,128)(2,1)S(1)}, bf16[40,3584]{1,0:T(8,128)(2,1)S(1)}, u32[]{:S(2)}, u32[]{:S(2)}) collective-permute-start(bf16[40,3584]{1,0:T(8,128)(2,1)S(1)} %get-tuple-element.32), channel_id=1, source_target_pairs={{0,12},{4,8},{8,4},{12,0},{1,13},{5,9},{9,5},{13,1},{2,14},{6,10},... | collective-permute-start | bytes 860168 | tf_op jit(solution)/shard_map/ppermute | solution.py:23
  25.5 1.9 %shard_map.105 = f32[4,64]{1,0:T(4,128)S(1)} custom-call(bf16[64,3584]{1,0:T(8,128)(2,1)} %refs_0_.1, bf16[3584,128]{1,0:T(8,128)(2,1)} %refs_1_.1, bf16[4,3584]{1,0:T(4,128)(2,1)} %bitcast.40, bf16[4,128]{1,0:T(4,128)(2,1)} %bitcast.47, s32[1,64]{1,0:T(1,128)} %bitcast.48, bf16[40,3584]{1,0:T(8,128)(2,1)S(1)} %get-tuple-element.26.refs_5_), custom_call_target="tpu_custom_call" | custom-call | tf_op jit(solution)/shard_map/pallas_call | solution.py:188
  27.4 1.8 %all-gather.4.parts_ref = f32[2,4,64]{2,1,0:T(4,128)S(1)} all-gather(f32[1,4,64]{2,1,0:T(4,128)S(1)} %bitcast.36), channel_id=2, replica_groups=mesh['rep'=2,'ep'=4,'node'=2,'sub'=2] {'sub'}, dimensions={0}, use_global_device_ids=true | all-gather | bytes 3072 | tf_op jit(solution)/shard_map/all_gather | solution.py:383
  29.2 1.0 %shard_map.106.refs_2_.info_ref = f32[2,64,4]{2,1,0:T(8,128)S(1)} custom-call(f32[2,4,64]{2,1,0:T(4,128)S(1)} %all-gather.4.parts_ref, f32[4,64]{1,0:T(4,128)S(1)} %get-tuple-element.27.place_ref, s32[1,4]{1,0:T(1,128)} %bitcast.46, s32[2,64]{1,0:T(2,128)} %bitcast.43), custom_call_target="tpu_custom_call" | custom-call | tf_op jit(solution)/shard_map/pallas_call | solution.py:216
  30.3 0.0 collective-permute-done.3
  30.3 0.0 collective-permute-done.4
  30.3 0.1 pad_maximum_fusion.rows_ref
  30.4 1.4 %shard_map.107 = (f32[160,1024]{1,0:T(8,128)S(1)}, bf16[160,1024]{1,0:T(8,128)(2,1)S(1)}) custom-call(bf16[160,3584]{1,0:T(8,128)(2,1)S(1)} %pad_maximum_fusion.rows_ref, bf16[3584,512]{1,0:T(8,128)(2,1)S(1)} %get-tuple-element.23.refs_0_, bf16[3584,512]{1,0:T(8,128)(2,1)S(1)} %get-tuple-element.28.refs_1_, f32[2,64,4]{2,1,0:T(8,128)S(1)} %shard_map.106.refs_2_.info_ref), custom_call_target="tpu_custom_call" | custom-call | tf_op jit(solution)/shard_map/pallas_call | solution.py:244
  31.7 2.3 %all-gather.1 = bf16[320,1024]{1,0:T(8,128)(2,1)S(1)} all-gather(bf16[160,1024]{1,0:T(8,128)(2,1)S(1)} %get-tuple-element.30), channel_id=3, replica_groups=mesh['rep'=2,'ep'=4,'node'=2,'sub'=2] {'sub'}, dimensions={0}, use_global_device_ids=true | all-gather | bytes 983040 | tf_op jit(solution)/shard_map/all_gather | solution.py:366
  34.0 0.1 shard_map.108.refs_0_
  34.2 0.5 collective-permute-start.5
  34.7 1.6 %collective-permute-done.8 = bf16[40,3584]{1,0:T(8,128)(2,1)S(1)} collective-permute-done((bf16[40,3584]{1,0:T(8,128)(2,1)S(1)}, bf16[40,3584]{1,0:T(8,128)(2,1)S(1)}, u32[]{:S(2)}, u32[]{:S(2)}) %collective-permute-start.8) | collective-permute-done | bytes 286752 | tf_op jit(solution)/shard_map/ppermute | solution.py:23
  36.3 0.5 collective-permute-start.9
  36.8 0.0 collective-permute-done.6.refs_3_
  36.8 4.4 %collective-permute-done.5.refs_1_ = bf16[160,512]{1,0:T(8,128)(2,1)S(1)} collective-permute-done((bf16[160,512]{1,0:T(8,128)(2,1)S(1)}, bf16[160,512]{1,0:T(8,128)(2,1)S(1)}, u32[]{:S(2)}, u32[]{:S(2)}) %collective-permute-start.5) | collective-permute-done | bytes 163872 | tf_op jit(solution)/shard_map/ppermute | solution.py:23
  41.3 0.8 %shard_map.109 = bf16[160,1792]{1,0:T(8,128)(2,1)S(1)} custom-call(bf16[160,512]{1,0:T(8,128)(2,1)S(1)} %shard_map.108.refs_0_, bf16[160,512]{1,0:T(8,128)(2,1)S(1)} %collective-permute-done.5.refs_1_, bf16[1024,1792]{1,0:T(8,128)(2,1)S(1)} %get-tuple-element.31.refs_2_, bf16[40,3584]{1,0:T(8,128)(2,1)S(1)} %collective-permute-done.6.refs_3_), custom_call_target="tpu_custom_call" | custom-call | tf_op jit(solution)/shard_map/pallas_call | solution.py:265
  42.1 1.0 %collective-permute-start.7 = (bf16[2,40,1792]{2,1,0:T(8,128)(2,1)S(1)}, bf16[2,40,1792]{2,1,0:T(8,128)(2,1)S(1)}, u32[]{:S(2)}, u32[]{:S(2)}) collective-permute-start(bf16[2,40,1792]{2,1,0:T(8,128)(2,1)S(1)} %slice_bitcast_fusion), channel_id=1, source_target_pairs={{0,8},{4,12},{8,0},{12,4},{1,9},{5,13},{9,1},{13,5},{2,10},{6,14},... | collective-permute-start | bytes 860168 | tf_op jit(solution)/shard_map/ppermute | solution.py:23
  43.1 3.6 %collective-permute-done.9 = bf16[40,3584]{1,0:T(8,128)(2,1)S(1)} collective-permute-done((bf16[40,3584]{1,0:T(8,128)(2,1)S(1)}, bf16[40,3584]{1,0:T(8,128)(2,1)S(1)}, u32[]{:S(2)}, u32[]{:S(2)}) %collective-permute-start.9) | collective-permute-done | bytes 286752 | tf_op jit(solution)/shard_map/ppermute | solution.py:23
  46.7 0.1 pad_maximum_fusion.1.rows_ref
  46.8 1.4 %shard_map.110 = (f32[160,1024]{1,0:T(8,128)S(1)}, bf16[160,1024]{1,0:T(8,128)(2,1)S(1)}) custom-call(bf16[160,3584]{1,0:T(8,128)(2,1)S(1)} %pad_maximum_fusion.1.rows_ref, bf16[3584,512]{1,0:T(8,128)(2,1)S(1)} %get-tuple-element.23.refs_0_, bf16[3584,512]{1,0:T(8,128)(2,1)S(1)} %get-tuple-element.28.refs_1_, bf16[2,2,40,1792]{3,2,1,0:T(8,128)(2,1)S(1)} %bitcast.30), custom_call_target="tpu_custom_call" | custom-call | tf_op jit(solution)/shard_map/pallas_call | solution.py:244
  48.1 2.3 %all-gather.2 = bf16[320,1024]{1,0:T(8,128)(2,1)S(1)} all-gather(bf16[160,1024]{1,0:T(8,128)(2,1)S(1)} %get-tuple-element.34), channel_id=4, replica_groups=mesh['rep'=2,'ep'=4,'node'=2,'sub'=2] {'sub'}, dimensions={0}, use_global_device_ids=true | all-gather | bytes 983040 | tf_op jit(solution)/shard_map/all_gather | solution.py:366
  50.4 0.1 shard_map.111.refs_0_
  50.6 6.9 %all-gather.3 = bf16[320,512]{1,0:T(8,128)(2,1)S(1)} all-gather(bf16[160,512]{1,0:T(8,128)(2,1)S(1)} %pad_maximum_fusion.5), channel_id=5, replica_groups=mesh['rep'=2,'ep'=4,'node'=2,'sub'=2] {'node'}, dimensions={0}, use_global_device_ids=true | all-gather | bytes 491520 | tf_op jit(solution)/shard_map/all_gather | solution.py:374
  57.5 0.8 %shard_map.112 = bf16[160,1792]{1,0:T(8,128)(2,1)S(1)} custom-call(bf16[160,512]{1,0:T(8,128)(2,1)S(1)} %shard_map.111.refs_0_, bf16[2,160,512]{2,1,0:T(8,128)(2,1)S(1)} %bitcast.35, bf16[1024,1792]{1,0:T(8,128)(2,1)S(1)} %get-tuple-element.31.refs_2_), custom_call_target="tpu_custom_call" | custom-call | tf_op jit(solution)/shard_map/pallas_call | solution.py:265
  58.2 0.0 collective-permute-done.7
  58.3 0.5 collective-permute-start.10
  58.9 1.2 %collective-permute-start.11 = (bf16[40,1792]{1,0:T(8,128)(2,1)S(1)}, bf16[40,1792]{1,0:T(8,128)(2,1)S(1)}, u32[]{:S(2)}, u32[]{:S(2)}) collective-permute-start(bf16[40,1792]{1,0:T(8,128)(2,1)S(1)} %get-tuple-element.40), channel_id=1, source_target_pairs={{0,4},{4,0},{8,12},{12,8},{1,5},{5,1},{9,13},{13,9},{2,6},{6,2},{1... | collective-permute-start | bytes 430088 | tf_op jit(solution)/shard_map/ppermute | solution.py:23
  60.1 1.4 %collective-permute-start.12 = (bf16[40,1792]{1,0:T(8,128)(2,1)S(1)}, bf16[40,1792]{1,0:T(8,128)(2,1)S(1)}, u32[]{:S(2)}, u32[]{:S(2)}) collective-permute-start(bf16[40,1792]{1,0:T(8,128)(2,1)S(1)} %get-tuple-element.39), channel_id=1, source_target_pairs={{0,12},{4,8},{8,4},{12,0},{1,13},{5,9},{9,5},{13,1},{2,14},{6,10},... | collective-permute-start | bytes 430088 | tf_op jit(solution)/shard_map/ppermute | solution.py:23
  61.5 1.4 %collective-permute-start.13 = (bf16[40,1792]{1,0:T(8,128)(2,1)S(1)}, bf16[40,1792]{1,0:T(8,128)(2,1)S(1)}, u32[]{:S(2)}, u32[]{:S(2)}) collective-permute-start(bf16[40,1792]{1,0:T(8,128)(2,1)S(1)} %get-tuple-element.38), channel_id=1, source_target_pairs={{0,6},{2,4},{4,2},{6,0},{8,14},{10,12},{12,10},{14,8},{1,7},{3,5},... | collective-permute-start | bytes 430088 | tf_op jit(solution)/shard_map/ppermute | solution.py:39
  62.8 2.1 %collective-permute-start.14 = (bf16[40,1792]{1,0:T(8,128)(2,1)S(1)}, bf16[40,1792]{1,0:T(8,128)(2,1)S(1)}, u32[]{:S(2)}, u32[]{:S(2)}) collective-permute-start(bf16[40,1792]{1,0:T(8,128)(2,1)S(1)} %get-tuple-element.37), channel_id=1, source_target_pairs={{0,14},{2,12},{4,10},{6,8},{8,6},{10,4},{12,2},{14,0},{1,15},{3,13... | collective-permute-start | bytes 430088 | tf_op jit(solution)/shard_map/ppermute | solution.py:39
  65.0 2.6 %collective-permute-done.10.refs_1_ = bf16[2,40,1792]{2,1,0:T(8,128)(2,1)S(1)} collective-permute-done((bf16[2,40,1792]{2,1,0:T(8,128)(2,1)S(1)}, bf16[2,40,1792]{2,1,0:T(8,128)(2,1)S(1)}, u32[]{:S(2)}, u32[]{:S(2)}) %collective-permute-start.10) | collective-permute-done | bytes 286752 | tf_op jit(solution)/shard_map/ppermute | solution.py:23
  67.6 0.7 shard_map.114
  68.3 0.6 collective-permute-done.12.refs_3_
  68.9 2.9 %collective-permute-done.13.refs_4_ = bf16[40,1792]{1,0:T(8,128)(2,1)S(1)} collective-permute-done((bf16[40,1792]{1,0:T(8,128)(2,1)S(1)}, bf16[40,1792]{1,0:T(8,128)(2,1)S(1)}, u32[]{:S(2)}, u32[]{:S(2)}) %collective-permute-start.13) | collective-permute-done | bytes 143392 | tf_op jit(solution)/shard_map/ppermute | solution.py:39
  71.8 3.0 %collective-permute-done.14.refs_5_ = bf16[40,1792]{1,0:T(8,128)(2,1)S(1)} collective-permute-done((bf16[40,1792]{1,0:T(8,128)(2,1)S(1)}, bf16[40,1792]{1,0:T(8,128)(2,1)S(1)}, u32[]{:S(2)}, u32[]{:S(2)}) %collective-permute-start.14) | collective-permute-done | bytes 143392 | tf_op jit(solution)/shard_map/ppermute | solution.py:39
  74.8 1.9 %shard_map.115 = bf16[64,3584]{1,0:T(8,128)(2,1)} custom-call(f32[2,64,4]{2,1,0:T(8,128)S(1)} %shard_map.106.refs_2_.info_ref, f32[64,1792]{1,0:T(8,128)S(1)} %get-tuple-element.35.refs_0_, f32[64,1792]{1,0:T(8,128)S(1)} %get-tuple-element.36.refs_1_, bf16[40,1792]{1,0:T(8,128)(2,1)S(1)} %collective-permute-done.11.refs_2_, ...), custom_call_target="tpu_custom_call" | custom-call | tf_op jit(solution)/shard_map/pallas_call | solution.py:313
  (14 shorter events, 0.2 us)
Async XLA Ops:
  3.0 16.0 %collective-permute-start = (bf16[40,3584]{1,0:T(8,128)(2,1)S(1)}, bf16[40,3584]{1,0:T(8,128)(2,1)S(1)}, u32[]{:S(2)}, u32[]{:S(2)}) collective-permute-start(bf16[40,3584]{1,0:T(8,128)(2,1)S(1)} %get-tuple-element.24), channel_id=1, source_target_pairs={{0,4},{4,0},{8,12},{12,8},{1,5},{5,1},{9,13},{13,9},{2,6},{6,2},{1... | collective-permute-start | bytes 860168 | tf_op jit(solution)/shard_map/ppermute | solution.py:23
  6.1 15.4 %collective-permute-start.1 = (bf16[40,3584]{1,0:T(8,128)(2,1)S(1)}, bf16[40,3584]{1,0:T(8,128)(2,1)S(1)}, u32[]{:S(2)}, u32[]{:S(2)}) collective-permute-start(bf16[40,3584]{1,0:T(8,128)(2,1)S(1)} %get-tuple-element.21.refs_0_), channel_id=1, source_target_pairs={{0,8},{4,12},{8,0},{12,4},{1,9},{5,13},{9,1},{13,5},{2,10},{6,14},... | collective-permute-start | bytes 860168 | tf_op jit(solution)/shard_map/ppermute | solution.py:23
  8.7 14.3 %collective-permute-start.2 = (bf16[40,3584]{1,0:T(8,128)(2,1)S(1)}, bf16[40,3584]{1,0:T(8,128)(2,1)S(1)}, u32[]{:S(2)}, u32[]{:S(2)}) collective-permute-start(bf16[40,3584]{1,0:T(8,128)(2,1)S(1)} %get-tuple-element.24), channel_id=1, source_target_pairs={{0,2},{2,0},{1,3},{3,1},{4,6},{6,4},{5,7},{7,5},{8,10},{10,8},{9,1... | collective-permute-start | bytes 860168 | tf_op jit(solution)/shard_map/ppermute | solution.py:23
  10.2 20.1 %collective-permute-start.3 = (bf16[40,3584]{1,0:T(8,128)(2,1)S(1)}, bf16[40,3584]{1,0:T(8,128)(2,1)S(1)}, u32[]{:S(2)}, u32[]{:S(2)}) collective-permute-start(bf16[40,3584]{1,0:T(8,128)(2,1)S(1)} %get-tuple-element.22.refs_3_), channel_id=1, source_target_pairs={{0,2},{2,0},{1,3},{3,1},{4,6},{6,4},{5,7},{7,5},{8,10},{10,8},{9,1... | collective-permute-start | bytes 860168 | tf_op jit(solution)/shard_map/ppermute | solution.py:23
  21.5 8.8 %collective-permute-start.4 = (bf16[40,3584]{1,0:T(8,128)(2,1)S(1)}, bf16[40,3584]{1,0:T(8,128)(2,1)S(1)}, u32[]{:S(2)}, u32[]{:S(2)}) collective-permute-start(bf16[40,3584]{1,0:T(8,128)(2,1)S(1)} %shard_map.103.refs_0_), channel_id=1, source_target_pairs={{0,2},{2,0},{1,3},{3,1},{4,6},{6,4},{5,7},{7,5},{8,10},{10,8},{9,1... | collective-permute-start | bytes 860168 | tf_op jit(solution)/shard_map/ppermute | solution.py:23
  23.0 13.9 %collective-permute-start.6 = (bf16[40,3584]{1,0:T(8,128)(2,1)S(1)}, bf16[40,3584]{1,0:T(8,128)(2,1)S(1)}, u32[]{:S(2)}, u32[]{:S(2)}) collective-permute-start(bf16[40,3584]{1,0:T(8,128)(2,1)S(1)} %get-tuple-element.26.refs_5_), channel_id=1, source_target_pairs={{0,4},{4,0},{8,12},{12,8},{1,5},{5,1},{9,13},{13,9},{2,6},{6,2},{1... | collective-permute-start | bytes 860168 | tf_op jit(solution)/shard_map/ppermute | solution.py:23
  23.4 12.9 %collective-permute-start.8 = (bf16[40,3584]{1,0:T(8,128)(2,1)S(1)}, bf16[40,3584]{1,0:T(8,128)(2,1)S(1)}, u32[]{:S(2)}, u32[]{:S(2)}) collective-permute-start(bf16[40,3584]{1,0:T(8,128)(2,1)S(1)} %get-tuple-element.32), channel_id=1, source_target_pairs={{0,12},{4,8},{8,4},{12,0},{1,13},{5,9},{9,5},{13,1},{2,14},{6,10},... | collective-permute-start | bytes 860168 | tf_op jit(solution)/shard_map/ppermute | solution.py:23
  34.2 7.1 %collective-permute-start.5 = (bf16[160,512]{1,0:T(8,128)(2,1)S(1)}, bf16[160,512]{1,0:T(8,128)(2,1)S(1)}, u32[]{:S(2)}, u32[]{:S(2)}) collective-permute-start(bf16[160,512]{1,0:T(8,128)(2,1)S(1)} %pad_maximum_fusion.4), channel_id=1, source_target_pairs={{0,2},{2,0},{1,3},{3,1},{4,6},{6,4},{5,7},{7,5},{8,10},{10,8},{9,1... | collective-permute-start | bytes 491528 | tf_op jit(solution)/shard_map/ppermute | solution.py:23
  36.3 10.4 %collective-permute-start.9 = (bf16[40,3584]{1,0:T(8,128)(2,1)S(1)}, bf16[40,3584]{1,0:T(8,128)(2,1)S(1)}, u32[]{:S(2)}, u32[]{:S(2)}) collective-permute-start(bf16[40,3584]{1,0:T(8,128)(2,1)S(1)} %collective-permute-done.8), channel_id=1, source_target_pairs={{0,2},{2,0},{1,3},{3,1},{4,6},{6,4},{5,7},{7,5},{8,10},{10,8},{9,1... | collective-permute-start | bytes 860168 | tf_op jit(solution)/shard_map/ppermute | solution.py:23
  42.1 16.2 %collective-permute-start.7 = (bf16[2,40,1792]{2,1,0:T(8,128)(2,1)S(1)}, bf16[2,40,1792]{2,1,0:T(8,128)(2,1)S(1)}, u32[]{:S(2)}, u32[]{:S(2)}) collective-permute-start(bf16[2,40,1792]{2,1,0:T(8,128)(2,1)S(1)} %slice_bitcast_fusion), channel_id=1, source_target_pairs={{0,8},{4,12},{8,0},{12,4},{1,9},{5,13},{9,1},{13,5},{2,10},{6,14},... | collective-permute-start | bytes 860168 | tf_op jit(solution)/shard_map/ppermute | solution.py:23
  58.3 9.3 %collective-permute-start.10 = (bf16[2,40,1792]{2,1,0:T(8,128)(2,1)S(1)}, bf16[2,40,1792]{2,1,0:T(8,128)(2,1)S(1)}, u32[]{:S(2)}, u32[]{:S(2)}) collective-permute-start(bf16[2,40,1792]{2,1,0:T(8,128)(2,1)S(1)} %shard_map.113), channel_id=1, source_target_pairs={{0,2},{2,0},{1,3},{3,1},{4,6},{6,4},{5,7},{7,5},{8,10},{10,8},{9,1... | collective-permute-start | bytes 860168 | tf_op jit(solution)/shard_map/ppermute | solution.py:23
  58.9 9.4 %collective-permute-start.11 = (bf16[40,1792]{1,0:T(8,128)(2,1)S(1)}, bf16[40,1792]{1,0:T(8,128)(2,1)S(1)}, u32[]{:S(2)}, u32[]{:S(2)}) collective-permute-start(bf16[40,1792]{1,0:T(8,128)(2,1)S(1)} %get-tuple-element.40), channel_id=1, source_target_pairs={{0,4},{4,0},{8,12},{12,8},{1,5},{5,1},{9,13},{13,9},{2,6},{6,2},{1... | collective-permute-start | bytes 430088 | tf_op jit(solution)/shard_map/ppermute | solution.py:23
  60.1 8.8 %collective-permute-start.12 = (bf16[40,1792]{1,0:T(8,128)(2,1)S(1)}, bf16[40,1792]{1,0:T(8,128)(2,1)S(1)}, u32[]{:S(2)}, u32[]{:S(2)}) collective-permute-start(bf16[40,1792]{1,0:T(8,128)(2,1)S(1)} %get-tuple-element.39), channel_id=1, source_target_pairs={{0,12},{4,8},{8,4},{12,0},{1,13},{5,9},{9,5},{13,1},{2,14},{6,10},... | collective-permute-start | bytes 430088 | tf_op jit(solution)/shard_map/ppermute | solution.py:23
  61.5 10.4 %collective-permute-start.13 = (bf16[40,1792]{1,0:T(8,128)(2,1)S(1)}, bf16[40,1792]{1,0:T(8,128)(2,1)S(1)}, u32[]{:S(2)}, u32[]{:S(2)}) collective-permute-start(bf16[40,1792]{1,0:T(8,128)(2,1)S(1)} %get-tuple-element.38), channel_id=1, source_target_pairs={{0,6},{2,4},{4,2},{6,0},{8,14},{10,12},{12,10},{14,8},{1,7},{3,5},... | collective-permute-start | bytes 430088 | tf_op jit(solution)/shard_map/ppermute | solution.py:39
  62.8 11.9 %collective-permute-start.14 = (bf16[40,1792]{1,0:T(8,128)(2,1)S(1)}, bf16[40,1792]{1,0:T(8,128)(2,1)S(1)}, u32[]{:S(2)}, u32[]{:S(2)}) collective-permute-start(bf16[40,1792]{1,0:T(8,128)(2,1)S(1)} %get-tuple-element.37), channel_id=1, source_target_pairs={{0,14},{2,12},{4,10},{6,8},{8,6},{10,4},{12,2},{14,0},{1,15},{3,13... | collective-permute-start | bytes 430088 | tf_op jit(solution)/shard_map/ppermute | solution.py:39

commit v3 on v2

--- a/solution.py
+++ b/solution.py
@@ -66,13 +66,13 @@
     return pltpu.with_memory_space_constraint(value, pltpu.HBM)
 
 
-def pack_rows(expert_place, routes_t, tokens, order, cap, behind=()):
+def pack_rows(expert_place, routes_t, tokens, order, cap):
     experts = expert_place.shape[0]
     topk, tok_rows = routes_t.shape
     width = tokens.shape[1]
 
     def kernel(where_hbm, routes_hbm, tokens_hbm, *refs):
-        place_ref, *refs = refs[len(behind) :]
+        place_ref, *refs = refs
         block_refs, (where_ref, routes_ref, tokens_ref, sems) = refs[: len(order)], refs[len(order) :]
         pairs = [(where_hbm, where_ref), (routes_hbm, routes_ref), (tokens_hbm, tokens_ref)]
         copies = [pltpu.make_async_copy(a, b, sems.at[i]) for i, (a, b) in enumerate(pairs)]
@@ -115,8 +115,8 @@
         pltpu.VMEM((tok_rows, width), bf16),
         pltpu.SemaphoreType.DMA((3,)),
     ]
-    return call(kernel, shapes, [IN_HBM] * 3 + [ANY] * len(behind), scratch)(
-        in_hbm(expert_place.reshape(1, experts)), in_hbm(routes_t), in_hbm(tokens), *behind
+    return call(kernel, shapes, [IN_HBM] * 3, scratch)(
+        in_hbm(expert_place.reshape(1, experts)), in_hbm(routes_t), in_hbm(tokens)
     )
 
 
@@ -188,12 +188,13 @@
     return call(kernel, shapes, specs, scratch)(*[in_hbm(a) for a in given], *behind)[0]
 
 
-def route_info(parts, place, expert_place, routes_t):
+def route_info(parts, place, expert_place, routes_t, behind):
     _, experts, tok_rows = parts.shape
     topk = routes_t.shape[0]
     given = [expert_place.reshape(1, experts), routes_t]
 
-    def kernel(parts_ref, place_ref, where_hbm, routes_hbm, out_ref, where_ref, routes_ref, sems):
+    def kernel(parts_ref, place_ref, where_hbm, routes_hbm, *refs):
+        out_ref, where_ref, routes_ref, sems = refs[len(behind) :]
         fetch([where_hbm, routes_hbm], [where_ref, routes_ref], sems)
         score = jax.nn.sigmoid(functools.reduce(jnp.add, [parts_ref[i] for i in range(parts.shape[0])]))
         expert = lax.broadcasted_iota(jnp.int32, (experts, tok_rows), 0)
@@ -213,8 +214,8 @@
     shapes = [jax.ShapeDtypeStruct((2, tok_rows, experts), f32)]
     scratch = [pltpu.VMEM(a.shape, a.dtype) for a in given]
     scratch.append(pltpu.SemaphoreType.DMA((len(given),)))
-    return call(kernel, shapes, [WHOLE] * 2 + [IN_HBM] * 2, scratch)(
-        parts, place, *[in_hbm(a) for a in given]
+    return call(kernel, shapes, [WHOLE] * 2 + [IN_HBM] * 2 + [ANY] * len(behind), scratch)(
+        parts, place, *[in_hbm(a) for a in given], *behind
     )[0]
 
 
@@ -265,44 +266,51 @@
     return call(kernel, shapes, specs)(*by_node, weight, *behind)[0]
 
 
-def weighted_sum(info, pieces):
-    tok_rows = info.shape[1]
-    total = None
-    for k, value in pieces:
-        row = lax.broadcasted_iota(jnp.int32, (tok_rows, value.shape[0]), 1).astype(f32)
-        factor = jnp.where(info[0, :, k : k + 1] == row, info[1, :, k : k + 1], f32(0.0))
-        high = factor.astype(bf16)
-        low = (factor - high.astype(f32)).astype(bf16)
-        for part in (high, low):
-            product = jnp.dot(part, value, preferred_element_type=f32)
-            total = product if total is None else total + product
-    return total
-
-
-def combine_early(info, order, pieces):
-    width = pieces[0].shape[-1]
-    tok_rows = info.shape[1]
+def weighted_sum(given, pieces):
+    return functools.reduce(
+        jnp.add, [jnp.dot(given[k], rows, preferred_element_type=f32) for k, rows in pieces]
+    )
+
+
+def combine_early(info, pieces, cap):
+    _, tok_rows, count = info.shape
+    flat = [rows for part in pieces for _, rows in part]
+    width = flat[0].shape[1]
 
     def kernel(info_ref, *refs):
-        for piece, out in zip(refs, refs[len(pieces) :]):
-            out[...] = weighted_sum(info_ref[...], [(k, piece[i]) for i, k in enumerate(order)])
-
-    shapes = [jax.ShapeDtypeStruct((tok_rows, width), f32)] * len(pieces)
-    return call(kernel, shapes, [WHOLE] * (1 + len(pieces)))(info, *pieces)
-
-
-def combine_late(info, early, pieces):
-    nodes = len(early)
-    order = [k for k, _ in pieces[0]]
+        given_ref, *sum_refs = refs[len(flat) :]
+        row = lax.broadcasted_iota(jnp.int32, (tok_rows, cap), 1).astype(f32)
+        low = [None] * count
+        for k in range(count):
+            hit = info_ref[0, :, k : k + 1] == row
+            factor = jnp.where(hit, info_ref[1, :, k : k + 1], f32(0.0))
+            given_ref[k] = factor.astype(bf16)
+            low[k] = (factor - factor.astype(bf16).astype(f32)).astype(bf16)
+        rest = list(refs[: len(flat)])
+        for part, out in zip(pieces, sum_refs):
+            mine = [(k, rest.pop(0)[...]) for k, _ in part]
+            out[...] = weighted_sum(given_ref, mine) + weighted_sum(low, mine)
+
+    shapes = [jax.ShapeDtypeStruct((count, tok_rows, cap), bf16)]
+    shapes += [jax.ShapeDtypeStruct((tok_rows, width), f32)] * len(pieces)
+    given, *sums = call(kernel, shapes, [WHOLE] * (1 + len(flat)))(info, *flat)
+    return given, sums
+
+
+def combine_late(given, sums, pieces, order, across):
+    nodes = len(sums)
+    tok_rows, width = sums[0].shape
     flat = [rows for part in pieces for _, rows in part]
-    tok_rows, width = early[0].shape
-
-    def kernel(info_ref, *refs):
-        early_refs, late_refs, out_ref = refs[:nodes], refs[nodes:-1], refs[-1]
+
+    def kernel(given_ref, *refs):
+        sum_refs, rest, across_refs = refs[:nodes], list(refs[nodes:-nodes]), refs[-nodes:-1]
+        out_ref = refs[-1]
         node_me = lax.axis_index("node")
         for j in range(nodes):
-            mine = [(k, late_refs[j * len(order) + i][...]) for i, k in enumerate(order)]
-            value = (early_refs[j][...] + weighted_sum(info_ref[...], mine)).astype(bf16)
+            mine = [(k, rest.pop(0)[...]) for k, _ in pieces[j]]
+            if j:
+                mine += [(k, across_refs[j - 1][i]) for i, k in enumerate(order)]
+            value = (sum_refs[j][...] + weighted_sum(given_ref, mine)).astype(bf16)
             for at in range(nodes):
 
                 @pl.when(node_me ^ j == at)
@@ -310,7 +318,8 @@
                     out_ref[:, at * width : (at + 1) * width] = value
 
     shapes = [jax.ShapeDtypeStruct((tok_rows, nodes * width), bf16)]
-    return call(kernel, shapes, [WHOLE] * (1 + nodes + len(flat)))(info, *early, *flat)[0]
+    specs = [WHOLE] * (1 + nodes + len(flat) + len(across))
+    return call(kernel, shapes, specs)(given, *sums, *flat, *across)[0]
 
 
 def body(
@@ -338,9 +347,9 @@
     far = range(3 * quarter, eps)
     others = range(1, nodes)
     routes_t = routes.T
-    place, *first_out = pack_rows(expert_place, routes_t, tokens, [*middle], cap)
-    _, *later_out = pack_rows(expert_place, routes_t, tokens, [0, *near, *far], cap, first_out)
-    outgoing = dict(zip([*middle, 0, *near, *far], first_out + later_out))
+    order = [*middle, 0, *near, *far]
+    place, *packed = pack_rows(expert_place, routes_t, tokens, order, cap)
+    outgoing = dict(zip(order, packed))
 
     blocks = [[outgoing[k]] + [None] * (nodes - 1) for k in range(eps)]
     for k in [*middle, *near]:
@@ -350,15 +359,17 @@
     gate_w, up_w, down_w = load(
         [gate_weight[0], up_weight[0], down_weight[0, 0]], [outgoing[0]]
     )
-    for k, rows in zip(middle, hold([blocks[k][0] for k in middle], [gate_w, blocks[1][0]])):
+    logits = partial_logits(tokens, tenant, router_weight, adapter_down, adapter_up, [gate_w])
+    logits = lax.all_gather(logits, "sub")
+    for k, rows in zip(far, hold([outgoing[k] for k in far], [logits])):
+        blocks[k][0] = swap(rows, "ep", k)
+    for k, rows in zip(middle, hold([blocks[k][0] for k in middle], [logits])):
         blocks[k] = [rows] + [swap(rows, "node", j) for j in others]
     crossed = [blocks[k][j] for k in near for j in others]
-    crossed = hold(crossed + [outgoing[k] for k in far], [blocks[middle[-1]][0]])
+    crossed = hold(crossed, [blocks[k][0] for k in (middle[-1], *near)])
     for i, k in enumerate(near):
         for j in others:
             blocks[k][j] = swap(crossed[i * len(others) + j - 1], "ep", k)
-    for i, k in enumerate(far):
-        blocks[k][0] = swap(crossed[len(near) * len(others) + i], "ep", k)
 
     def gate_up(chunk, behind):
         rows = [blocks[k][j] for j in range(nodes) for k in chunk]
@@ -377,29 +388,27 @@
         out = project(by_node, down_w, behind)
         return out.reshape(nodes, len(chunk), cap, out_width)
 
-    logits = partial_logits(
-        tokens, tenant, router_weight, adapter_down, adapter_up, crossed[:1]
-    )
-    info = route_info(lax.all_gather(logits, "sub"), place, expert_place, routes_t)
-
-    early_chunk, late_chunk = [0, *middle], [*near, *far]
+    info = route_info(logits, place, expert_place, routes_t, crossed[:1])
+
+    early_chunk, late_chunk = [0, *middle], [*far, *near]
     hidden = gate_up(early_chunk, [info])
-    for k in far:
-        for j in others:
-            blocks[k][j] = swap(blocks[k][0], "node", j)
+    for k, rows in zip(far, hold([blocks[k][0] for k in far], [hidden])):
+        blocks[k] = [rows] + [swap(rows, "node", j) for j in others]
     early_out = down(early_chunk, hidden, behind=[blocks[k][j] for k in near for j in others])
     hidden = gate_up(late_chunk, [early_out])
-    late_out = down(late_chunk, hidden, True)
-
     back = [early_out[:, 0]]
     back += [swap(early_out[:, i], "ep", k) for i, k in enumerate(early_chunk) if k]
+    late_out = down(late_chunk, hidden, False, back[1:])
     late = [
         [(k, send(late_out[j, i], k, j)) for i, k in enumerate(late_chunk)] for j in range(nodes)
     ]
-    across = [jnp.stack([part[j] for part in back]) for j in range(nodes)]
-    across[1:] = hold(across[1:], [late_out])
-    across[1:] = [swap(across[j], "node", j) for j in others]
-    return combine_late(info, combine_early(info, early_chunk, across), late)
+    across = hold([jnp.stack([part[j] for part in back]) for j in others], [late_out])
+    across = [swap(rows, "node", j) for j, rows in zip(others, across)]
+    count = len(far)
+    pieces = [part[:count] for part in late]
+    pieces[0] = pieces[0] + [(k, part[0]) for k, part in zip(early_chunk, back)]
+    given, sums = combine_early(info, pieces, cap)
+    return combine_late(given, sums, [part[count:] for part in late], early_chunk, across)
 
 
 def solution(mesh):

time: 76.9 us -> 74.2 us (0.965)
  blocking collectives: 13.2 us -> 6.33 us
  starting transfers between devices: 20.4 us -> 25.1 us
  Pallas kernels: 17.2 us -> 15.3 us
  waiting for transfers between devices: 25.2 us -> 26.8 us
    all_gather x2 -> x1, blocking collectives: 8.7 us -> 1.78 us  [body(): logits = lax.all_gather(logits, 'sub')]
    ppermute x13 -> x14, starting transfers between devices: 16.9 us -> 21.7 us  [swap(): lax.ppermute(value, axis, [(i, partner(i, step)) for i in range(count)])]
    pallas_call x5 -> x4, Pallas kernels: 6.6 us -> 4.67 us  [the longest x1 1.57 us: pack_rows(): call(kernel, shapes, [IN_HBM] * 3, scratch)]
    ppermute x2, waiting for transfers between devices: 5.88 us -> 7.73 us  [send(): return lax.ppermute(value, ('ep', 'node'), pairs)]
    ppermute x13 -> x14, waiting for transfers between devices: 19.4 us -> 19 us  [swap(): lax.ppermute(value, axis, [(i, partner(i, step)) for i in range(count)])]
  transfers between devices with their start and end apart: 15 -> 16, of which waited for: 9 -> 10; matrix products, arithmetic and copies ran while one was open for 0% -> 0% of each run, Pallas kernels for 16% -> 16%
where the time goes in v3:
time: 74.2 us; the launch traced here: 74 us
  waiting for transfers between devices  26.8 us (36%)
  starting transfers between devices  25.1 us (34%)
  Pallas kernels  15.3 us (21%)
  blocking collectives  6.33 us (9%)
    ppermute x14, starting transfers between devices, swap(): lax.ppermute(value, axis, [(i, partner(i, step)) for i in range(count)])  21.7 us
    ppermute x14, waiting for transfers between devices, swap(): lax.ppermute(value, axis, [(i, partner(i, step)) for i in range(count)])  19 us
    ppermute x2, waiting for transfers between devices, send(): return lax.ppermute(value, ('ep', 'node'), pairs)  7.73 us
    all_gather x2, blocking collectives, gate_up(): return activate(own, lax.all_gather(sent, 'sub'))  4.55 us
    pallas_call x1, Pallas kernels, load(): call(kernel, shapes, specs, [pltpu.SemaphoreType.DMA((count,))])  4.23 us
    ppermute x2, starting transfers between devices, send(): return lax.ppermute(value, ('ep', 'node'), pairs)  3.35 us
    pallas_call x2, Pallas kernels, dots(): return call(kernel, shapes, specs)(rows, *weights, *behind)  2.71 us
    pallas_call x1, Pallas kernels, partial_logits(): call(kernel, shapes, specs, scratch)(*[in_hbm(a) for a in given], *behind)  1.93 us
  transfers between devices with their start and end apart: 16, of which 10 were waited for; matrix products, arithmetic and copies ran while one was open for 0% of the time, Pallas kernels for 16%

profile of v3, /device:TPU:0, one launch (start us, length us, event | category | flops | bytes accessed | tf_op | source)
XLA Modules:
  0.0 74.0 jit_solution(15812554928202053661)
XLA Ops:
  0.0 1.6 %shard_map.100 = (f32[4,64]{1,0:T(4,128)S(1)}, bf16[40,3584]{1,0:T(8,128)(2,1)S(1)}, bf16[40,3584]{1,0:T(8,128)(2,1)S(1)}, bf16[40,3584]{1,0:T(8,128)(2,1)S(1)}, bf16[40,3584]{1,0:T(8,128)(2,1)S(1)}) custom-call(s32[1,4]{1,0:T(1,128)} %bitcast.45, s32[2,64]{1,0:T(2,128)} %bitcast.43, bf16[64,3584]{1,0:T(8,128)(2,1)} %refs_0_.1), custom_call_target="tpu_custom_call" | custom-call | tf_op jit(solution)/shard_map/pallas_call | solution.py:118
  1.6 4.1 %collective-permute-start = (bf16[40,3584]{1,0:T(8,128)(2,1)S(1)}, bf16[40,3584]{1,0:T(8,128)(2,1)S(1)}, u32[]{:S(2)}, u32[]{:S(2)}) collective-permute-start(bf16[40,3584]{1,0:T(8,128)(2,1)S(1)} %get-tuple-element.23), channel_id=1, source_target_pairs={{0,8},{4,12},{8,0},{12,4},{1,9},{5,13},{9,1},{13,5},{2,10},{6,14},... | collective-permute-start | bytes 860168 | tf_op jit(solution)/shard_map/ppermute | solution.py:23
  5.7 1.6 %collective-permute-start.1 = (bf16[40,3584]{1,0:T(8,128)(2,1)S(1)}, bf16[40,3584]{1,0:T(8,128)(2,1)S(1)}, u32[]{:S(2)}, u32[]{:S(2)}) collective-permute-start(bf16[40,3584]{1,0:T(8,128)(2,1)S(1)} %get-tuple-element.24), channel_id=1, source_target_pairs={{0,4},{4,0},{8,12},{12,8},{1,5},{5,1},{9,13},{13,9},{2,6},{6,2},{1... | collective-permute-start | bytes 860168 | tf_op jit(solution)/shard_map/ppermute | solution.py:23
  7.3 1.5 %collective-permute-start.2 = (bf16[40,3584]{1,0:T(8,128)(2,1)S(1)}, bf16[40,3584]{1,0:T(8,128)(2,1)S(1)}, u32[]{:S(2)}, u32[]{:S(2)}) collective-permute-start(bf16[40,3584]{1,0:T(8,128)(2,1)S(1)} %get-tuple-element.24), channel_id=1, source_target_pairs={{0,2},{2,0},{1,3},{3,1},{4,6},{6,4},{5,7},{7,5},{8,10},{10,8},{9,1... | collective-permute-start | bytes 860168 | tf_op jit(solution)/shard_map/ppermute | solution.py:23
  8.8 0.5 collective-permute-start.3
  9.3 4.2 %shard_map.101 = (bf16[3584,512]{1,0:T(8,128)(2,1)S(1)}, bf16[3584,512]{1,0:T(8,128)(2,1)S(1)}, bf16[1024,1792]{1,0:T(8,128)(2,1)S(1)}) custom-call(bf16[3584,512]{1,0:T(8,128)(2,1)} %bitcast.39, bf16[3584,512]{1,0:T(8,128)(2,1)} %bitcast.40, bf16[1024,1792]{1,0:T(8,128)(2,1)} %bitcast.41, bf16[40,3584]{1,0:T(8,128)(2,1)S(1)} %get-tuple-element.20.refs_3_), custom_call_target="tpu_custom_call" | custom-call | tf_op jit(solution)/shard_map/pallas_call | solution.py:139
  13.5 1.9 %shard_map.102 = f32[4,64]{1,0:T(4,128)S(1)} custom-call(bf16[64,3584]{1,0:T(8,128)(2,1)} %refs_0_.1, bf16[3584,128]{1,0:T(8,128)(2,1)} %refs_1_.1, bf16[4,3584]{1,0:T(4,128)(2,1)} %bitcast.42, bf16[4,128]{1,0:T(4,128)(2,1)} %bitcast.47, s32[1,64]{1,0:T(1,128)} %bitcast.48, bf16[3584,512]{1,0:T(8,128)(2,1)S(1)} %get-tuple-element.21.refs_5_.refs_0_), custom_call_target="tpu_custom_call" | custom-call | tf_op jit(solution)/shard_map/pallas_call | solution.py:188
  15.5 1.8 %all-gather.3.refs_0_.parts_ref = f32[2,4,64]{2,1,0:T(4,128)S(1)} all-gather(f32[1,4,64]{2,1,0:T(4,128)S(1)} %bitcast.38), channel_id=2, replica_groups=mesh['rep'=2,'ep'=4,'node'=2,'sub'=2] {'sub'}, dimensions={0}, use_global_device_ids=true | all-gather | bytes 3072 | tf_op jit(solution)/shard_map/all_gather | solution.py:363
  17.2 1.5 %collective-permute-done.refs_1_ = bf16[40,3584]{1,0:T(8,128)(2,1)S(1)} collective-permute-done((bf16[40,3584]{1,0:T(8,128)(2,1)S(1)}, bf16[40,3584]{1,0:T(8,128)(2,1)S(1)}, u32[]{:S(2)}, u32[]{:S(2)}) %collective-permute-start) | collective-permute-done | bytes 286752 | tf_op jit(solution)/shard_map/ppermute | solution.py:23
  18.8 1.5 %collective-permute-start.4 = (bf16[40,3584]{1,0:T(8,128)(2,1)S(1)}, bf16[40,3584]{1,0:T(8,128)(2,1)S(1)}, u32[]{:S(2)}, u32[]{:S(2)}) collective-permute-start(bf16[40,3584]{1,0:T(8,128)(2,1)S(1)} %shard_map.103.refs_0_), channel_id=1, source_target_pairs={{0,2},{2,0},{1,3},{3,1},{4,6},{6,4},{5,7},{7,5},{8,10},{10,8},{9,1... | collective-permute-start | bytes 860168 | tf_op jit(solution)/shard_map/ppermute | solution.py:23
  20.3 3.4 %collective-permute-start.5 = (bf16[40,3584]{1,0:T(8,128)(2,1)S(1)}, bf16[40,3584]{1,0:T(8,128)(2,1)S(1)}, u32[]{:S(2)}, u32[]{:S(2)}) collective-permute-start(bf16[40,3584]{1,0:T(8,128)(2,1)S(1)} %shard_map.108), channel_id=1, source_target_pairs={{0,12},{4,8},{8,4},{12,0},{1,13},{5,9},{9,5},{13,1},{2,14},{6,10},... | collective-permute-start | bytes 860168 | tf_op jit(solution)/shard_map/ppermute | solution.py:23
  23.7 0.0 collective-permute-done.1.refs_1_
  23.7 0.0 collective-permute-done.2.refs_2_
  23.7 0.0 collective-permute-start.7
  23.7 1.0 %shard_map.105.refs_2_.info_ref = f32[2,64,4]{2,1,0:T(8,128)S(1)} custom-call(f32[2,4,64]{2,1,0:T(4,128)S(1)} %all-gather.3.refs_0_.parts_ref, f32[4,64]{1,0:T(4,128)S(1)} %get-tuple-element.22.place_ref, s32[1,4]{1,0:T(1,128)} %bitcast.46, s32[2,64]{1,0:T(2,128)} %bitcast.44, bf16[40,3584]{1,0:T(8,128)(2,1)S(1)} %shard_map.104.refs_0_), custom_call_target="tpu_custom_call" | custom-call | tf_op jit(solution)/shard_map/pallas_call | solution.py:217
  24.8 0.0 collective-permute-done.3
  24.8 2.8 %collective-permute-done.4 = bf16[40,3584]{1,0:T(8,128)(2,1)S(1)} collective-permute-done((bf16[40,3584]{1,0:T(8,128)(2,1)S(1)}, bf16[40,3584]{1,0:T(8,128)(2,1)S(1)}, u32[]{:S(2)}, u32[]{:S(2)}) %collective-permute-start.4) | collective-permute-done | bytes 286752 | tf_op jit(solution)/shard_map/ppermute | solution.py:23
  27.6 0.1 pad_maximum_fusion.rows_ref
  27.7 1.4 %shard_map.106 = (f32[160,1024]{1,0:T(8,128)S(1)}, bf16[160,1024]{1,0:T(8,128)(2,1)S(1)}) custom-call(bf16[160,3584]{1,0:T(8,128)(2,1)S(1)} %pad_maximum_fusion.rows_ref, bf16[3584,512]{1,0:T(8,128)(2,1)S(1)} %get-tuple-element.21.refs_5_.refs_0_, bf16[3584,512]{1,0:T(8,128)(2,1)S(1)} %get-tuple-element.25.refs_1_, f32[2,64,4]{2,1,0:T(8,128)S(1)} %shard_map.105.refs_2_.info_ref), custom_call_target="tpu_custom_call" | custom-call | tf_op jit(solution)/shard_map/pallas_call | solution.py:245
  29.0 2.3 %all-gather.1 = bf16[320,1024]{1,0:T(8,128)(2,1)S(1)} all-gather(bf16[160,1024]{1,0:T(8,128)(2,1)S(1)} %get-tuple-element.27), channel_id=3, replica_groups=mesh['rep'=2,'ep'=4,'node'=2,'sub'=2] {'sub'}, dimensions={0}, use_global_device_ids=true | all-gather | bytes 983040 | tf_op jit(solution)/shard_map/all_gather | solution.py:377
  31.3 0.1 shard_map.107.refs_0_
  31.4 1.6 %collective-permute-start.8 = (bf16[160,512]{1,0:T(8,128)(2,1)S(1)}, bf16[160,512]{1,0:T(8,128)(2,1)S(1)}, u32[]{:S(2)}, u32[]{:S(2)}) collective-permute-start(bf16[160,512]{1,0:T(8,128)(2,1)S(1)} %pad_maximum_fusion.3), channel_id=1, source_target_pairs={{0,2},{2,0},{1,3},{3,1},{4,6},{6,4},{5,7},{7,5},{8,10},{10,8},{9,1... | collective-permute-start | bytes 491528 | tf_op jit(solution)/shard_map/ppermute | solution.py:23
  33.0 0.5 collective-permute-start.6
  33.5 3.1 %collective-permute-done.7.refs_3_ = bf16[40,3584]{1,0:T(8,128)(2,1)S(1)} collective-permute-done((bf16[40,3584]{1,0:T(8,128)(2,1)S(1)}, bf16[40,3584]{1,0:T(8,128)(2,1)S(1)}, u32[]{:S(2)}, u32[]{:S(2)}) %collective-permute-start.7) | collective-permute-done | bytes 286752 | tf_op jit(solution)/shard_map/ppermute | solution.py:23
  36.7 1.9 %collective-permute-done.8.refs_1_ = bf16[160,512]{1,0:T(8,128)(2,1)S(1)} collective-permute-done((bf16[160,512]{1,0:T(8,128)(2,1)S(1)}, bf16[160,512]{1,0:T(8,128)(2,1)S(1)}, u32[]{:S(2)}, u32[]{:S(2)}) %collective-permute-start.8) | collective-permute-done | bytes 163872 | tf_op jit(solution)/shard_map/ppermute | solution.py:23
  38.6 0.8 %shard_map.110 = bf16[160,1792]{1,0:T(8,128)(2,1)S(1)} custom-call(bf16[160,512]{1,0:T(8,128)(2,1)S(1)} %shard_map.107.refs_0_, bf16[160,512]{1,0:T(8,128)(2,1)S(1)} %collective-permute-done.8.refs_1_, bf16[1024,1792]{1,0:T(8,128)(2,1)S(1)} %get-tuple-element.29.refs_2_, bf16[40,3584]{1,0:T(8,128)(2,1)S(1)} %collective-permute-done.7.refs_3_), custom_call_target="tpu_custom_call" | custom-call | tf_op jit(solution)/shard_map/pallas_call | solution.py:266
  39.4 0.4 collective-permute-start.10
  39.8 4.1 %collective-permute-done.6 = bf16[40,3584]{1,0:T(8,128)(2,1)S(1)} collective-permute-done((bf16[40,3584]{1,0:T(8,128)(2,1)S(1)}, bf16[40,3584]{1,0:T(8,128)(2,1)S(1)}, u32[]{:S(2)}, u32[]{:S(2)}) %collective-permute-start.6) | collective-permute-done | bytes 286752 | tf_op jit(solution)/shard_map/ppermute | solution.py:23
  43.9 0.1 pad_maximum_fusion.1.rows_ref
  44.0 1.4 %shard_map.111 = (f32[160,1024]{1,0:T(8,128)S(1)}, bf16[160,1024]{1,0:T(8,128)(2,1)S(1)}) custom-call(bf16[160,3584]{1,0:T(8,128)(2,1)S(1)} %pad_maximum_fusion.1.rows_ref, bf16[3584,512]{1,0:T(8,128)(2,1)S(1)} %get-tuple-element.21.refs_5_.refs_0_, bf16[3584,512]{1,0:T(8,128)(2,1)S(1)} %get-tuple-element.25.refs_1_, bf16[2,2,40,1792]{3,2,1,0:T(8,128)(2,1)S(1)} %bitcast.33), custom_call_target="tpu_custom_call" | custom-call | tf_op jit(solution)/shard_map/pallas_call | solution.py:245
  45.3 2.3 %all-gather.2 = bf16[320,1024]{1,0:T(8,128)(2,1)S(1)} all-gather(bf16[160,1024]{1,0:T(8,128)(2,1)S(1)} %get-tuple-element.31), channel_id=4, replica_groups=mesh['rep'=2,'ep'=4,'node'=2,'sub'=2] {'sub'}, dimensions={0}, use_global_device_ids=true | all-gather | bytes 983040 | tf_op jit(solution)/shard_map/all_gather | solution.py:377
  47.6 0.1 shard_map.112.refs_0_
  47.8 1.6 %collective-permute-start.9 = (bf16[160,512]{1,0:T(8,128)(2,1)S(1)}, bf16[160,512]{1,0:T(8,128)(2,1)S(1)}, u32[]{:S(2)}, u32[]{:S(2)}) collective-permute-start(bf16[160,512]{1,0:T(8,128)(2,1)S(1)} %pad_maximum_fusion.4), channel_id=1, source_target_pairs={{0,2},{2,0},{1,3},{3,1},{4,6},{6,4},{5,7},{7,5},{8,10},{10,8},{9,1... | collective-permute-start | bytes 491528 | tf_op jit(solution)/shard_map/ppermute | solution.py:23
  49.3 4.4 %collective-permute-done.10.refs_3_ = bf16[2,40,1792]{2,1,0:T(8,128)(2,1)S(1)} collective-permute-done((bf16[2,40,1792]{2,1,0:T(8,128)(2,1)S(1)}, bf16[2,40,1792]{2,1,0:T(8,128)(2,1)S(1)}, u32[]{:S(2)}, u32[]{:S(2)}) %collective-permute-start.10) | collective-permute-done | bytes 286752 | tf_op jit(solution)/shard_map/ppermute | solution.py:23
  53.8 0.3 collective-permute-done.9.refs_1_
  54.1 0.8 %shard_map.113 = bf16[160,1792]{1,0:T(8,128)(2,1)S(1)} custom-call(bf16[160,512]{1,0:T(8,128)(2,1)S(1)} %shard_map.112.refs_0_, bf16[160,512]{1,0:T(8,128)(2,1)S(1)} %collective-permute-done.9.refs_1_, bf16[1024,1792]{1,0:T(8,128)(2,1)S(1)} %get-tuple-element.29.refs_2_, bf16[2,40,1792]{2,1,0:T(8,128)(2,1)S(1)} %collective-permute-done.10.refs_3_), custom_call_target="tpu_custom_call" | custom-call | tf_op jit(solution)/shard_map/pallas_call | solution.py:266
  54.9 1.6 %collective-permute-start.15 = (bf16[2,40,1792]{2,1,0:T(8,128)(2,1)S(1)}, bf16[2,40,1792]{2,1,0:T(8,128)(2,1)S(1)}, u32[]{:S(2)}, u32[]{:S(2)}) collective-permute-start(bf16[2,40,1792]{2,1,0:T(8,128)(2,1)S(1)} %shard_map.115), channel_id=1, source_target_pairs={{0,2},{2,0},{1,3},{3,1},{4,6},{6,4},{5,7},{7,5},{8,10},{10,8},{9,1... | collective-permute-start | bytes 860168 | tf_op jit(solution)/shard_map/ppermute | solution.py:23
  56.5 3.5 %collective-permute-start.11 = (bf16[40,1792]{1,0:T(8,128)(2,1)S(1)}, bf16[40,1792]{1,0:T(8,128)(2,1)S(1)}, u32[]{:S(2)}, u32[]{:S(2)}) collective-permute-start(bf16[40,1792]{1,0:T(8,128)(2,1)S(1)} %get-tuple-element.40), channel_id=1, source_target_pairs={{0,12},{4,8},{8,4},{12,0},{1,13},{5,9},{9,5},{13,1},{2,14},{6,10},... | collective-permute-start | bytes 430088 | tf_op jit(solution)/shard_map/ppermute | solution.py:23
  59.9 0.4 collective-permute-start.12
  60.3 0.0 collective-permute-start.13
  60.3 2.9 %collective-permute-start.14 = (bf16[40,1792]{1,0:T(8,128)(2,1)S(1)}, bf16[40,1792]{1,0:T(8,128)(2,1)S(1)}, u32[]{:S(2)}, u32[]{:S(2)}) collective-permute-start(bf16[40,1792]{1,0:T(8,128)(2,1)S(1)} %get-tuple-element.37), channel_id=1, source_target_pairs={{0,6},{2,4},{4,2},{6,0},{8,14},{10,12},{12,10},{14,8},{1,7},{3,5},... | collective-permute-start | bytes 430088 | tf_op jit(solution)/shard_map/ppermute | solution.py:39
  63.3 0.9 %collective-permute-done.11.refs_0_ = bf16[40,1792]{1,0:T(8,128)(2,1)S(1)} collective-permute-done((bf16[40,1792]{1,0:T(8,128)(2,1)S(1)}, bf16[40,1792]{1,0:T(8,128)(2,1)S(1)}, u32[]{:S(2)}, u32[]{:S(2)}) %collective-permute-start.11) | collective-permute-done | bytes 143392 | tf_op jit(solution)/shard_map/ppermute | solution.py:23
  64.2 5.1 %collective-permute-done.12.refs_3_ = bf16[40,1792]{1,0:T(8,128)(2,1)S(1)} collective-permute-done((bf16[40,1792]{1,0:T(8,128)(2,1)S(1)}, bf16[40,1792]{1,0:T(8,128)(2,1)S(1)}, u32[]{:S(2)}, u32[]{:S(2)}) %collective-permute-start.12) | collective-permute-done | bytes 143392 | tf_op jit(solution)/shard_map/ppermute | solution.py:39
  69.3 0.7 shard_map.114
  70.0 0.0 collective-permute-done.13.refs_2_
  70.0 2.6 %collective-permute-done.14.refs_3_ = bf16[40,1792]{1,0:T(8,128)(2,1)S(1)} collective-permute-done((bf16[40,1792]{1,0:T(8,128)(2,1)S(1)}, bf16[40,1792]{1,0:T(8,128)(2,1)S(1)}, u32[]{:S(2)}, u32[]{:S(2)}) %collective-permute-start.14) | collective-permute-done | bytes 143392 | tf_op jit(solution)/shard_map/ppermute | solution.py:39
  72.6 0.0 collective-permute-done.15.refs_4_
  72.6 1.4 %shard_map.116 = bf16[64,3584]{1,0:T(8,128)(2,1)} custom-call(bf16[4,64,40]{2,1,0:T(8,128)(2,1)S(1)} %get-tuple-element.32.given_ref, f32[64,1792]{1,0:T(8,128)S(1)} %get-tuple-element.33.refs_0_, f32[64,1792]{1,0:T(8,128)S(1)} %get-tuple-element.34.refs_1_, bf16[40,1792]{1,0:T(8,128)(2,1)S(1)} %collective-permute-done.13.refs_2_, ...), custom_call_target="tpu_custom_call" | custom-call | tf_op jit(solution)/shard_map/pallas_call | solution.py:322
  (15 shorter events, 0.2 us)
Async XLA Ops:
  1.6 17.2 %collective-permute-start = (bf16[40,3584]{1,0:T(8,128)(2,1)S(1)}, bf16[40,3584]{1,0:T(8,128)(2,1)S(1)}, u32[]{:S(2)}, u32[]{:S(2)}) collective-permute-start(bf16[40,3584]{1,0:T(8,128)(2,1)S(1)} %get-tuple-element.23), channel_id=1, source_target_pairs={{0,8},{4,12},{8,0},{12,4},{1,9},{5,13},{9,1},{13,5},{2,10},{6,14},... | collective-permute-start | bytes 860168 | tf_op jit(solution)/shard_map/ppermute | solution.py:23
  5.7 18.0 %collective-permute-start.1 = (bf16[40,3584]{1,0:T(8,128)(2,1)S(1)}, bf16[40,3584]{1,0:T(8,128)(2,1)S(1)}, u32[]{:S(2)}, u32[]{:S(2)}) collective-permute-start(bf16[40,3584]{1,0:T(8,128)(2,1)S(1)} %get-tuple-element.24), channel_id=1, source_target_pairs={{0,4},{4,0},{8,12},{12,8},{1,5},{5,1},{9,13},{13,9},{2,6},{6,2},{1... | collective-permute-start | bytes 860168 | tf_op jit(solution)/shard_map/ppermute | solution.py:23
  7.3 16.4 %collective-permute-start.2 = (bf16[40,3584]{1,0:T(8,128)(2,1)S(1)}, bf16[40,3584]{1,0:T(8,128)(2,1)S(1)}, u32[]{:S(2)}, u32[]{:S(2)}) collective-permute-start(bf16[40,3584]{1,0:T(8,128)(2,1)S(1)} %get-tuple-element.24), channel_id=1, source_target_pairs={{0,2},{2,0},{1,3},{3,1},{4,6},{6,4},{5,7},{7,5},{8,10},{10,8},{9,1... | collective-permute-start | bytes 860168 | tf_op jit(solution)/shard_map/ppermute | solution.py:23
  8.8 16.0 %collective-permute-start.3 = (bf16[40,3584]{1,0:T(8,128)(2,1)S(1)}, bf16[40,3584]{1,0:T(8,128)(2,1)S(1)}, u32[]{:S(2)}, u32[]{:S(2)}) collective-permute-start(bf16[40,3584]{1,0:T(8,128)(2,1)S(1)} %get-tuple-element.20.refs_3_), channel_id=1, source_target_pairs={{0,2},{2,0},{1,3},{3,1},{4,6},{6,4},{5,7},{7,5},{8,10},{10,8},{9,1... | collective-permute-start | bytes 860168 | tf_op jit(solution)/shard_map/ppermute | solution.py:23
  18.8 8.8 %collective-permute-start.4 = (bf16[40,3584]{1,0:T(8,128)(2,1)S(1)}, bf16[40,3584]{1,0:T(8,128)(2,1)S(1)}, u32[]{:S(2)}, u32[]{:S(2)}) collective-permute-start(bf16[40,3584]{1,0:T(8,128)(2,1)S(1)} %shard_map.103.refs_0_), channel_id=1, source_target_pairs={{0,2},{2,0},{1,3},{3,1},{4,6},{6,4},{5,7},{7,5},{8,10},{10,8},{9,1... | collective-permute-start | bytes 860168 | tf_op jit(solution)/shard_map/ppermute | solution.py:23
  20.3 12.7 %collective-permute-start.5 = (bf16[40,3584]{1,0:T(8,128)(2,1)S(1)}, bf16[40,3584]{1,0:T(8,128)(2,1)S(1)}, u32[]{:S(2)}, u32[]{:S(2)}) collective-permute-start(bf16[40,3584]{1,0:T(8,128)(2,1)S(1)} %shard_map.108), channel_id=1, source_target_pairs={{0,12},{4,8},{8,4},{12,0},{1,13},{5,9},{9,5},{13,1},{2,14},{6,10},... | collective-permute-start | bytes 860168 | tf_op jit(solution)/shard_map/ppermute | solution.py:23
  23.7 13.0 %collective-permute-start.7 = (bf16[40,3584]{1,0:T(8,128)(2,1)S(1)}, bf16[40,3584]{1,0:T(8,128)(2,1)S(1)}, u32[]{:S(2)}, u32[]{:S(2)}) collective-permute-start(bf16[40,3584]{1,0:T(8,128)(2,1)S(1)} %shard_map.104.refs_0_), channel_id=1, source_target_pairs={{0,4},{4,0},{8,12},{12,8},{1,5},{5,1},{9,13},{13,9},{2,6},{6,2},{1... | collective-permute-start | bytes 860168 | tf_op jit(solution)/shard_map/ppermute | solution.py:23
  31.4 7.1 %collective-permute-start.8 = (bf16[160,512]{1,0:T(8,128)(2,1)S(1)}, bf16[160,512]{1,0:T(8,128)(2,1)S(1)}, u32[]{:S(2)}, u32[]{:S(2)}) collective-permute-start(bf16[160,512]{1,0:T(8,128)(2,1)S(1)} %pad_maximum_fusion.3), channel_id=1, source_target_pairs={{0,2},{2,0},{1,3},{3,1},{4,6},{6,4},{5,7},{7,5},{8,10},{10,8},{9,1... | collective-permute-start | bytes 491528 | tf_op jit(solution)/shard_map/ppermute | solution.py:23
  33.0 10.9 %collective-permute-start.6 = (bf16[40,3584]{1,0:T(8,128)(2,1)S(1)}, bf16[40,3584]{1,0:T(8,128)(2,1)S(1)}, u32[]{:S(2)}, u32[]{:S(2)}) collective-permute-start(bf16[40,3584]{1,0:T(8,128)(2,1)S(1)} %shard_map.109), channel_id=1, source_target_pairs={{0,2},{2,0},{1,3},{3,1},{4,6},{6,4},{5,7},{7,5},{8,10},{10,8},{9,1... | collective-permute-start | bytes 860168 | tf_op jit(solution)/shard_map/ppermute | solution.py:23
  39.4 14.4 %collective-permute-start.10 = (bf16[2,40,1792]{2,1,0:T(8,128)(2,1)S(1)}, bf16[2,40,1792]{2,1,0:T(8,128)(2,1)S(1)}, u32[]{:S(2)}, u32[]{:S(2)}) collective-permute-start(bf16[2,40,1792]{2,1,0:T(8,128)(2,1)S(1)} %slice_bitcast_fusion), channel_id=1, source_target_pairs={{0,8},{4,12},{8,0},{12,4},{1,9},{5,13},{9,1},{13,5},{2,10},{6,14},... | collective-permute-start | bytes 860168 | tf_op jit(solution)/shard_map/ppermute | solution.py:23
  47.8 6.3 %collective-permute-start.9 = (bf16[160,512]{1,0:T(8,128)(2,1)S(1)}, bf16[160,512]{1,0:T(8,128)(2,1)S(1)}, u32[]{:S(2)}, u32[]{:S(2)}) collective-permute-start(bf16[160,512]{1,0:T(8,128)(2,1)S(1)} %pad_maximum_fusion.4), channel_id=1, source_target_pairs={{0,2},{2,0},{1,3},{3,1},{4,6},{6,4},{5,7},{7,5},{8,10},{10,8},{9,1... | collective-permute-start | bytes 491528 | tf_op jit(solution)/shard_map/ppermute | solution.py:23
  54.9 17.8 %collective-permute-start.15 = (bf16[2,40,1792]{2,1,0:T(8,128)(2,1)S(1)}, bf16[2,40,1792]{2,1,0:T(8,128)(2,1)S(1)}, u32[]{:S(2)}, u32[]{:S(2)}) collective-permute-start(bf16[2,40,1792]{2,1,0:T(8,128)(2,1)S(1)} %shard_map.115), channel_id=1, source_target_pairs={{0,2},{2,0},{1,3},{3,1},{4,6},{6,4},{5,7},{7,5},{8,10},{10,8},{9,1... | collective-permute-start | bytes 860168 | tf_op jit(solution)/shard_map/ppermute | solution.py:23
  56.5 7.7 %collective-permute-start.11 = (bf16[40,1792]{1,0:T(8,128)(2,1)S(1)}, bf16[40,1792]{1,0:T(8,128)(2,1)S(1)}, u32[]{:S(2)}, u32[]{:S(2)}) collective-permute-start(bf16[40,1792]{1,0:T(8,128)(2,1)S(1)} %get-tuple-element.40), channel_id=1, source_target_pairs={{0,12},{4,8},{8,4},{12,0},{1,13},{5,9},{9,5},{13,1},{2,14},{6,10},... | collective-permute-start | bytes 430088 | tf_op jit(solution)/shard_map/ppermute | solution.py:23
  59.9 9.4 %collective-permute-start.12 = (bf16[40,1792]{1,0:T(8,128)(2,1)S(1)}, bf16[40,1792]{1,0:T(8,128)(2,1)S(1)}, u32[]{:S(2)}, u32[]{:S(2)}) collective-permute-start(bf16[40,1792]{1,0:T(8,128)(2,1)S(1)} %get-tuple-element.39), channel_id=1, source_target_pairs={{0,14},{2,12},{4,10},{6,8},{8,6},{10,4},{12,2},{14,0},{1,15},{3,13... | collective-permute-start | bytes 430088 | tf_op jit(solution)/shard_map/ppermute | solution.py:39
  60.3 9.7 %collective-permute-start.13 = (bf16[40,1792]{1,0:T(8,128)(2,1)S(1)}, bf16[40,1792]{1,0:T(8,128)(2,1)S(1)}, u32[]{:S(2)}, u32[]{:S(2)}) collective-permute-start(bf16[40,1792]{1,0:T(8,128)(2,1)S(1)} %get-tuple-element.38), channel_id=1, source_target_pairs={{0,4},{4,0},{8,12},{12,8},{1,5},{5,1},{9,13},{13,9},{2,6},{6,2},{1... | collective-permute-start | bytes 430088 | tf_op jit(solution)/shard_map/ppermute | solution.py:23
  60.3 12.3 %collective-permute-start.14 = (bf16[40,1792]{1,0:T(8,128)(2,1)S(1)}, bf16[40,1792]{1,0:T(8,128)(2,1)S(1)}, u32[]{:S(2)}, u32[]{:S(2)}) collective-permute-start(bf16[40,1792]{1,0:T(8,128)(2,1)S(1)} %get-tuple-element.37), channel_id=1, source_target_pairs={{0,6},{2,4},{4,2},{6,0},{8,14},{10,12},{12,10},{14,8},{1,7},{3,5},... | collective-permute-start | bytes 430088 | tf_op jit(solution)/shard_map/ppermute | solution.py:39

commit v4 on v3

--- a/solution.py
+++ b/solution.py
@@ -66,14 +66,17 @@
     return pltpu.with_memory_space_constraint(value, pltpu.HBM)
 
 
-def pack_rows(expert_place, routes_t, tokens, order, cap):
+def pack_rows(expert_place, routes_t, tokens, order, halved, cap):
     experts = expert_place.shape[0]
     topk, tok_rows = routes_t.shape
     width = tokens.shape[1]
 
+    whole, half = [slice(0, width)], [slice(0, width // 2), slice(width // 2, width)]
+    spans = {k: half if k in halved else whole for k in order}
+
     def kernel(where_hbm, routes_hbm, tokens_hbm, *refs):
         place_ref, *refs = refs
-        block_refs, (where_ref, routes_ref, tokens_ref, sems) = refs[: len(order)], refs[len(order) :]
+        block_refs, (where_ref, routes_ref, tokens_ref, sems) = list(refs[:-4]), refs[-4:]
         pairs = [(where_hbm, where_ref), (routes_hbm, routes_ref), (tokens_hbm, tokens_ref)]
         copies = [pltpu.make_async_copy(a, b, sems.at[i]) for i, (a, b) in enumerate(pairs)]
         for copy in copies:
@@ -101,14 +104,17 @@
         place_ref[...] = place
         row = lax.broadcasted_iota(jnp.int32, (cap, tok_rows), 0).astype(f32)
         copies[2].wait()
-        for block_ref, k in zip(block_refs, order):
+        for k in order:
             placing = jnp.where(place[k : k + 1] == row, f32(1.0), f32(0.0)).astype(bf16)
-            block_ref[...] = jnp.dot(
-                placing, tokens_ref[...], preferred_element_type=f32
-            ).astype(bf16)
+            for at in spans[k]:
+                block_refs.pop(0)[...] = jnp.dot(
+                    placing, tokens_ref[:, at], preferred_element_type=f32
+                ).astype(bf16)
 
     shapes = [jax.ShapeDtypeStruct((experts, tok_rows), f32)]
-    shapes += [jax.ShapeDtypeStruct((cap, width), bf16)] * len(order)
+    shapes += [
+        jax.ShapeDtypeStruct((cap, at.stop - at.start), bf16) for k in order for at in spans[k]
+    ]
     scratch = [
         pltpu.VMEM((1, experts), jnp.int32),
         pltpu.VMEM((topk, tok_rows), jnp.int32),
@@ -125,7 +131,7 @@
     shapes = [jax.ShapeDtypeStruct(a.shape, a.dtype) for a in held]
     aliases = {count + i: i for i in range(len(held))}
     specs = [ANY] * (count + len(held))
-    return call(lambda *refs: None, shapes, specs, aliases=aliases)(*behind, *held)
+    return list(call(lambda *refs: None, shapes, specs, aliases=aliases)(*behind, *held))
 
 
 def load(arrays, behind):
@@ -255,9 +261,8 @@
         total = None
         for i in range(nodes):
             node = node_me ^ i
-            hidden = hidden_refs[i][...] if by_node[i].ndim == 2 else hidden_refs[i][node]
             at = pl.ds(pl.multiple_of(node * part, part), part)
-            value = jnp.dot(hidden, weight_ref[at, :], preferred_element_type=f32)
+            value = jnp.dot(hidden_refs[i][...], weight_ref[at, :], preferred_element_type=f32)
             total = value if total is None else total + value
         out_ref[...] = total.astype(bf16)
 
@@ -275,7 +280,7 @@
 def combine_early(info, pieces, cap):
     _, tok_rows, count = info.shape
     flat = [rows for part in pieces for _, rows in part]
-    width = flat[0].shape[1]
+    width = flat[0].shape[-1]
 
     def kernel(info_ref, *refs):
         given_ref, *sum_refs = refs[len(flat) :]
@@ -288,7 +293,10 @@
             low[k] = (factor - factor.astype(bf16).astype(f32)).astype(bf16)
         rest = list(refs[: len(flat)])
         for part, out in zip(pieces, sum_refs):
-            mine = [(k, rest.pop(0)[...]) for k, _ in part]
+            mine = []
+            for ks, rows in part:
+                ref = rest.pop(0)
+                mine += [(k, ref[i] if rows.ndim == 3 else ref[...]) for i, k in enumerate(ks)]
             out[...] = weighted_sum(given_ref, mine) + weighted_sum(low, mine)
 
     shapes = [jax.ShapeDtypeStruct((count, tok_rows, cap), bf16)]
@@ -297,19 +305,16 @@
     return given, sums
 
 
-def combine_late(given, sums, pieces, order, across):
+def combine_late(given, sums, pieces):
     nodes = len(sums)
     tok_rows, width = sums[0].shape
     flat = [rows for part in pieces for _, rows in part]
 
     def kernel(given_ref, *refs):
-        sum_refs, rest, across_refs = refs[:nodes], list(refs[nodes:-nodes]), refs[-nodes:-1]
-        out_ref = refs[-1]
+        sum_refs, rest, out_ref = refs[:nodes], list(refs[nodes:-1]), refs[-1]
         node_me = lax.axis_index("node")
         for j in range(nodes):
             mine = [(k, rest.pop(0)[...]) for k, _ in pieces[j]]
-            if j:
-                mine += [(k, across_refs[j - 1][i]) for i, k in enumerate(order)]
             value = (sum_refs[j][...] + weighted_sum(given_ref, mine)).astype(bf16)
             for at in range(nodes):
 
@@ -318,8 +323,7 @@
                     out_ref[:, at * width : (at + 1) * width] = value
 
     shapes = [jax.ShapeDtypeStruct((tok_rows, nodes * width), bf16)]
-    specs = [WHOLE] * (1 + nodes + len(flat) + len(across))
-    return call(kernel, shapes, specs)(given, *sums, *flat, *across)[0]
+    return call(kernel, shapes, [WHOLE] * (1 + nodes + len(flat)))(given, *sums, *flat)[0]
 
 
 def body(
@@ -348,67 +352,74 @@
     others = range(1, nodes)
     routes_t = routes.T
     order = [*middle, 0, *near, *far]
-    place, *packed = pack_rows(expert_place, routes_t, tokens, order, cap)
-    outgoing = dict(zip(order, packed))
+    place, *packed = pack_rows(expert_place, routes_t, tokens, order, middle, cap)
+    outgoing = {k: [packed.pop(0) for _ in range(2 if k in middle else 1)] for k in order}
 
     blocks = [[outgoing[k]] + [None] * (nodes - 1) for k in range(eps)]
     for k in [*middle, *near]:
-        blocks[k][0] = swap(outgoing[k], "ep", k)
+        blocks[k][0] = [swap(part, "ep", k) for part in outgoing[k]]
     for k in [0, *near]:
-        blocks[k][1:] = [swap(outgoing[k], "node", j) for j in others]
+        blocks[k][1:] = [[swap(outgoing[k][0], "node", j)] for j in others]
     gate_w, up_w, down_w = load(
-        [gate_weight[0], up_weight[0], down_weight[0, 0]], [outgoing[0]]
-    )
-    logits = partial_logits(tokens, tenant, router_weight, adapter_down, adapter_up, [gate_w])
+        [gate_weight[0], up_weight[0], down_weight[0, 0]], [outgoing[0][0]]
+    )
+    firsts = hold([blocks[k][0][0] for k in middle], [gate_w])
+    logits = partial_logits(tokens, tenant, router_weight, adapter_down, adapter_up, firsts[:1])
     logits = lax.all_gather(logits, "sub")
-    for k, rows in zip(far, hold([outgoing[k] for k in far], [logits])):
-        blocks[k][0] = swap(rows, "ep", k)
-    for k, rows in zip(middle, hold([blocks[k][0] for k in middle], [logits])):
-        blocks[k] = [rows] + [swap(rows, "node", j) for j in others]
-    crossed = [blocks[k][j] for k in near for j in others]
-    crossed = hold(crossed, [blocks[k][0] for k in (middle[-1], *near)])
-    for i, k in enumerate(near):
+    for k, part in zip(middle, firsts):
+        blocks[k][0][0] = part
+        blocks[k][1:] = [[swap(part, "node", j)] for j in others]
+    seconds = hold(
+        [blocks[k][0][1] for k in middle], [logits] + [blocks[0][j][0] for j in others]
+    )
+    for k, part in zip(middle, seconds):
+        blocks[k][0][1] = part
         for j in others:
-            blocks[k][j] = swap(crossed[i * len(others) + j - 1], "ep", k)
+            blocks[k][j].append(swap(part, "node", j))
+    for k, rows in zip(far, hold([outgoing[k][0] for k in far], [logits])):
+        blocks[k][0] = [swap(rows, "ep", k)]
+    crossed = [blocks[k][j][0] for k in near for j in others]
+    crossed = hold(crossed, seconds[:1] + [blocks[k][0][0] for k in near])
+    anchor = crossed[:1]
+    for k in near:
+        blocks[k][1:] = [[swap(crossed.pop(0), "ep", k)] for j in others]
 
     def gate_up(chunk, behind):
-        rows = [blocks[k][j] for j in range(nodes) for k in chunk]
+        rows = [jnp.concatenate(blocks[k][j], axis=1) for j in range(nodes) for k in chunk]
         own, sent = dots(jnp.concatenate(rows, axis=0), [gate_w, up_w], [f32, bf16], behind)
         return activate(own, lax.all_gather(sent, "sub"))
 
-    def down(chunk, hidden, gather=False, behind=()):
+    def down(chunk, hidden, behind=()):
         size = len(chunk) * cap
         by_node = [hidden]
         for i in others:
-            sent = regroup(hidden, i, size)
-            if gather:
-                by_node.append(lax.all_gather(sent, "node"))
-            else:
-                by_node.append(swap(sent, "node", i))
+            by_node.append(swap(regroup(hidden, i, size), "node", i))
         out = project(by_node, down_w, behind)
         return out.reshape(nodes, len(chunk), cap, out_width)
 
-    info = route_info(logits, place, expert_place, routes_t, crossed[:1])
+    info = route_info(logits, place, expert_place, routes_t, anchor)
 
     early_chunk, late_chunk = [0, *middle], [*far, *near]
     hidden = gate_up(early_chunk, [info])
-    for k, rows in zip(far, hold([blocks[k][0] for k in far], [hidden])):
-        blocks[k] = [rows] + [swap(rows, "node", j) for j in others]
-    early_out = down(early_chunk, hidden, behind=[blocks[k][j] for k in near for j in others])
+    for k, rows in zip(far, hold([blocks[k][0][0] for k in far], [hidden])):
+        blocks[k] = [[rows]] + [[swap(rows, "node", j)] for j in others]
+    early_out = down(early_chunk, hidden)
     hidden = gate_up(late_chunk, [early_out])
     back = [early_out[:, 0]]
     back += [swap(early_out[:, i], "ep", k) for i, k in enumerate(early_chunk) if k]
-    late_out = down(late_chunk, hidden, False, back[1:])
+    late_out = down(late_chunk, hidden, back[1:])
     late = [
         [(k, send(late_out[j, i], k, j)) for i, k in enumerate(late_chunk)] for j in range(nodes)
     ]
-    across = hold([jnp.stack([part[j] for part in back]) for j in others], [late_out])
+    across = [jnp.stack([part[j] for part in back]) for j in others]
     across = [swap(rows, "node", j) for j, rows in zip(others, across)]
     count = len(far)
-    pieces = [part[:count] for part in late]
-    pieces[0] = pieces[0] + [(k, part[0]) for k, part in zip(early_chunk, back)]
+    pieces = [[([k], rows) for k, rows in part[:count]] for part in late]
+    pieces[0] += [([k], part[0]) for k, part in zip(early_chunk, back)]
+    for part, rows in zip(pieces[1:], across):
+        part.append((early_chunk, rows))
     given, sums = combine_early(info, pieces, cap)
-    return combine_late(given, sums, [part[count:] for part in late], early_chunk, across)
+    return combine_late(given, sums, [part[count:] for part in late])
 
 
 def solution(mesh):

time: 74.2 us -> 71.3 us (0.961)
  waiting for transfers between devices: 26.8 us -> 20.2 us
  starting transfers between devices: 25.1 us -> 28.7 us
    ppermute x14 -> x16, waiting for transfers between devices: 19 us -> 13.6 us  [swap(): lax.ppermute(value, axis, [(i, partner(i, step)) for i in range(count)])]
    ppermute x14 -> x16, starting transfers between devices: 21.7 us -> 25 us  [swap(): lax.ppermute(value, axis, [(i, partner(i, step)) for i in range(count)])]
    ppermute x2, waiting for transfers between devices: 7.73 us -> 6.61 us  [send(): return lax.ppermute(value, ('ep', 'node'), pairs)]
  transfers between devices with their start and end apart: 16 -> 18, of which waited for: 10 -> 10; matrix products, arithmetic and copies ran while one was open for 0% -> 0% of each run, Pallas kernels for 16% -> 18%
where the time goes in v4:
time: 71.3 us; the launch traced here: 71.1 us
  starting transfers between devices  28.7 us (40%)
  waiting for transfers between devices  20.2 us (28%)
  Pallas kernels  15.4 us (22%)
  blocking collectives  6.33 us (9%)
    ppermute x16, starting transfers between devices, swap(): lax.ppermute(value, axis, [(i, partner(i, step)) for i in range(count)])  25 us
    ppermute x16, waiting for transfers between devices, swap(): lax.ppermute(value, axis, [(i, partner(i, step)) for i in range(count)])  13.6 us
    ppermute x2, waiting for transfers between devices, send(): return lax.ppermute(value, ('ep', 'node'), pairs)  6.61 us
    all_gather x2, blocking collectives, gate_up(): return activate(own, lax.all_gather(sent, 'sub'))  4.55 us
    pallas_call x1, Pallas kernels, load(): call(kernel, shapes, specs, [pltpu.SemaphoreType.DMA((count,))])  4.23 us
    ppermute x2, starting transfers between devices, send(): return lax.ppermute(value, ('ep', 'node'), pairs)  3.68 us
    pallas_call x2, Pallas kernels, dots(): return call(kernel, shapes, specs)(rows, *weights, *behind)  2.71 us
    pallas_call x1, Pallas kernels, partial_logits(): call(kernel, shapes, specs, scratch)(*[in_hbm(a) for a in given], *behind)  1.92 us
  transfers between devices with their start and end apart: 18, of which 10 were waited for; matrix products, arithmetic and copies ran while one was open for 0% of the time, Pallas kernels for 18%

profile of v4, /device:TPU:0, one launch (start us, length us, event | category | flops | bytes accessed | tf_op | source)
XLA Modules:
  0.0 71.1 jit_solution(10893483061132372365)
XLA Ops:
  0.0 1.6 %shard_map.100 = (f32[4,64]{1,0:T(4,128)S(1)}, bf16[40,1792]{1,0:T(8,128)(2,1)S(1)}, bf16[40,1792]{1,0:T(8,128)(2,1)S(1)}, bf16[40,3584]{1,0:T(8,128)(2,1)S(1)},...) custom-call(s32[1,4]{1,0:T(1,128)} %bitcast.44, s32[2,64]{1,0:T(2,128)} %bitcast.42, bf16[64,3584]{1,0:T(8,128)(2,1)} %refs_0_.1), custom_call_target="tpu_custom_call" | custom-call | tf_op jit(solution)/shard_map/pallas_call | solution.py:124
  1.6 3.0 %collective-permute-start.1 = (bf16[40,3584]{1,0:T(8,128)(2,1)S(1)}, bf16[40,3584]{1,0:T(8,128)(2,1)S(1)}, u32[]{:S(2)}, u32[]{:S(2)}) collective-permute-start(bf16[40,3584]{1,0:T(8,128)(2,1)S(1)} %get-tuple-element.21.refs_3_), channel_id=1, source_target_pairs={{0,2},{2,0},{1,3},{3,1},{4,6},{6,4},{5,7},{7,5},{8,10},{10,8},{9,1... | collective-permute-start | bytes 860168 | tf_op jit(solution)/shard_map/ppermute | solution.py:23
  4.6 2.6 %collective-permute-start = (bf16[40,1792]{1,0:T(8,128)(2,1)S(1)}, bf16[40,1792]{1,0:T(8,128)(2,1)S(1)}, u32[]{:S(2)}, u32[]{:S(2)}) collective-permute-start(bf16[40,1792]{1,0:T(8,128)(2,1)S(1)} %get-tuple-element.23), channel_id=1, source_target_pairs={{0,8},{4,12},{8,0},{12,4},{1,9},{5,13},{9,1},{13,5},{2,10},{6,14},... | collective-permute-start | bytes 430088 | tf_op jit(solution)/shard_map/ppermute | solution.py:23
  7.2 1.6 %collective-permute-start.3 = (bf16[40,3584]{1,0:T(8,128)(2,1)S(1)}, bf16[40,3584]{1,0:T(8,128)(2,1)S(1)}, u32[]{:S(2)}, u32[]{:S(2)}) collective-permute-start(bf16[40,3584]{1,0:T(8,128)(2,1)S(1)} %get-tuple-element.26), channel_id=1, source_target_pairs={{0,4},{4,0},{8,12},{12,8},{1,5},{5,1},{9,13},{13,9},{2,6},{6,2},{1... | collective-permute-start | bytes 860168 | tf_op jit(solution)/shard_map/ppermute | solution.py:23
  8.8 0.5 collective-permute-start.4
  9.3 0.3 collective-permute-start.2
  9.6 4.2 %shard_map.101 = (bf16[3584,512]{1,0:T(8,128)(2,1)S(1)}, bf16[3584,512]{1,0:T(8,128)(2,1)S(1)}, bf16[1024,1792]{1,0:T(8,128)(2,1)S(1)}) custom-call(bf16[3584,512]{1,0:T(8,128)(2,1)} %bitcast.38, bf16[3584,512]{1,0:T(8,128)(2,1)} %bitcast.39, bf16[1024,1792]{1,0:T(8,128)(2,1)} %bitcast.40, bf16[40,3584]{1,0:T(8,128)(2,1)S(1)} %get-tuple-element.21.refs_3_), custom_call_target="tpu_custom_call" | custom-call | tf_op jit(solution)/shard_map/pallas_call | solution.py:145
  13.9 1.2 %collective-permute-done.refs_1_ = bf16[40,1792]{1,0:T(8,128)(2,1)S(1)} collective-permute-done((bf16[40,1792]{1,0:T(8,128)(2,1)S(1)}, bf16[40,1792]{1,0:T(8,128)(2,1)S(1)}, u32[]{:S(2)}, u32[]{:S(2)}) %collective-permute-start) | collective-permute-done | bytes 143392 | tf_op jit(solution)/shard_map/ppermute | solution.py:23
  15.0 0.4 collective-permute-start.5
  15.4 1.9 %shard_map.103 = f32[4,64]{1,0:T(4,128)S(1)} custom-call(bf16[64,3584]{1,0:T(8,128)(2,1)} %refs_0_.1, bf16[3584,128]{1,0:T(8,128)(2,1)} %refs_1_.1, bf16[4,3584]{1,0:T(4,128)(2,1)} %bitcast.41, bf16[4,128]{1,0:T(4,128)(2,1)} %bitcast.46, s32[1,64]{1,0:T(1,128)} %bitcast.47, bf16[40,1792]{1,0:T(8,128)(2,1)S(1)} %shard_map.102.refs_5_), custom_call_target="tpu_custom_call" | custom-call | tf_op jit(solution)/shard_map/pallas_call | solution.py:194
  17.4 1.8 %all-gather.3.refs_0_.parts_ref = f32[2,4,64]{2,1,0:T(4,128)S(1)} all-gather(f32[1,4,64]{2,1,0:T(4,128)S(1)} %bitcast.37), channel_id=2, replica_groups=mesh['rep'=2,'ep'=4,'node'=2,'sub'=2] {'sub'}, dimensions={0}, use_global_device_ids=true | all-gather | bytes 3072 | tf_op jit(solution)/shard_map/all_gather | solution.py:368
  19.1 0.0 collective-permute-done.2.refs_2_
  19.1 0.0 collective-permute-done.1.refs_1_
  19.2 1.7 %collective-permute-start.6 = (bf16[40,1792]{1,0:T(8,128)(2,1)S(1)}, bf16[40,1792]{1,0:T(8,128)(2,1)S(1)}, u32[]{:S(2)}, u32[]{:S(2)}) collective-permute-start(bf16[40,1792]{1,0:T(8,128)(2,1)S(1)} %shard_map.104.refs_0_), channel_id=1, source_target_pairs={{0,2},{2,0},{1,3},{3,1},{4,6},{6,4},{5,7},{7,5},{8,10},{10,8},{9,1... | collective-permute-start | bytes 430088 | tf_op jit(solution)/shard_map/ppermute | solution.py:23
  20.9 2.4 %collective-permute-start.7 = (bf16[40,3584]{1,0:T(8,128)(2,1)S(1)}, bf16[40,3584]{1,0:T(8,128)(2,1)S(1)}, u32[]{:S(2)}, u32[]{:S(2)}) collective-permute-start(bf16[40,3584]{1,0:T(8,128)(2,1)S(1)} %shard_map.109), channel_id=1, source_target_pairs={{0,12},{4,8},{8,4},{12,0},{1,13},{5,9},{9,5},{13,1},{2,14},{6,10},... | collective-permute-start | bytes 860168 | tf_op jit(solution)/shard_map/ppermute | solution.py:23
  23.3 0.0 collective-permute-done.3.refs_1_
  23.3 1.0 %shard_map.106.refs_2_.info_ref = f32[2,64,4]{2,1,0:T(8,128)S(1)} custom-call(f32[2,4,64]{2,1,0:T(4,128)S(1)} %all-gather.3.refs_0_.parts_ref, f32[4,64]{1,0:T(4,128)S(1)} %get-tuple-element.24.place_ref, s32[1,4]{1,0:T(1,128)} %bitcast.45, s32[2,64]{1,0:T(2,128)} %bitcast.43, bf16[40,3584]{1,0:T(8,128)(2,1)S(1)} %shard_map.105.refs_0_), custom_call_target="tpu_custom_call" | custom-call | tf_op jit(solution)/shard_map/pallas_call | solution.py:223
  24.4 0.7 collective-permute-done.6
  25.0 0.1 maximum_maximum_fusion.rows_ref
  25.1 1.4 %shard_map.107 = (f32[160,1024]{1,0:T(8,128)S(1)}, bf16[160,1024]{1,0:T(8,128)(2,1)S(1)}) custom-call(bf16[160,3584]{1,0:T(8,128)(2,1)S(1)} %maximum_maximum_fusion.rows_ref, bf16[3584,512]{1,0:T(8,128)(2,1)S(1)} %get-tuple-element.22.refs_0_, bf16[3584,512]{1,0:T(8,128)(2,1)S(1)} %get-tuple-element.27.refs_1_, f32[2,64,4]{2,1,0:T(8,128)S(1)} %shard_map.106.refs_2_.info_ref), custom_call_target="tpu_custom_call" | custom-call | tf_op jit(solution)/shard_map/pallas_call | solution.py:251
  26.5 2.3 %all-gather.1 = bf16[320,1024]{1,0:T(8,128)(2,1)S(1)} all-gather(bf16[160,1024]{1,0:T(8,128)(2,1)S(1)} %get-tuple-element.29), channel_id=3, replica_groups=mesh['rep'=2,'ep'=4,'node'=2,'sub'=2] {'sub'}, dimensions={0}, use_global_device_ids=true | all-gather | bytes 983040 | tf_op jit(solution)/shard_map/all_gather | solution.py:390
  28.7 0.1 shard_map.108.refs_0_
  28.9 1.7 %collective-permute-start.10 = (bf16[160,512]{1,0:T(8,128)(2,1)S(1)}, bf16[160,512]{1,0:T(8,128)(2,1)S(1)}, u32[]{:S(2)}, u32[]{:S(2)}) collective-permute-start(bf16[160,512]{1,0:T(8,128)(2,1)S(1)} %pad_maximum_fusion.2), channel_id=1, source_target_pairs={{0,2},{2,0},{1,3},{3,1},{4,6},{6,4},{5,7},{7,5},{8,10},{10,8},{9,1... | collective-permute-start | bytes 491528 | tf_op jit(solution)/shard_map/ppermute | solution.py:23
  30.6 0.5 collective-permute-start.9
  31.1 0.2 collective-permute-done.7.refs_1_
  31.4 1.3 %collective-permute-start.8 = (bf16[40,3584]{1,0:T(8,128)(2,1)S(1)}, bf16[40,3584]{1,0:T(8,128)(2,1)S(1)}, u32[]{:S(2)}, u32[]{:S(2)}) collective-permute-start(bf16[40,3584]{1,0:T(8,128)(2,1)S(1)} %shard_map.110), channel_id=1, source_target_pairs={{0,2},{2,0},{1,3},{3,1},{4,6},{6,4},{5,7},{7,5},{8,10},{10,8},{9,1... | collective-permute-start | bytes 860168 | tf_op jit(solution)/shard_map/ppermute | solution.py:23
  32.6 3.4 %collective-permute-done.10.refs_1_ = bf16[160,512]{1,0:T(8,128)(2,1)S(1)} collective-permute-done((bf16[160,512]{1,0:T(8,128)(2,1)S(1)}, bf16[160,512]{1,0:T(8,128)(2,1)S(1)}, u32[]{:S(2)}, u32[]{:S(2)}) %collective-permute-start.10) | collective-permute-done | bytes 163872 | tf_op jit(solution)/shard_map/ppermute | solution.py:23
  36.0 0.8 %shard_map.111 = bf16[160,1792]{1,0:T(8,128)(2,1)S(1)} custom-call(bf16[160,512]{1,0:T(8,128)(2,1)S(1)} %shard_map.108.refs_0_, bf16[160,512]{1,0:T(8,128)(2,1)S(1)} %collective-permute-done.10.refs_1_, bf16[1024,1792]{1,0:T(8,128)(2,1)S(1)} %get-tuple-element.31.refs_2_), custom_call_target="tpu_custom_call" | custom-call | tf_op jit(solution)/shard_map/pallas_call | solution.py:271
  36.8 2.6 %collective-permute-start.12 = (bf16[2,40,1792]{2,1,0:T(8,128)(2,1)S(1)}, bf16[2,40,1792]{2,1,0:T(8,128)(2,1)S(1)}, u32[]{:S(2)}, u32[]{:S(2)}) collective-permute-start(bf16[2,40,1792]{2,1,0:T(8,128)(2,1)S(1)} %slice_bitcast_fusion), channel_id=1, source_target_pairs={{0,8},{4,12},{8,0},{12,4},{1,9},{5,13},{9,1},{13,5},{2,10},{6,14},... | collective-permute-start | bytes 860168 | tf_op jit(solution)/shard_map/ppermute | solution.py:23
  39.5 1.9 %collective-permute-done.8 = bf16[40,3584]{1,0:T(8,128)(2,1)S(1)} collective-permute-done((bf16[40,3584]{1,0:T(8,128)(2,1)S(1)}, bf16[40,3584]{1,0:T(8,128)(2,1)S(1)}, u32[]{:S(2)}, u32[]{:S(2)}) %collective-permute-start.8) | collective-permute-done | bytes 286752 | tf_op jit(solution)/shard_map/ppermute | solution.py:23
  41.3 0.1 pad_maximum_fusion.rows_ref
  41.4 1.4 %shard_map.112 = (f32[160,1024]{1,0:T(8,128)S(1)}, bf16[160,1024]{1,0:T(8,128)(2,1)S(1)}) custom-call(bf16[160,3584]{1,0:T(8,128)(2,1)S(1)} %pad_maximum_fusion.rows_ref, bf16[3584,512]{1,0:T(8,128)(2,1)S(1)} %get-tuple-element.22.refs_0_, bf16[3584,512]{1,0:T(8,128)(2,1)S(1)} %get-tuple-element.27.refs_1_, bf16[2,2,40,1792]{3,2,1,0:T(8,128)(2,1)S(1)} %bitcast.33), custom_call_target="tpu_custom_call" | custom-call | tf_op jit(solution)/shard_map/pallas_call | solution.py:251
  42.8 2.3 %all-gather.2 = bf16[320,1024]{1,0:T(8,128)(2,1)S(1)} all-gather(bf16[160,1024]{1,0:T(8,128)(2,1)S(1)} %get-tuple-element.33), channel_id=4, replica_groups=mesh['rep'=2,'ep'=4,'node'=2,'sub'=2] {'sub'}, dimensions={0}, use_global_device_ids=true | all-gather | bytes 983040 | tf_op jit(solution)/shard_map/all_gather | solution.py:390
  45.1 0.1 shard_map.113.refs_0_
  45.2 1.7 %collective-permute-start.11 = (bf16[160,512]{1,0:T(8,128)(2,1)S(1)}, bf16[160,512]{1,0:T(8,128)(2,1)S(1)}, u32[]{:S(2)}, u32[]{:S(2)}) collective-permute-start(bf16[160,512]{1,0:T(8,128)(2,1)S(1)} %pad_maximum_fusion.3), channel_id=1, source_target_pairs={{0,2},{2,0},{1,3},{3,1},{4,6},{6,4},{5,7},{7,5},{8,10},{10,8},{9,1... | collective-permute-start | bytes 491528 | tf_op jit(solution)/shard_map/ppermute | solution.py:23
  46.9 4.5 %collective-permute-done.12.refs_3_ = bf16[2,40,1792]{2,1,0:T(8,128)(2,1)S(1)} collective-permute-done((bf16[2,40,1792]{2,1,0:T(8,128)(2,1)S(1)}, bf16[2,40,1792]{2,1,0:T(8,128)(2,1)S(1)}, u32[]{:S(2)}, u32[]{:S(2)}) %collective-permute-start.12) | collective-permute-done | bytes 286752 | tf_op jit(solution)/shard_map/ppermute | solution.py:23
  51.5 1.5 %collective-permute-start.15 = (bf16[2,40,1792]{2,1,0:T(8,128)(2,1)S(1)}, bf16[2,40,1792]{2,1,0:T(8,128)(2,1)S(1)}, u32[]{:S(2)}, u32[]{:S(2)}) collective-permute-start(bf16[2,40,1792]{2,1,0:T(8,128)(2,1)S(1)} %pad_maximum_fusion.1), channel_id=1, source_target_pairs={{0,2},{2,0},{1,3},{3,1},{4,6},{6,4},{5,7},{7,5},{8,10},{10,8},{9,1... | collective-permute-start | bytes 860168 | tf_op jit(solution)/shard_map/ppermute | solution.py:23
  52.9 0.8 %shard_map.114 = bf16[160,1792]{1,0:T(8,128)(2,1)S(1)} custom-call(bf16[160,512]{1,0:T(8,128)(2,1)S(1)} %shard_map.113.refs_0_, bf16[160,512]{1,0:T(8,128)(2,1)S(1)} %collective-permute-done.11.refs_1_, bf16[1024,1792]{1,0:T(8,128)(2,1)S(1)} %get-tuple-element.31.refs_2_, bf16[2,40,1792]{2,1,0:T(8,128)(2,1)S(1)} %collective-permute-done.12.refs_3_), custom_call_target="tpu_custom_call" | custom-call | tf_op jit(solution)/shard_map/pallas_call | solution.py:271
  53.7 2.5 %collective-permute-start.13 = (bf16[40,1792]{1,0:T(8,128)(2,1)S(1)}, bf16[40,1792]{1,0:T(8,128)(2,1)S(1)}, u32[]{:S(2)}, u32[]{:S(2)}) collective-permute-start(bf16[40,1792]{1,0:T(8,128)(2,1)S(1)} %get-tuple-element.40), channel_id=1, source_target_pairs={{0,12},{4,8},{8,4},{12,0},{1,13},{5,9},{9,5},{13,1},{2,14},{6,10},... | collective-permute-start | bytes 430088 | tf_op jit(solution)/shard_map/ppermute | solution.py:23
  56.2 1.5 %collective-permute-start.14 = (bf16[40,1792]{1,0:T(8,128)(2,1)S(1)}, bf16[40,1792]{1,0:T(8,128)(2,1)S(1)}, u32[]{:S(2)}, u32[]{:S(2)}) collective-permute-start(bf16[40,1792]{1,0:T(8,128)(2,1)S(1)} %get-tuple-element.39), channel_id=1, source_target_pairs={{0,14},{2,12},{4,10},{6,8},{8,6},{10,4},{12,2},{14,0},{1,15},{3,13... | collective-permute-start | bytes 430088 | tf_op jit(solution)/shard_map/ppermute | solution.py:39
  57.7 0.6 collective-permute-start.16
  58.3 2.2 %collective-permute-start.17 = (bf16[40,1792]{1,0:T(8,128)(2,1)S(1)}, bf16[40,1792]{1,0:T(8,128)(2,1)S(1)}, u32[]{:S(2)}, u32[]{:S(2)}) collective-permute-start(bf16[40,1792]{1,0:T(8,128)(2,1)S(1)} %get-tuple-element.37), channel_id=1, source_target_pairs={{0,6},{2,4},{4,2},{6,0},{8,14},{10,12},{12,10},{14,8},{1,7},{3,5},... | collective-permute-start | bytes 430088 | tf_op jit(solution)/shard_map/ppermute | solution.py:39
  60.6 1.3 %collective-permute-done.13.refs_0_ = bf16[40,1792]{1,0:T(8,128)(2,1)S(1)} collective-permute-done((bf16[40,1792]{1,0:T(8,128)(2,1)S(1)}, bf16[40,1792]{1,0:T(8,128)(2,1)S(1)}, u32[]{:S(2)}, u32[]{:S(2)}) %collective-permute-start.13) | collective-permute-done | bytes 143392 | tf_op jit(solution)/shard_map/ppermute | solution.py:23
  61.9 3.7 %collective-permute-done.14.refs_3_ = bf16[40,1792]{1,0:T(8,128)(2,1)S(1)} collective-permute-done((bf16[40,1792]{1,0:T(8,128)(2,1)S(1)}, bf16[40,1792]{1,0:T(8,128)(2,1)S(1)}, u32[]{:S(2)}, u32[]{:S(2)}) %collective-permute-start.14) | collective-permute-done | bytes 143392 | tf_op jit(solution)/shard_map/ppermute | solution.py:39
  65.6 0.9 %shard_map.115 = (bf16[4,64,40]{2,1,0:T(8,128)(2,1)S(1)}, f32[64,1792]{1,0:T(8,128)S(1)}, f32[64,1792]{1,0:T(8,128)S(1)}) custom-call(f32[2,64,4]{2,1,0:T(8,128)S(1)} %shard_map.106.refs_2_.info_ref, bf16[40,1792]{1,0:T(8,128)(2,1)S(1)} %collective-permute-done.13.refs_0_, bf16[40,1792]{1,0:T(8,128)(2,1)S(1)} %get-tuple-element.42.refs_1_, ...), custom_call_target="tpu_custom_call" | custom-call | tf_op jit(solution)/shard_map/pallas_call | solution.py:304
  66.6 0.5 collective-permute-done.16.refs_2_
  67.1 2.9 %collective-permute-done.17.refs_3_ = bf16[40,1792]{1,0:T(8,128)(2,1)S(1)} collective-permute-done((bf16[40,1792]{1,0:T(8,128)(2,1)S(1)}, bf16[40,1792]{1,0:T(8,128)(2,1)S(1)}, u32[]{:S(2)}, u32[]{:S(2)}) %collective-permute-start.17) | collective-permute-done | bytes 143392 | tf_op jit(solution)/shard_map/ppermute | solution.py:39
  69.9 1.2 %shard_map.116 = bf16[64,3584]{1,0:T(8,128)(2,1)} custom-call(bf16[4,64,40]{2,1,0:T(8,128)(2,1)S(1)} %get-tuple-element.34.given_ref, f32[64,1792]{1,0:T(8,128)S(1)} %get-tuple-element.35.refs_0_, f32[64,1792]{1,0:T(8,128)S(1)} %get-tuple-element.36.refs_1_, bf16[40,1792]{1,0:T(8,128)(2,1)S(1)} %collective-permute-done.16.refs_2_, ...), custom_call_target="tpu_custom_call" | custom-call | tf_op jit(solution)/shard_map/pallas_call | solution.py:326
  (19 shorter events, 0.2 us)
Async XLA Ops:
  1.6 17.6 %collective-permute-start.1 = (bf16[40,3584]{1,0:T(8,128)(2,1)S(1)}, bf16[40,3584]{1,0:T(8,128)(2,1)S(1)}, u32[]{:S(2)}, u32[]{:S(2)}) collective-permute-start(bf16[40,3584]{1,0:T(8,128)(2,1)S(1)} %get-tuple-element.21.refs_3_), channel_id=1, source_target_pairs={{0,2},{2,0},{1,3},{3,1},{4,6},{6,4},{5,7},{7,5},{8,10},{10,8},{9,1... | collective-permute-start | bytes 860168 | tf_op jit(solution)/shard_map/ppermute | solution.py:23
  4.6 10.5 %collective-permute-start = (bf16[40,1792]{1,0:T(8,128)(2,1)S(1)}, bf16[40,1792]{1,0:T(8,128)(2,1)S(1)}, u32[]{:S(2)}, u32[]{:S(2)}) collective-permute-start(bf16[40,1792]{1,0:T(8,128)(2,1)S(1)} %get-tuple-element.23), channel_id=1, source_target_pairs={{0,8},{4,12},{8,0},{12,4},{1,9},{5,13},{9,1},{13,5},{2,10},{6,14},... | collective-permute-start | bytes 430088 | tf_op jit(solution)/shard_map/ppermute | solution.py:23
  7.2 16.1 %collective-permute-start.3 = (bf16[40,3584]{1,0:T(8,128)(2,1)S(1)}, bf16[40,3584]{1,0:T(8,128)(2,1)S(1)}, u32[]{:S(2)}, u32[]{:S(2)}) collective-permute-start(bf16[40,3584]{1,0:T(8,128)(2,1)S(1)} %get-tuple-element.26), channel_id=1, source_target_pairs={{0,4},{4,0},{8,12},{12,8},{1,5},{5,1},{9,13},{13,9},{2,6},{6,2},{1... | collective-permute-start | bytes 860168 | tf_op jit(solution)/shard_map/ppermute | solution.py:23
  8.8 14.5 %collective-permute-start.4 = (bf16[40,3584]{1,0:T(8,128)(2,1)S(1)}, bf16[40,3584]{1,0:T(8,128)(2,1)S(1)}, u32[]{:S(2)}, u32[]{:S(2)}) collective-permute-start(bf16[40,3584]{1,0:T(8,128)(2,1)S(1)} %get-tuple-element.26), channel_id=1, source_target_pairs={{0,2},{2,0},{1,3},{3,1},{4,6},{6,4},{5,7},{7,5},{8,10},{10,8},{9,1... | collective-permute-start | bytes 860168 | tf_op jit(solution)/shard_map/ppermute | solution.py:23
  9.3 9.9 %collective-permute-start.2 = (bf16[40,1792]{1,0:T(8,128)(2,1)S(1)}, bf16[40,1792]{1,0:T(8,128)(2,1)S(1)}, u32[]{:S(2)}, u32[]{:S(2)}) collective-permute-start(bf16[40,1792]{1,0:T(8,128)(2,1)S(1)} %get-tuple-element.25), channel_id=1, source_target_pairs={{0,8},{4,12},{8,0},{12,4},{1,9},{5,13},{9,1},{13,5},{2,10},{6,14},... | collective-permute-start | bytes 430088 | tf_op jit(solution)/shard_map/ppermute | solution.py:23
  15.0 9.3 %collective-permute-start.5 = (bf16[40,1792]{1,0:T(8,128)(2,1)S(1)}, bf16[40,1792]{1,0:T(8,128)(2,1)S(1)}, u32[]{:S(2)}, u32[]{:S(2)}) collective-permute-start(bf16[40,1792]{1,0:T(8,128)(2,1)S(1)} %shard_map.102.refs_5_), channel_id=1, source_target_pairs={{0,2},{2,0},{1,3},{3,1},{4,6},{6,4},{5,7},{7,5},{8,10},{10,8},{9,1... | collective-permute-start | bytes 430088 | tf_op jit(solution)/shard_map/ppermute | solution.py:23
  19.2 5.9 %collective-permute-start.6 = (bf16[40,1792]{1,0:T(8,128)(2,1)S(1)}, bf16[40,1792]{1,0:T(8,128)(2,1)S(1)}, u32[]{:S(2)}, u32[]{:S(2)}) collective-permute-start(bf16[40,1792]{1,0:T(8,128)(2,1)S(1)} %shard_map.104.refs_0_), channel_id=1, source_target_pairs={{0,2},{2,0},{1,3},{3,1},{4,6},{6,4},{5,7},{7,5},{8,10},{10,8},{9,1... | collective-permute-start | bytes 430088 | tf_op jit(solution)/shard_map/ppermute | solution.py:23
  20.9 10.5 %collective-permute-start.7 = (bf16[40,3584]{1,0:T(8,128)(2,1)S(1)}, bf16[40,3584]{1,0:T(8,128)(2,1)S(1)}, u32[]{:S(2)}, u32[]{:S(2)}) collective-permute-start(bf16[40,3584]{1,0:T(8,128)(2,1)S(1)} %shard_map.109), channel_id=1, source_target_pairs={{0,12},{4,8},{8,4},{12,0},{1,13},{5,9},{9,5},{13,1},{2,14},{6,10},... | collective-permute-start | bytes 860168 | tf_op jit(solution)/shard_map/ppermute | solution.py:23
  28.9 7.1 %collective-permute-start.10 = (bf16[160,512]{1,0:T(8,128)(2,1)S(1)}, bf16[160,512]{1,0:T(8,128)(2,1)S(1)}, u32[]{:S(2)}, u32[]{:S(2)}) collective-permute-start(bf16[160,512]{1,0:T(8,128)(2,1)S(1)} %pad_maximum_fusion.2), channel_id=1, source_target_pairs={{0,2},{2,0},{1,3},{3,1},{4,6},{6,4},{5,7},{7,5},{8,10},{10,8},{9,1... | collective-permute-start | bytes 491528 | tf_op jit(solution)/shard_map/ppermute | solution.py:23
  30.6 8.9 %collective-permute-start.9 = (bf16[40,3584]{1,0:T(8,128)(2,1)S(1)}, bf16[40,3584]{1,0:T(8,128)(2,1)S(1)}, u32[]{:S(2)}, u32[]{:S(2)}) collective-permute-start(bf16[40,3584]{1,0:T(8,128)(2,1)S(1)} %shard_map.105.refs_0_), channel_id=1, source_target_pairs={{0,4},{4,0},{8,12},{12,8},{1,5},{5,1},{9,13},{13,9},{2,6},{6,2},{1... | collective-permute-start | bytes 860168 | tf_op jit(solution)/shard_map/ppermute | solution.py:23
  31.4 10.0 %collective-permute-start.8 = (bf16[40,3584]{1,0:T(8,128)(2,1)S(1)}, bf16[40,3584]{1,0:T(8,128)(2,1)S(1)}, u32[]{:S(2)}, u32[]{:S(2)}) collective-permute-start(bf16[40,3584]{1,0:T(8,128)(2,1)S(1)} %shard_map.110), channel_id=1, source_target_pairs={{0,2},{2,0},{1,3},{3,1},{4,6},{6,4},{5,7},{7,5},{8,10},{10,8},{9,1... | collective-permute-start | bytes 860168 | tf_op jit(solution)/shard_map/ppermute | solution.py:23
  36.8 14.6 %collective-permute-start.12 = (bf16[2,40,1792]{2,1,0:T(8,128)(2,1)S(1)}, bf16[2,40,1792]{2,1,0:T(8,128)(2,1)S(1)}, u32[]{:S(2)}, u32[]{:S(2)}) collective-permute-start(bf16[2,40,1792]{2,1,0:T(8,128)(2,1)S(1)} %slice_bitcast_fusion), channel_id=1, source_target_pairs={{0,8},{4,12},{8,0},{12,4},{1,9},{5,13},{9,1},{13,5},{2,10},{6,14},... | collective-permute-start | bytes 860168 | tf_op jit(solution)/shard_map/ppermute | solution.py:23
  45.2 7.7 %collective-permute-start.11 = (bf16[160,512]{1,0:T(8,128)(2,1)S(1)}, bf16[160,512]{1,0:T(8,128)(2,1)S(1)}, u32[]{:S(2)}, u32[]{:S(2)}) collective-permute-start(bf16[160,512]{1,0:T(8,128)(2,1)S(1)} %pad_maximum_fusion.3), channel_id=1, source_target_pairs={{0,2},{2,0},{1,3},{3,1},{4,6},{6,4},{5,7},{7,5},{8,10},{10,8},{9,1... | collective-permute-start | bytes 491528 | tf_op jit(solution)/shard_map/ppermute | solution.py:23
  51.5 14.2 %collective-permute-start.15 = (bf16[2,40,1792]{2,1,0:T(8,128)(2,1)S(1)}, bf16[2,40,1792]{2,1,0:T(8,128)(2,1)S(1)}, u32[]{:S(2)}, u32[]{:S(2)}) collective-permute-start(bf16[2,40,1792]{2,1,0:T(8,128)(2,1)S(1)} %pad_maximum_fusion.1), channel_id=1, source_target_pairs={{0,2},{2,0},{1,3},{3,1},{4,6},{6,4},{5,7},{7,5},{8,10},{10,8},{9,1... | collective-permute-start | bytes 860168 | tf_op jit(solution)/shard_map/ppermute | solution.py:23
  53.7 8.1 %collective-permute-start.13 = (bf16[40,1792]{1,0:T(8,128)(2,1)S(1)}, bf16[40,1792]{1,0:T(8,128)(2,1)S(1)}, u32[]{:S(2)}, u32[]{:S(2)}) collective-permute-start(bf16[40,1792]{1,0:T(8,128)(2,1)S(1)} %get-tuple-element.40), channel_id=1, source_target_pairs={{0,12},{4,8},{8,4},{12,0},{1,13},{5,9},{9,5},{13,1},{2,14},{6,10},... | collective-permute-start | bytes 430088 | tf_op jit(solution)/shard_map/ppermute | solution.py:23
  56.2 9.4 %collective-permute-start.14 = (bf16[40,1792]{1,0:T(8,128)(2,1)S(1)}, bf16[40,1792]{1,0:T(8,128)(2,1)S(1)}, u32[]{:S(2)}, u32[]{:S(2)}) collective-permute-start(bf16[40,1792]{1,0:T(8,128)(2,1)S(1)} %get-tuple-element.39), channel_id=1, source_target_pairs={{0,14},{2,12},{4,10},{6,8},{8,6},{10,4},{12,2},{14,0},{1,15},{3,13... | collective-permute-start | bytes 430088 | tf_op jit(solution)/shard_map/ppermute | solution.py:39
  57.7 9.4 %collective-permute-start.16 = (bf16[40,1792]{1,0:T(8,128)(2,1)S(1)}, bf16[40,1792]{1,0:T(8,128)(2,1)S(1)}, u32[]{:S(2)}, u32[]{:S(2)}) collective-permute-start(bf16[40,1792]{1,0:T(8,128)(2,1)S(1)} %get-tuple-element.38), channel_id=1, source_target_pairs={{0,4},{4,0},{8,12},{12,8},{1,5},{5,1},{9,13},{13,9},{2,6},{6,2},{1... | collective-permute-start | bytes 430088 | tf_op jit(solution)/shard_map/ppermute | solution.py:23
  58.3 11.6 %collective-permute-start.17 = (bf16[40,1792]{1,0:T(8,128)(2,1)S(1)}, bf16[40,1792]{1,0:T(8,128)(2,1)S(1)}, u32[]{:S(2)}, u32[]{:S(2)}) collective-permute-start(bf16[40,1792]{1,0:T(8,128)(2,1)S(1)} %get-tuple-element.37), channel_id=1, source_target_pairs={{0,6},{2,4},{4,2},{6,0},{8,14},{10,12},{12,10},{14,8},{1,7},{3,5},... | collective-permute-start | bytes 430088 | tf_op jit(solution)/shard_map/ppermute | solution.py:39

commit v5 on v4

--- a/solution.py
+++ b/solution.py
@@ -134,19 +134,6 @@
     return list(call(lambda *refs: None, shapes, specs, aliases=aliases)(*behind, *held))
 
 
-def load(arrays, behind):
-    count = len(arrays)
-
-    def kernel(*refs):
-        fetch(refs[:count], refs[count + len(behind) : -1], refs[-1])
-
-    shapes = [pltpu.VMEM(a.shape, a.dtype) for a in arrays]
-    specs = [IN_HBM] * count + [ANY] * len(behind)
-    return call(kernel, shapes, specs, [pltpu.SemaphoreType.DMA((count,))])(
-        *[in_hbm(a) for a in arrays], *behind
-    )
-
-
 def as_column(row, size):
     same = lax.broadcasted_iota(jnp.int32, (size, size), 0) == (
         lax.broadcasted_iota(jnp.int32, (size, size), 1)
@@ -162,14 +149,22 @@
         copy.wait()
 
 
-def partial_logits(tokens, tenant, router_weight, adapter_down, adapter_up, behind):
+def load_and_route(arrays, tokens, tenant, router_weight, adapter_down, adapter_up, behind):
+    count = len(arrays)
     tok_rows = tokens.shape[0]
     ranks, experts = adapter_up.shape
     given = [tokens, adapter_down, router_weight.T, adapter_up.T, tenant.reshape(1, tok_rows)]
+    total = count + len(given)
 
     def kernel(*refs):
-        out_ref, *held, sems = refs[len(given) + len(behind) :]
-        fetch(refs[: len(given)], held, sems)
+        taken, rest = refs[total + len(behind) :][:count], refs[total + len(behind) + count :]
+        out_ref, *held, sems = rest
+        pairs = list(zip(refs[count:total], held)) + list(zip(refs[:count], taken))
+        copies = [pltpu.make_async_copy(a, b, sems.at[i]) for i, (a, b) in enumerate(pairs)]
+        for copy in copies:
+            copy.start()
+        for copy in copies[: len(given)]:
+            copy.wait()
         tokens_ref, down_ref, router_ref, up_ref, tenant_ref = held
         lowrank = jnp.dot(tokens_ref[...], down_ref[...], preferred_element_type=f32)
         owner = (lax.broadcasted_iota(jnp.int32, (tok_rows, ranks), 1) // RANK).astype(f32)
@@ -186,12 +181,18 @@
             precision=lax.Precision.HIGHEST,
             preferred_element_type=f32,
         )
-
-    shapes = [jax.ShapeDtypeStruct((experts, tok_rows), f32)]
-    specs = [IN_HBM] * len(given) + [ANY] * len(behind)
+        for copy in copies[len(given) :]:
+            copy.wait()
+
+    shapes = [pltpu.VMEM(a.shape, a.dtype) for a in arrays]
+    shapes.append(jax.ShapeDtypeStruct((experts, tok_rows), f32))
+    specs = [IN_HBM] * total + [ANY] * len(behind)
     scratch = [pltpu.VMEM(a.shape, a.dtype) for a in given]
-    scratch.append(pltpu.SemaphoreType.DMA((len(given),)))
-    return call(kernel, shapes, specs, scratch)(*[in_hbm(a) for a in given], *behind)[0]
+    scratch.append(pltpu.SemaphoreType.DMA((total,)))
+    *taken, logits = call(kernel, shapes, specs, scratch)(
+        *[in_hbm(a) for a in (*arrays, *given)], *behind
+    )
+    return taken, logits
 
 
 def route_info(parts, place, expert_place, routes_t, behind):
@@ -360,12 +361,17 @@
         blocks[k][0] = [swap(part, "ep", k) for part in outgoing[k]]
     for k in [0, *near]:
         blocks[k][1:] = [[swap(outgoing[k][0], "node", j)] for j in others]
-    gate_w, up_w, down_w = load(
-        [gate_weight[0], up_weight[0], down_weight[0, 0]], [outgoing[0][0]]
-    )
-    firsts = hold([blocks[k][0][0] for k in middle], [gate_w])
-    logits = partial_logits(tokens, tenant, router_weight, adapter_down, adapter_up, firsts[:1])
-    logits = lax.all_gather(logits, "sub")
+    (gate_w, up_w, down_w), logits = load_and_route(
+        [gate_weight[0], up_weight[0], down_weight[0, 0]],
+        tokens,
+        tenant,
+        router_weight,
+        adapter_down,
+        adapter_up,
+        outgoing[0],
+    )
+    firsts = hold([blocks[k][0][0] for k in middle], [logits])
+    logits = lax.all_gather(hold([logits], firsts[:1])[0], "sub")
     for k, part in zip(middle, firsts):
         blocks[k][0][0] = part
         blocks[k][1:] = [[swap(part, "node", j)] for j in others]

time: 71.3 us -> 71.3 us (level)
  waiting for transfers between devices: 20.2 us -> 21.7 us
  Pallas kernels: 15.4 us -> 14 us
    ppermute x2, waiting for transfers between devices: 6.61 us -> 8.42 us  [send(): return lax.ppermute(value, ('ep', 'node'), pairs)]
    pallas_call x2 -> x1, Pallas kernels: 6.15 us -> 4.74 us  [load_and_route(): call(kernel, shapes, specs, scratch)]
    ppermute x2, starting transfers between devices: 3.68 us -> 2.78 us  [send(): return lax.ppermute(value, ('ep', 'node'), pairs)]
    ppermute x16, starting transfers between devices: 25 us -> 25.8 us  [swap(): lax.ppermute(value, axis, [(i, partner(i, step)) for i in range(count)])]
  transfers between devices with their start and end apart: 18 -> 18, of which waited for: 10 -> 9; matrix products, arithmetic and copies ran while one was open for 0% -> 0% of each run, Pallas kernels for 18% -> 16%
where the time goes in v5:
time: 71.3 us; the launch traced here: 71.1 us
  starting transfers between devices  28.6 us (40%)
  waiting for transfers between devices  21.7 us (30%)
  Pallas kernels  14 us (20%)
  blocking collectives  6.32 us (9%)
    ppermute x16, starting transfers between devices, swap(): lax.ppermute(value, axis, [(i, partner(i, step)) for i in range(count)])  25.8 us
    ppermute x16, waiting for transfers between devices, swap(): lax.ppermute(value, axis, [(i, partner(i, step)) for i in range(count)])  13.3 us
    ppermute x2, waiting for transfers between devices, send(): return lax.ppermute(value, ('ep', 'node'), pairs)  8.42 us
    pallas_call x1, Pallas kernels, load_and_route(): call(kernel, shapes, specs, scratch)  4.74 us
    all_gather x2, blocking collectives, gate_up(): return activate(own, lax.all_gather(sent, 'sub'))  4.55 us
    ppermute x2, starting transfers between devices, send(): return lax.ppermute(value, ('ep', 'node'), pairs)  2.78 us
    pallas_call x2, Pallas kernels, dots(): return call(kernel, shapes, specs)(rows, *weights, *behind)  2.73 us
    all_gather x1, blocking collectives, body(): logits = lax.all_gather(hold([logits], firsts[:1])[0], 'sub')  1.77 us
  transfers between devices with their start and end apart: 18, of which 9 were waited for; matrix products, arithmetic and copies ran while one was open for 0% of the time, Pallas kernels for 16%

profile of v5, /device:TPU:0, one launch (start us, length us, event | category | flops | bytes accessed | tf_op | source)
XLA Modules:
  0.0 71.1 jit_solution(9627313339069417693)
XLA Ops:
  0.0 1.6 %shard_map.100 = (f32[4,64]{1,0:T(4,128)S(1)}, bf16[40,1792]{1,0:T(8,128)(2,1)S(1)}, bf16[40,1792]{1,0:T(8,128)(2,1)S(1)}, bf16[40,3584]{1,0:T(8,128)(2,1)S(1)},...) custom-call(s32[1,4]{1,0:T(1,128)} %bitcast.44, s32[2,64]{1,0:T(2,128)} %bitcast.42, bf16[64,3584]{1,0:T(8,128)(2,1)} %refs_3_.1), custom_call_target="tpu_custom_call" | custom-call | tf_op jit(solution)/shard_map/pallas_call | solution.py:124
  1.6 3.0 %collective-permute-start.1 = (bf16[40,3584]{1,0:T(8,128)(2,1)S(1)}, bf16[40,3584]{1,0:T(8,128)(2,1)S(1)}, u32[]{:S(2)}, u32[]{:S(2)}) collective-permute-start(bf16[40,3584]{1,0:T(8,128)(2,1)S(1)} %get-tuple-element.22.refs_8_), channel_id=1, source_target_pairs={{0,2},{2,0},{1,3},{3,1},{4,6},{6,4},{5,7},{7,5},{8,10},{10,8},{9,1... | collective-permute-start | bytes 860168 | tf_op jit(solution)/shard_map/ppermute | solution.py:23
  4.6 2.6 %collective-permute-start = (bf16[40,1792]{1,0:T(8,128)(2,1)S(1)}, bf16[40,1792]{1,0:T(8,128)(2,1)S(1)}, u32[]{:S(2)}, u32[]{:S(2)}) collective-permute-start(bf16[40,1792]{1,0:T(8,128)(2,1)S(1)} %get-tuple-element.24), channel_id=1, source_target_pairs={{0,8},{4,12},{8,0},{12,4},{1,9},{5,13},{9,1},{13,5},{2,10},{6,14},... | collective-permute-start | bytes 430088 | tf_op jit(solution)/shard_map/ppermute | solution.py:23
  7.2 1.6 %collective-permute-start.3 = (bf16[40,3584]{1,0:T(8,128)(2,1)S(1)}, bf16[40,3584]{1,0:T(8,128)(2,1)S(1)}, u32[]{:S(2)}, u32[]{:S(2)}) collective-permute-start(bf16[40,3584]{1,0:T(8,128)(2,1)S(1)} %get-tuple-element.27), channel_id=1, source_target_pairs={{0,4},{4,0},{8,12},{12,8},{1,5},{5,1},{9,13},{13,9},{2,6},{6,2},{1... | collective-permute-start | bytes 860168 | tf_op jit(solution)/shard_map/ppermute | solution.py:23
  8.8 0.5 collective-permute-start.4
  9.3 0.3 collective-permute-start.2
  9.6 4.7 %shard_map.101 = (bf16[3584,512]{1,0:T(8,128)(2,1)S(1)}, bf16[3584,512]{1,0:T(8,128)(2,1)S(1)}, bf16[1024,1792]{1,0:T(8,128)(2,1)S(1)}, f32[4,64]{1,0:T(4,128)S(1)}) custom-call(bf16[3584,512]{1,0:T(8,128)(2,1)} %bitcast.38, bf16[3584,512]{1,0:T(8,128)(2,1)} %bitcast.39, bf16[1024,1792]{1,0:T(8,128)(2,1)} %bitcast.40, bf16[64,3584]{1,0:T(8,128)(2,1)} %refs_3_.1, ...), custom_call_target="tpu_custom_call" | custom-call | tf_op jit(solution)/shard_map/pallas_call | solution.py:192
  14.4 0.7 collective-permute-done.refs_1_
  15.0 0.9 %collective-permute-start.5 = (bf16[40,1792]{1,0:T(8,128)(2,1)S(1)}, bf16[40,1792]{1,0:T(8,128)(2,1)S(1)}, u32[]{:S(2)}, u32[]{:S(2)}) collective-permute-start(bf16[40,1792]{1,0:T(8,128)(2,1)S(1)} %shard_map.102.refs_0_), channel_id=1, source_target_pairs={{0,2},{2,0},{1,3},{3,1},{4,6},{6,4},{5,7},{7,5},{8,10},{10,8},{9,1... | collective-permute-start | bytes 430088 | tf_op jit(solution)/shard_map/ppermute | solution.py:23
  16.0 1.8 %all-gather.3.refs_0_.parts_ref = f32[2,4,64]{2,1,0:T(4,128)S(1)} all-gather(f32[1,4,64]{2,1,0:T(4,128)S(1)} %bitcast.37), channel_id=2, replica_groups=mesh['rep'=2,'ep'=4,'node'=2,'sub'=2] {'sub'}, dimensions={0}, use_global_device_ids=true | all-gather | bytes 3072 | tf_op jit(solution)/shard_map/all_gather | solution.py:374
  17.7 1.4 %collective-permute-done.2.refs_2_ = bf16[40,1792]{1,0:T(8,128)(2,1)S(1)} collective-permute-done((bf16[40,1792]{1,0:T(8,128)(2,1)S(1)}, bf16[40,1792]{1,0:T(8,128)(2,1)S(1)}, u32[]{:S(2)}, u32[]{:S(2)}) %collective-permute-start.2) | collective-permute-done | bytes 143392 | tf_op jit(solution)/shard_map/ppermute | solution.py:23
  19.1 0.0 collective-permute-done.1.refs_1_
  19.1 0.5 collective-permute-start.6
  19.7 2.7 %collective-permute-start.7 = (bf16[40,3584]{1,0:T(8,128)(2,1)S(1)}, bf16[40,3584]{1,0:T(8,128)(2,1)S(1)}, u32[]{:S(2)}, u32[]{:S(2)}) collective-permute-start(bf16[40,3584]{1,0:T(8,128)(2,1)S(1)} %shard_map.109), channel_id=1, source_target_pairs={{0,12},{4,8},{8,4},{12,0},{1,13},{5,9},{9,5},{13,1},{2,14},{6,10},... | collective-permute-start | bytes 860168 | tf_op jit(solution)/shard_map/ppermute | solution.py:23
  22.4 1.0 %shard_map.106.refs_2_.info_ref = f32[2,64,4]{2,1,0:T(8,128)S(1)} custom-call(f32[2,4,64]{2,1,0:T(4,128)S(1)} %all-gather.3.refs_0_.parts_ref, f32[4,64]{1,0:T(4,128)S(1)} %get-tuple-element.25.place_ref, s32[1,4]{1,0:T(1,128)} %bitcast.45, s32[2,64]{1,0:T(2,128)} %bitcast.43, bf16[40,3584]{1,0:T(8,128)(2,1)S(1)} %shard_map.105.refs_0_), custom_call_target="tpu_custom_call" | custom-call | tf_op jit(solution)/shard_map/pallas_call | solution.py:224
  23.5 0.0 collective-permute-done.5
  23.5 0.8 %collective-permute-done.6 = bf16[40,1792]{1,0:T(8,128)(2,1)S(1)} collective-permute-done((bf16[40,1792]{1,0:T(8,128)(2,1)S(1)}, bf16[40,1792]{1,0:T(8,128)(2,1)S(1)}, u32[]{:S(2)}, u32[]{:S(2)}) %collective-permute-start.6) | collective-permute-done | bytes 143392 | tf_op jit(solution)/shard_map/ppermute | solution.py:23
  24.2 0.1 maximum_maximum_fusion.rows_ref
  24.3 1.4 %shard_map.107 = (f32[160,1024]{1,0:T(8,128)S(1)}, bf16[160,1024]{1,0:T(8,128)(2,1)S(1)}) custom-call(bf16[160,3584]{1,0:T(8,128)(2,1)S(1)} %maximum_maximum_fusion.rows_ref, bf16[3584,512]{1,0:T(8,128)(2,1)S(1)} %get-tuple-element.28.refs_0_, bf16[3584,512]{1,0:T(8,128)(2,1)S(1)} %get-tuple-element.29.refs_1_, f32[2,64,4]{2,1,0:T(8,128)S(1)} %shard_map.106.refs_2_.info_ref), custom_call_target="tpu_custom_call" | custom-call | tf_op jit(solution)/shard_map/pallas_call | solution.py:252
  25.7 2.3 %all-gather.1 = bf16[320,1024]{1,0:T(8,128)(2,1)S(1)} all-gather(bf16[160,1024]{1,0:T(8,128)(2,1)S(1)} %get-tuple-element.31), channel_id=3, replica_groups=mesh['rep'=2,'ep'=4,'node'=2,'sub'=2] {'sub'}, dimensions={0}, use_global_device_ids=true | all-gather | bytes 983040 | tf_op jit(solution)/shard_map/all_gather | solution.py:396
  28.0 0.1 shard_map.108.refs_0_
  28.1 1.3 %collective-permute-start.10 = (bf16[160,512]{1,0:T(8,128)(2,1)S(1)}, bf16[160,512]{1,0:T(8,128)(2,1)S(1)}, u32[]{:S(2)}, u32[]{:S(2)}) collective-permute-start(bf16[160,512]{1,0:T(8,128)(2,1)S(1)} %pad_maximum_fusion.2), channel_id=1, source_target_pairs={{0,2},{2,0},{1,3},{3,1},{4,6},{6,4},{5,7},{7,5},{8,10},{10,8},{9,1... | collective-permute-start | bytes 491528 | tf_op jit(solution)/shard_map/ppermute | solution.py:23
  29.4 1.7 %collective-permute-start.9 = (bf16[40,3584]{1,0:T(8,128)(2,1)S(1)}, bf16[40,3584]{1,0:T(8,128)(2,1)S(1)}, u32[]{:S(2)}, u32[]{:S(2)}) collective-permute-start(bf16[40,3584]{1,0:T(8,128)(2,1)S(1)} %shard_map.105.refs_0_), channel_id=1, source_target_pairs={{0,4},{4,0},{8,12},{12,8},{1,5},{5,1},{9,13},{13,9},{2,6},{6,2},{1... | collective-permute-start | bytes 860168 | tf_op jit(solution)/shard_map/ppermute | solution.py:23
  31.1 1.5 %collective-permute-start.8 = (bf16[40,3584]{1,0:T(8,128)(2,1)S(1)}, bf16[40,3584]{1,0:T(8,128)(2,1)S(1)}, u32[]{:S(2)}, u32[]{:S(2)}) collective-permute-start(bf16[40,3584]{1,0:T(8,128)(2,1)S(1)} %shard_map.110), channel_id=1, source_target_pairs={{0,2},{2,0},{1,3},{3,1},{4,6},{6,4},{5,7},{7,5},{8,10},{10,8},{9,1... | collective-permute-start | bytes 860168 | tf_op jit(solution)/shard_map/ppermute | solution.py:23
  32.6 2.6 %collective-permute-done.10.refs_1_ = bf16[160,512]{1,0:T(8,128)(2,1)S(1)} collective-permute-done((bf16[160,512]{1,0:T(8,128)(2,1)S(1)}, bf16[160,512]{1,0:T(8,128)(2,1)S(1)}, u32[]{:S(2)}, u32[]{:S(2)}) %collective-permute-start.10) | collective-permute-done | bytes 163872 | tf_op jit(solution)/shard_map/ppermute | solution.py:23
  35.2 0.8 %shard_map.111 = bf16[160,1792]{1,0:T(8,128)(2,1)S(1)} custom-call(bf16[160,512]{1,0:T(8,128)(2,1)S(1)} %shard_map.108.refs_0_, bf16[160,512]{1,0:T(8,128)(2,1)S(1)} %collective-permute-done.10.refs_1_, bf16[1024,1792]{1,0:T(8,128)(2,1)S(1)} %get-tuple-element.33.refs_2_), custom_call_target="tpu_custom_call" | custom-call | tf_op jit(solution)/shard_map/pallas_call | solution.py:272
  36.0 3.2 %collective-permute-start.12 = (bf16[2,40,1792]{2,1,0:T(8,128)(2,1)S(1)}, bf16[2,40,1792]{2,1,0:T(8,128)(2,1)S(1)}, u32[]{:S(2)}, u32[]{:S(2)}) collective-permute-start(bf16[2,40,1792]{2,1,0:T(8,128)(2,1)S(1)} %slice_bitcast_fusion), channel_id=1, source_target_pairs={{0,8},{4,12},{8,0},{12,4},{1,9},{5,13},{9,1},{13,5},{2,10},{6,14},... | collective-permute-start | bytes 860168 | tf_op jit(solution)/shard_map/ppermute | solution.py:23
  39.2 1.3 %collective-permute-done.8 = bf16[40,3584]{1,0:T(8,128)(2,1)S(1)} collective-permute-done((bf16[40,3584]{1,0:T(8,128)(2,1)S(1)}, bf16[40,3584]{1,0:T(8,128)(2,1)S(1)}, u32[]{:S(2)}, u32[]{:S(2)}) %collective-permute-start.8) | collective-permute-done | bytes 286752 | tf_op jit(solution)/shard_map/ppermute | solution.py:23
  40.6 0.1 pad_maximum_fusion.rows_ref
  40.7 1.4 %shard_map.112 = (f32[160,1024]{1,0:T(8,128)S(1)}, bf16[160,1024]{1,0:T(8,128)(2,1)S(1)}) custom-call(bf16[160,3584]{1,0:T(8,128)(2,1)S(1)} %pad_maximum_fusion.rows_ref, bf16[3584,512]{1,0:T(8,128)(2,1)S(1)} %get-tuple-element.28.refs_0_, bf16[3584,512]{1,0:T(8,128)(2,1)S(1)} %get-tuple-element.29.refs_1_, bf16[2,2,40,1792]{3,2,1,0:T(8,128)(2,1)S(1)} %bitcast.33), custom_call_target="tpu_custom_call" | custom-call | tf_op jit(solution)/shard_map/pallas_call | solution.py:252
  42.0 2.3 %all-gather.2 = bf16[320,1024]{1,0:T(8,128)(2,1)S(1)} all-gather(bf16[160,1024]{1,0:T(8,128)(2,1)S(1)} %get-tuple-element.35), channel_id=4, replica_groups=mesh['rep'=2,'ep'=4,'node'=2,'sub'=2] {'sub'}, dimensions={0}, use_global_device_ids=true | all-gather | bytes 983040 | tf_op jit(solution)/shard_map/all_gather | solution.py:396
  44.3 0.1 shard_map.113.refs_0_
  44.5 1.3 %collective-permute-start.11 = (bf16[160,512]{1,0:T(8,128)(2,1)S(1)}, bf16[160,512]{1,0:T(8,128)(2,1)S(1)}, u32[]{:S(2)}, u32[]{:S(2)}) collective-permute-start(bf16[160,512]{1,0:T(8,128)(2,1)S(1)} %pad_maximum_fusion.3), channel_id=1, source_target_pairs={{0,2},{2,0},{1,3},{3,1},{4,6},{6,4},{5,7},{7,5},{8,10},{10,8},{9,1... | collective-permute-start | bytes 491528 | tf_op jit(solution)/shard_map/ppermute | solution.py:23
  45.7 5.4 %collective-permute-done.12.refs_3_ = bf16[2,40,1792]{2,1,0:T(8,128)(2,1)S(1)} collective-permute-done((bf16[2,40,1792]{2,1,0:T(8,128)(2,1)S(1)}, bf16[2,40,1792]{2,1,0:T(8,128)(2,1)S(1)}, u32[]{:S(2)}, u32[]{:S(2)}) %collective-permute-start.12) | collective-permute-done | bytes 286752 | tf_op jit(solution)/shard_map/ppermute | solution.py:23
  51.2 0.6 collective-permute-start.15
  51.8 0.0 collective-permute-done.11.refs_1_
  51.8 0.8 %shard_map.114 = bf16[160,1792]{1,0:T(8,128)(2,1)S(1)} custom-call(bf16[160,512]{1,0:T(8,128)(2,1)S(1)} %shard_map.113.refs_0_, bf16[160,512]{1,0:T(8,128)(2,1)S(1)} %collective-permute-done.11.refs_1_, bf16[1024,1792]{1,0:T(8,128)(2,1)S(1)} %get-tuple-element.33.refs_2_, bf16[2,40,1792]{2,1,0:T(8,128)(2,1)S(1)} %collective-permute-done.12.refs_3_), custom_call_target="tpu_custom_call" | custom-call | tf_op jit(solution)/shard_map/pallas_call | solution.py:272
  52.7 3.6 %collective-permute-start.13 = (bf16[40,1792]{1,0:T(8,128)(2,1)S(1)}, bf16[40,1792]{1,0:T(8,128)(2,1)S(1)}, u32[]{:S(2)}, u32[]{:S(2)}) collective-permute-start(bf16[40,1792]{1,0:T(8,128)(2,1)S(1)} %get-tuple-element.42), channel_id=1, source_target_pairs={{0,12},{4,8},{8,4},{12,0},{1,13},{5,9},{9,5},{13,1},{2,14},{6,10},... | collective-permute-start | bytes 430088 | tf_op jit(solution)/shard_map/ppermute | solution.py:23
  56.2 1.3 %collective-permute-start.14 = (bf16[40,1792]{1,0:T(8,128)(2,1)S(1)}, bf16[40,1792]{1,0:T(8,128)(2,1)S(1)}, u32[]{:S(2)}, u32[]{:S(2)}) collective-permute-start(bf16[40,1792]{1,0:T(8,128)(2,1)S(1)} %get-tuple-element.41), channel_id=1, source_target_pairs={{0,14},{2,12},{4,10},{6,8},{8,6},{10,4},{12,2},{14,0},{1,15},{3,13... | collective-permute-start | bytes 430088 | tf_op jit(solution)/shard_map/ppermute | solution.py:39
  57.5 0.5 collective-permute-start.16
  58.0 1.5 %collective-permute-start.17 = (bf16[40,1792]{1,0:T(8,128)(2,1)S(1)}, bf16[40,1792]{1,0:T(8,128)(2,1)S(1)}, u32[]{:S(2)}, u32[]{:S(2)}) collective-permute-start(bf16[40,1792]{1,0:T(8,128)(2,1)S(1)} %get-tuple-element.39), channel_id=1, source_target_pairs={{0,6},{2,4},{4,2},{6,0},{8,14},{10,12},{12,10},{14,8},{1,7},{3,5},... | collective-permute-start | bytes 430088 | tf_op jit(solution)/shard_map/ppermute | solution.py:39
  59.5 1.0 %collective-permute-done.13.refs_0_ = bf16[40,1792]{1,0:T(8,128)(2,1)S(1)} collective-permute-done((bf16[40,1792]{1,0:T(8,128)(2,1)S(1)}, bf16[40,1792]{1,0:T(8,128)(2,1)S(1)}, u32[]{:S(2)}, u32[]{:S(2)}) %collective-permute-start.13) | collective-permute-done | bytes 143392 | tf_op jit(solution)/shard_map/ppermute | solution.py:23
  60.5 5.2 %collective-permute-done.14.refs_3_ = bf16[40,1792]{1,0:T(8,128)(2,1)S(1)} collective-permute-done((bf16[40,1792]{1,0:T(8,128)(2,1)S(1)}, bf16[40,1792]{1,0:T(8,128)(2,1)S(1)}, u32[]{:S(2)}, u32[]{:S(2)}) %collective-permute-start.14) | collective-permute-done | bytes 143392 | tf_op jit(solution)/shard_map/ppermute | solution.py:39
  65.6 0.0 collective-permute-done.15.refs_4_
  65.6 0.9 %shard_map.115 = (bf16[4,64,40]{2,1,0:T(8,128)(2,1)S(1)}, f32[64,1792]{1,0:T(8,128)S(1)}, f32[64,1792]{1,0:T(8,128)S(1)}) custom-call(f32[2,64,4]{2,1,0:T(8,128)S(1)} %shard_map.106.refs_2_.info_ref, bf16[40,1792]{1,0:T(8,128)(2,1)S(1)} %collective-permute-done.13.refs_0_, bf16[40,1792]{1,0:T(8,128)(2,1)S(1)} %get-tuple-element.44.refs_1_, ...), custom_call_target="tpu_custom_call" | custom-call | tf_op jit(solution)/shard_map/pallas_call | solution.py:305
  66.6 0.0 collective-permute-done.16.refs_2_
  66.6 3.3 %collective-permute-done.17.refs_3_ = bf16[40,1792]{1,0:T(8,128)(2,1)S(1)} collective-permute-done((bf16[40,1792]{1,0:T(8,128)(2,1)S(1)}, bf16[40,1792]{1,0:T(8,128)(2,1)S(1)}, u32[]{:S(2)}, u32[]{:S(2)}) %collective-permute-start.17) | collective-permute-done | bytes 143392 | tf_op jit(solution)/shard_map/ppermute | solution.py:39
  69.9 1.2 %shard_map.116 = bf16[64,3584]{1,0:T(8,128)(2,1)} custom-call(bf16[4,64,40]{2,1,0:T(8,128)(2,1)S(1)} %get-tuple-element.36.given_ref, f32[64,1792]{1,0:T(8,128)S(1)} %get-tuple-element.37.refs_0_, f32[64,1792]{1,0:T(8,128)S(1)} %get-tuple-element.38.refs_1_, bf16[40,1792]{1,0:T(8,128)(2,1)S(1)} %collective-permute-done.16.refs_2_, ...), custom_call_target="tpu_custom_call" | custom-call | tf_op jit(solution)/shard_map/pallas_call | solution.py:327
  (19 shorter events, 0.2 us)
Async XLA Ops:
  1.6 17.6 %collective-permute-start.1 = (bf16[40,3584]{1,0:T(8,128)(2,1)S(1)}, bf16[40,3584]{1,0:T(8,128)(2,1)S(1)}, u32[]{:S(2)}, u32[]{:S(2)}) collective-permute-start(bf16[40,3584]{1,0:T(8,128)(2,1)S(1)} %get-tuple-element.22.refs_8_), channel_id=1, source_target_pairs={{0,2},{2,0},{1,3},{3,1},{4,6},{6,4},{5,7},{7,5},{8,10},{10,8},{9,1... | collective-permute-start | bytes 860168 | tf_op jit(solution)/shard_map/ppermute | solution.py:23
  4.6 10.5 %collective-permute-start = (bf16[40,1792]{1,0:T(8,128)(2,1)S(1)}, bf16[40,1792]{1,0:T(8,128)(2,1)S(1)}, u32[]{:S(2)}, u32[]{:S(2)}) collective-permute-start(bf16[40,1792]{1,0:T(8,128)(2,1)S(1)} %get-tuple-element.24), channel_id=1, source_target_pairs={{0,8},{4,12},{8,0},{12,4},{1,9},{5,13},{9,1},{13,5},{2,10},{6,14},... | collective-permute-start | bytes 430088 | tf_op jit(solution)/shard_map/ppermute | solution.py:23
  7.2 15.2 %collective-permute-start.3 = (bf16[40,3584]{1,0:T(8,128)(2,1)S(1)}, bf16[40,3584]{1,0:T(8,128)(2,1)S(1)}, u32[]{:S(2)}, u32[]{:S(2)}) collective-permute-start(bf16[40,3584]{1,0:T(8,128)(2,1)S(1)} %get-tuple-element.27), channel_id=1, source_target_pairs={{0,4},{4,0},{8,12},{12,8},{1,5},{5,1},{9,13},{13,9},{2,6},{6,2},{1... | collective-permute-start | bytes 860168 | tf_op jit(solution)/shard_map/ppermute | solution.py:23
  8.8 13.7 %collective-permute-start.4 = (bf16[40,3584]{1,0:T(8,128)(2,1)S(1)}, bf16[40,3584]{1,0:T(8,128)(2,1)S(1)}, u32[]{:S(2)}, u32[]{:S(2)}) collective-permute-start(bf16[40,3584]{1,0:T(8,128)(2,1)S(1)} %get-tuple-element.27), channel_id=1, source_target_pairs={{0,2},{2,0},{1,3},{3,1},{4,6},{6,4},{5,7},{7,5},{8,10},{10,8},{9,1... | collective-permute-start | bytes 860168 | tf_op jit(solution)/shard_map/ppermute | solution.py:23
  9.3 9.8 %collective-permute-start.2 = (bf16[40,1792]{1,0:T(8,128)(2,1)S(1)}, bf16[40,1792]{1,0:T(8,128)(2,1)S(1)}, u32[]{:S(2)}, u32[]{:S(2)}) collective-permute-start(bf16[40,1792]{1,0:T(8,128)(2,1)S(1)} %get-tuple-element.26), channel_id=1, source_target_pairs={{0,8},{4,12},{8,0},{12,4},{1,9},{5,13},{9,1},{13,5},{2,10},{6,14},... | collective-permute-start | bytes 430088 | tf_op jit(solution)/shard_map/ppermute | solution.py:23
  15.0 8.4 %collective-permute-start.5 = (bf16[40,1792]{1,0:T(8,128)(2,1)S(1)}, bf16[40,1792]{1,0:T(8,128)(2,1)S(1)}, u32[]{:S(2)}, u32[]{:S(2)}) collective-permute-start(bf16[40,1792]{1,0:T(8,128)(2,1)S(1)} %shard_map.102.refs_0_), channel_id=1, source_target_pairs={{0,2},{2,0},{1,3},{3,1},{4,6},{6,4},{5,7},{7,5},{8,10},{10,8},{9,1... | collective-permute-start | bytes 430088 | tf_op jit(solution)/shard_map/ppermute | solution.py:23
  19.1 5.1 %collective-permute-start.6 = (bf16[40,1792]{1,0:T(8,128)(2,1)S(1)}, bf16[40,1792]{1,0:T(8,128)(2,1)S(1)}, u32[]{:S(2)}, u32[]{:S(2)}) collective-permute-start(bf16[40,1792]{1,0:T(8,128)(2,1)S(1)} %shard_map.104.refs_0_), channel_id=1, source_target_pairs={{0,2},{2,0},{1,3},{3,1},{4,6},{6,4},{5,7},{7,5},{8,10},{10,8},{9,1... | collective-permute-start | bytes 430088 | tf_op jit(solution)/shard_map/ppermute | solution.py:23
  19.7 11.5 %collective-permute-start.7 = (bf16[40,3584]{1,0:T(8,128)(2,1)S(1)}, bf16[40,3584]{1,0:T(8,128)(2,1)S(1)}, u32[]{:S(2)}, u32[]{:S(2)}) collective-permute-start(bf16[40,3584]{1,0:T(8,128)(2,1)S(1)} %shard_map.109), channel_id=1, source_target_pairs={{0,12},{4,8},{8,4},{12,0},{1,13},{5,9},{9,5},{13,1},{2,14},{6,10},... | collective-permute-start | bytes 860168 | tf_op jit(solution)/shard_map/ppermute | solution.py:23
  28.1 7.1 %collective-permute-start.10 = (bf16[160,512]{1,0:T(8,128)(2,1)S(1)}, bf16[160,512]{1,0:T(8,128)(2,1)S(1)}, u32[]{:S(2)}, u32[]{:S(2)}) collective-permute-start(bf16[160,512]{1,0:T(8,128)(2,1)S(1)} %pad_maximum_fusion.2), channel_id=1, source_target_pairs={{0,2},{2,0},{1,3},{3,1},{4,6},{6,4},{5,7},{7,5},{8,10},{10,8},{9,1... | collective-permute-start | bytes 491528 | tf_op jit(solution)/shard_map/ppermute | solution.py:23
  29.4 9.8 %collective-permute-start.9 = (bf16[40,3584]{1,0:T(8,128)(2,1)S(1)}, bf16[40,3584]{1,0:T(8,128)(2,1)S(1)}, u32[]{:S(2)}, u32[]{:S(2)}) collective-permute-start(bf16[40,3584]{1,0:T(8,128)(2,1)S(1)} %shard_map.105.refs_0_), channel_id=1, source_target_pairs={{0,4},{4,0},{8,12},{12,8},{1,5},{5,1},{9,13},{13,9},{2,6},{6,2},{1... | collective-permute-start | bytes 860168 | tf_op jit(solution)/shard_map/ppermute | solution.py:23
  31.1 9.4 %collective-permute-start.8 = (bf16[40,3584]{1,0:T(8,128)(2,1)S(1)}, bf16[40,3584]{1,0:T(8,128)(2,1)S(1)}, u32[]{:S(2)}, u32[]{:S(2)}) collective-permute-start(bf16[40,3584]{1,0:T(8,128)(2,1)S(1)} %shard_map.110), channel_id=1, source_target_pairs={{0,2},{2,0},{1,3},{3,1},{4,6},{6,4},{5,7},{7,5},{8,10},{10,8},{9,1... | collective-permute-start | bytes 860168 | tf_op jit(solution)/shard_map/ppermute | solution.py:23
  36.0 15.1 %collective-permute-start.12 = (bf16[2,40,1792]{2,1,0:T(8,128)(2,1)S(1)}, bf16[2,40,1792]{2,1,0:T(8,128)(2,1)S(1)}, u32[]{:S(2)}, u32[]{:S(2)}) collective-permute-start(bf16[2,40,1792]{2,1,0:T(8,128)(2,1)S(1)} %slice_bitcast_fusion), channel_id=1, source_target_pairs={{0,8},{4,12},{8,0},{12,4},{1,9},{5,13},{9,1},{13,5},{2,10},{6,14},... | collective-permute-start | bytes 860168 | tf_op jit(solution)/shard_map/ppermute | solution.py:23
  44.5 7.4 %collective-permute-start.11 = (bf16[160,512]{1,0:T(8,128)(2,1)S(1)}, bf16[160,512]{1,0:T(8,128)(2,1)S(1)}, u32[]{:S(2)}, u32[]{:S(2)}) collective-permute-start(bf16[160,512]{1,0:T(8,128)(2,1)S(1)} %pad_maximum_fusion.3), channel_id=1, source_target_pairs={{0,2},{2,0},{1,3},{3,1},{4,6},{6,4},{5,7},{7,5},{8,10},{10,8},{9,1... | collective-permute-start | bytes 491528 | tf_op jit(solution)/shard_map/ppermute | solution.py:23
  51.2 14.4 %collective-permute-start.15 = (bf16[2,40,1792]{2,1,0:T(8,128)(2,1)S(1)}, bf16[2,40,1792]{2,1,0:T(8,128)(2,1)S(1)}, u32[]{:S(2)}, u32[]{:S(2)}) collective-permute-start(bf16[2,40,1792]{2,1,0:T(8,128)(2,1)S(1)} %pad_maximum_fusion.1), channel_id=1, source_target_pairs={{0,2},{2,0},{1,3},{3,1},{4,6},{6,4},{5,7},{7,5},{8,10},{10,8},{9,1... | collective-permute-start | bytes 860168 | tf_op jit(solution)/shard_map/ppermute | solution.py:23
  52.7 7.8 %collective-permute-start.13 = (bf16[40,1792]{1,0:T(8,128)(2,1)S(1)}, bf16[40,1792]{1,0:T(8,128)(2,1)S(1)}, u32[]{:S(2)}, u32[]{:S(2)}) collective-permute-start(bf16[40,1792]{1,0:T(8,128)(2,1)S(1)} %get-tuple-element.42), channel_id=1, source_target_pairs={{0,12},{4,8},{8,4},{12,0},{1,13},{5,9},{9,5},{13,1},{2,14},{6,10},... | collective-permute-start | bytes 430088 | tf_op jit(solution)/shard_map/ppermute | solution.py:23
  56.2 9.4 %collective-permute-start.14 = (bf16[40,1792]{1,0:T(8,128)(2,1)S(1)}, bf16[40,1792]{1,0:T(8,128)(2,1)S(1)}, u32[]{:S(2)}, u32[]{:S(2)}) collective-permute-start(bf16[40,1792]{1,0:T(8,128)(2,1)S(1)} %get-tuple-element.41), channel_id=1, source_target_pairs={{0,14},{2,12},{4,10},{6,8},{8,6},{10,4},{12,2},{14,0},{1,15},{3,13... | collective-permute-start | bytes 430088 | tf_op jit(solution)/shard_map/ppermute | solution.py:39
  57.5 9.1 %collective-permute-start.16 = (bf16[40,1792]{1,0:T(8,128)(2,1)S(1)}, bf16[40,1792]{1,0:T(8,128)(2,1)S(1)}, u32[]{:S(2)}, u32[]{:S(2)}) collective-permute-start(bf16[40,1792]{1,0:T(8,128)(2,1)S(1)} %get-tuple-element.40), channel_id=1, source_target_pairs={{0,4},{4,0},{8,12},{12,8},{1,5},{5,1},{9,13},{13,9},{2,6},{6,2},{1... | collective-permute-start | bytes 430088 | tf_op jit(solution)/shard_map/ppermute | solution.py:23
  58.0 11.9 %collective-permute-start.17 = (bf16[40,1792]{1,0:T(8,128)(2,1)S(1)}, bf16[40,1792]{1,0:T(8,128)(2,1)S(1)}, u32[]{:S(2)}, u32[]{:S(2)}) collective-permute-start(bf16[40,1792]{1,0:T(8,128)(2,1)S(1)} %get-tuple-element.39), channel_id=1, source_target_pairs={{0,6},{2,4},{4,2},{6,0},{8,14},{10,12},{12,10},{14,8},{1,7},{3,5},... | collective-permute-start | bytes 430088 | tf_op jit(solution)/shard_map/ppermute | solution.py:39

commit v6 on v5

--- a/solution.py
+++ b/solution.py
@@ -316,7 +316,10 @@
         node_me = lax.axis_index("node")
         for j in range(nodes):
             mine = [(k, rest.pop(0)[...]) for k, _ in pieces[j]]
-            value = (sum_refs[j][...] + weighted_sum(given_ref, mine)).astype(bf16)
+            value = sum_refs[j][...]
+            if mine:
+                value = value + weighted_sum(given_ref, mine)
+            value = value.astype(bf16)
             for at in range(nodes):
 
                 @pl.when(node_me ^ j == at)
@@ -422,10 +425,11 @@
     count = len(far)
     pieces = [[([k], rows) for k, rows in part[:count]] for part in late]
     pieces[0] += [([k], part[0]) for k, part in zip(early_chunk, back)]
+    pieces[0] += [([k], rows) for k, rows in late[0][count:]]
     for part, rows in zip(pieces[1:], across):
         part.append((early_chunk, rows))
     given, sums = combine_early(info, pieces, cap)
-    return combine_late(given, sums, [part[count:] for part in late])
+    return combine_late(given, sums, [[]] + [part[count:] for part in late[1:]])
 
 
 def solution(mesh):

time: 71.3 us -> 70 us (0.982)
    ppermute x2, waiting for transfers between devices: 8.42 us -> 1.7 us  [send(): return lax.ppermute(value, ('ep', 'node'), pairs)]
    ppermute x16, waiting for transfers between devices: 13.3 us -> 19.4 us  [swap(): lax.ppermute(value, axis, [(i, partner(i, step)) for i in range(count)])]
  transfers between devices with their start and end apart: 18 -> 18, of which waited for: 9 -> 10; matrix products, arithmetic and copies ran while one was open for 0% -> 1% of each run, Pallas kernels for 16% -> 16%
where the time goes in v6:
time: 70 us; the launch traced here: 69.8 us
  starting transfers between devices  28 us (40%)
  waiting for transfers between devices  21.1 us (30%)
  Pallas kernels  13.9 us (20%)
  blocking collectives  6.32 us (9%)
    ppermute x16, starting transfers between devices, swap(): lax.ppermute(value, axis, [(i, partner(i, step)) for i in range(count)])  25.5 us
    ppermute x16, waiting for transfers between devices, swap(): lax.ppermute(value, axis, [(i, partner(i, step)) for i in range(count)])  19.4 us
    pallas_call x1, Pallas kernels, load_and_route(): call(kernel, shapes, specs, scratch)  4.74 us
    all_gather x2, blocking collectives, gate_up(): return activate(own, lax.all_gather(sent, 'sub'))  4.55 us
    pallas_call x2, Pallas kernels, dots(): return call(kernel, shapes, specs)(rows, *weights, *behind)  2.73 us
    ppermute x2, starting transfers between devices, send(): return lax.ppermute(value, ('ep', 'node'), pairs)  2.41 us
    all_gather x1, blocking collectives, body(): logits = lax.all_gather(hold([logits], firsts[:1])[0], 'sub')  1.77 us
    ppermute x2, waiting for transfers between devices, send(): return lax.ppermute(value, ('ep', 'node'), pairs)  1.7 us
  transfers between devices with their start and end apart: 18, of which 10 were waited for; matrix products, arithmetic and copies ran while one was open for 1% of the time, Pallas kernels for 16%

profile of v6, /device:TPU:0, one launch (start us, length us, event | category | flops | bytes accessed | tf_op | source)
XLA Modules:
  0.0 69.8 jit_solution(17648866968968900677)
XLA Ops:
  0.0 1.6 %shard_map.100 = (f32[4,64]{1,0:T(4,128)S(1)}, bf16[40,1792]{1,0:T(8,128)(2,1)S(1)}, bf16[40,1792]{1,0:T(8,128)(2,1)S(1)}, bf16[40,3584]{1,0:T(8,128)(2,1)S(1)},...) custom-call(s32[1,4]{1,0:T(1,128)} %bitcast.44, s32[2,64]{1,0:T(2,128)} %bitcast.42, bf16[64,3584]{1,0:T(8,128)(2,1)} %refs_3_.1), custom_call_target="tpu_custom_call" | custom-call | tf_op jit(solution)/shard_map/pallas_call | solution.py:124
  1.6 3.0 %collective-permute-start.1 = (bf16[40,3584]{1,0:T(8,128)(2,1)S(1)}, bf16[40,3584]{1,0:T(8,128)(2,1)S(1)}, u32[]{:S(2)}, u32[]{:S(2)}) collective-permute-start(bf16[40,3584]{1,0:T(8,128)(2,1)S(1)} %get-tuple-element.22.refs_8_), channel_id=1, source_target_pairs={{0,2},{2,0},{1,3},{3,1},{4,6},{6,4},{5,7},{7,5},{8,10},{10,8},{9,1... | collective-permute-start | bytes 860168 | tf_op jit(solution)/shard_map/ppermute | solution.py:23
  4.6 2.6 %collective-permute-start = (bf16[40,1792]{1,0:T(8,128)(2,1)S(1)}, bf16[40,1792]{1,0:T(8,128)(2,1)S(1)}, u32[]{:S(2)}, u32[]{:S(2)}) collective-permute-start(bf16[40,1792]{1,0:T(8,128)(2,1)S(1)} %get-tuple-element.24), channel_id=1, source_target_pairs={{0,8},{4,12},{8,0},{12,4},{1,9},{5,13},{9,1},{13,5},{2,10},{6,14},... | collective-permute-start | bytes 430088 | tf_op jit(solution)/shard_map/ppermute | solution.py:23
  7.2 1.6 %collective-permute-start.3 = (bf16[40,3584]{1,0:T(8,128)(2,1)S(1)}, bf16[40,3584]{1,0:T(8,128)(2,1)S(1)}, u32[]{:S(2)}, u32[]{:S(2)}) collective-permute-start(bf16[40,3584]{1,0:T(8,128)(2,1)S(1)} %get-tuple-element.27), channel_id=1, source_target_pairs={{0,4},{4,0},{8,12},{12,8},{1,5},{5,1},{9,13},{13,9},{2,6},{6,2},{1... | collective-permute-start | bytes 860168 | tf_op jit(solution)/shard_map/ppermute | solution.py:23
  8.8 0.5 collective-permute-start.4
  9.3 0.3 collective-permute-start.2
  9.6 4.7 %shard_map.101 = (bf16[3584,512]{1,0:T(8,128)(2,1)S(1)}, bf16[3584,512]{1,0:T(8,128)(2,1)S(1)}, bf16[1024,1792]{1,0:T(8,128)(2,1)S(1)}, f32[4,64]{1,0:T(4,128)S(1)}) custom-call(bf16[3584,512]{1,0:T(8,128)(2,1)} %bitcast.38, bf16[3584,512]{1,0:T(8,128)(2,1)} %bitcast.39, bf16[1024,1792]{1,0:T(8,128)(2,1)} %bitcast.40, bf16[64,3584]{1,0:T(8,128)(2,1)} %refs_3_.1, ...), custom_call_target="tpu_custom_call" | custom-call | tf_op jit(solution)/shard_map/pallas_call | solution.py:192
  14.4 0.7 collective-permute-done.refs_1_
  15.0 0.9 %collective-permute-start.5 = (bf16[40,1792]{1,0:T(8,128)(2,1)S(1)}, bf16[40,1792]{1,0:T(8,128)(2,1)S(1)}, u32[]{:S(2)}, u32[]{:S(2)}) collective-permute-start(bf16[40,1792]{1,0:T(8,128)(2,1)S(1)} %shard_map.102.refs_0_), channel_id=1, source_target_pairs={{0,2},{2,0},{1,3},{3,1},{4,6},{6,4},{5,7},{7,5},{8,10},{10,8},{9,1... | collective-permute-start | bytes 430088 | tf_op jit(solution)/shard_map/ppermute | solution.py:23
  16.0 1.8 %all-gather.3.refs_0_.parts_ref = f32[2,4,64]{2,1,0:T(4,128)S(1)} all-gather(f32[1,4,64]{2,1,0:T(4,128)S(1)} %bitcast.37), channel_id=2, replica_groups=mesh['rep'=2,'ep'=4,'node'=2,'sub'=2] {'sub'}, dimensions={0}, use_global_device_ids=true | all-gather | bytes 3072 | tf_op jit(solution)/shard_map/all_gather | solution.py:377
  17.7 1.4 %collective-permute-done.2.refs_2_ = bf16[40,1792]{1,0:T(8,128)(2,1)S(1)} collective-permute-done((bf16[40,1792]{1,0:T(8,128)(2,1)S(1)}, bf16[40,1792]{1,0:T(8,128)(2,1)S(1)}, u32[]{:S(2)}, u32[]{:S(2)}) %collective-permute-start.2) | collective-permute-done | bytes 143392 | tf_op jit(solution)/shard_map/ppermute | solution.py:23
  19.1 0.0 collective-permute-done.1.refs_1_
  19.1 0.5 collective-permute-start.6
  19.7 2.7 %collective-permute-start.7 = (bf16[40,3584]{1,0:T(8,128)(2,1)S(1)}, bf16[40,3584]{1,0:T(8,128)(2,1)S(1)}, u32[]{:S(2)}, u32[]{:S(2)}) collective-permute-start(bf16[40,3584]{1,0:T(8,128)(2,1)S(1)} %shard_map.109), channel_id=1, source_target_pairs={{0,12},{4,8},{8,4},{12,0},{1,13},{5,9},{9,5},{13,1},{2,14},{6,10},... | collective-permute-start | bytes 860168 | tf_op jit(solution)/shard_map/ppermute | solution.py:23
  22.4 0.0 collective-permute-done.3.refs_1_
  22.4 0.0 collective-permute-done.4.refs_2_
  22.4 1.0 %shard_map.106.refs_2_.info_ref = f32[2,64,4]{2,1,0:T(8,128)S(1)} custom-call(f32[2,4,64]{2,1,0:T(4,128)S(1)} %all-gather.3.refs_0_.parts_ref, f32[4,64]{1,0:T(4,128)S(1)} %get-tuple-element.25.place_ref, s32[1,4]{1,0:T(1,128)} %bitcast.45, s32[2,64]{1,0:T(2,128)} %bitcast.43, bf16[40,3584]{1,0:T(8,128)(2,1)S(1)} %shard_map.105.refs_0_), custom_call_target="tpu_custom_call" | custom-call | tf_op jit(solution)/shard_map/pallas_call | solution.py:224
  23.5 0.0 collective-permute-done.5
  23.5 0.8 %collective-permute-done.6 = bf16[40,1792]{1,0:T(8,128)(2,1)S(1)} collective-permute-done((bf16[40,1792]{1,0:T(8,128)(2,1)S(1)}, bf16[40,1792]{1,0:T(8,128)(2,1)S(1)}, u32[]{:S(2)}, u32[]{:S(2)}) %collective-permute-start.6) | collective-permute-done | bytes 143392 | tf_op jit(solution)/shard_map/ppermute | solution.py:23
  24.2 0.1 maximum_maximum_fusion.rows_ref
  24.3 1.4 %shard_map.107 = (f32[160,1024]{1,0:T(8,128)S(1)}, bf16[160,1024]{1,0:T(8,128)(2,1)S(1)}) custom-call(bf16[160,3584]{1,0:T(8,128)(2,1)S(1)} %maximum_maximum_fusion.rows_ref, bf16[3584,512]{1,0:T(8,128)(2,1)S(1)} %get-tuple-element.28.refs_0_, bf16[3584,512]{1,0:T(8,128)(2,1)S(1)} %get-tuple-element.29.refs_1_, f32[2,64,4]{2,1,0:T(8,128)S(1)} %shard_map.106.refs_2_.info_ref), custom_call_target="tpu_custom_call" | custom-call | tf_op jit(solution)/shard_map/pallas_call | solution.py:252
  25.7 2.3 %all-gather.1 = bf16[320,1024]{1,0:T(8,128)(2,1)S(1)} all-gather(bf16[160,1024]{1,0:T(8,128)(2,1)S(1)} %get-tuple-element.31), channel_id=3, replica_groups=mesh['rep'=2,'ep'=4,'node'=2,'sub'=2] {'sub'}, dimensions={0}, use_global_device_ids=true | all-gather | bytes 983040 | tf_op jit(solution)/shard_map/all_gather | solution.py:399
  28.0 0.1 shard_map.108.refs_0_
  28.1 1.3 %collective-permute-start.10 = (bf16[160,512]{1,0:T(8,128)(2,1)S(1)}, bf16[160,512]{1,0:T(8,128)(2,1)S(1)}, u32[]{:S(2)}, u32[]{:S(2)}) collective-permute-start(bf16[160,512]{1,0:T(8,128)(2,1)S(1)} %pad_maximum_fusion.2), channel_id=1, source_target_pairs={{0,2},{2,0},{1,3},{3,1},{4,6},{6,4},{5,7},{7,5},{8,10},{10,8},{9,1... | collective-permute-start | bytes 491528 | tf_op jit(solution)/shard_map/ppermute | solution.py:23
  29.4 1.7 %collective-permute-start.9 = (bf16[40,3584]{1,0:T(8,128)(2,1)S(1)}, bf16[40,3584]{1,0:T(8,128)(2,1)S(1)}, u32[]{:S(2)}, u32[]{:S(2)}) collective-permute-start(bf16[40,3584]{1,0:T(8,128)(2,1)S(1)} %shard_map.105.refs_0_), channel_id=1, source_target_pairs={{0,4},{4,0},{8,12},{12,8},{1,5},{5,1},{9,13},{13,9},{2,6},{6,2},{1... | collective-permute-start | bytes 860168 | tf_op jit(solution)/shard_map/ppermute | solution.py:23
  31.1 0.0 collective-permute-done.7.refs_1_
  31.1 1.5 %collective-permute-start.8 = (bf16[40,3584]{1,0:T(8,128)(2,1)S(1)}, bf16[40,3584]{1,0:T(8,128)(2,1)S(1)}, u32[]{:S(2)}, u32[]{:S(2)}) collective-permute-start(bf16[40,3584]{1,0:T(8,128)(2,1)S(1)} %shard_map.110), channel_id=1, source_target_pairs={{0,2},{2,0},{1,3},{3,1},{4,6},{6,4},{5,7},{7,5},{8,10},{10,8},{9,1... | collective-permute-start | bytes 860168 | tf_op jit(solution)/shard_map/ppermute | solution.py:23
  32.6 2.6 %collective-permute-done.10.refs_1_ = bf16[160,512]{1,0:T(8,128)(2,1)S(1)} collective-permute-done((bf16[160,512]{1,0:T(8,128)(2,1)S(1)}, bf16[160,512]{1,0:T(8,128)(2,1)S(1)}, u32[]{:S(2)}, u32[]{:S(2)}) %collective-permute-start.10) | collective-permute-done | bytes 163872 | tf_op jit(solution)/shard_map/ppermute | solution.py:23
  35.2 0.8 %shard_map.111 = bf16[160,1792]{1,0:T(8,128)(2,1)S(1)} custom-call(bf16[160,512]{1,0:T(8,128)(2,1)S(1)} %shard_map.108.refs_0_, bf16[160,512]{1,0:T(8,128)(2,1)S(1)} %collective-permute-done.10.refs_1_, bf16[1024,1792]{1,0:T(8,128)(2,1)S(1)} %get-tuple-element.33.refs_2_), custom_call_target="tpu_custom_call" | custom-call | tf_op jit(solution)/shard_map/pallas_call | solution.py:272
  36.0 3.2 %collective-permute-start.12 = (bf16[2,40,1792]{2,1,0:T(8,128)(2,1)S(1)}, bf16[2,40,1792]{2,1,0:T(8,128)(2,1)S(1)}, u32[]{:S(2)}, u32[]{:S(2)}) collective-permute-start(bf16[2,40,1792]{2,1,0:T(8,128)(2,1)S(1)} %slice_bitcast_fusion), channel_id=1, source_target_pairs={{0,8},{4,12},{8,0},{12,4},{1,9},{5,13},{9,1},{13,5},{2,10},{6,14},... | collective-permute-start | bytes 860168 | tf_op jit(solution)/shard_map/ppermute | solution.py:23
  39.2 1.3 %collective-permute-done.8 = bf16[40,3584]{1,0:T(8,128)(2,1)S(1)} collective-permute-done((bf16[40,3584]{1,0:T(8,128)(2,1)S(1)}, bf16[40,3584]{1,0:T(8,128)(2,1)S(1)}, u32[]{:S(2)}, u32[]{:S(2)}) %collective-permute-start.8) | collective-permute-done | bytes 286752 | tf_op jit(solution)/shard_map/ppermute | solution.py:23
  40.6 0.1 pad_maximum_fusion.rows_ref
  40.7 1.4 %shard_map.112 = (f32[160,1024]{1,0:T(8,128)S(1)}, bf16[160,1024]{1,0:T(8,128)(2,1)S(1)}) custom-call(bf16[160,3584]{1,0:T(8,128)(2,1)S(1)} %pad_maximum_fusion.rows_ref, bf16[3584,512]{1,0:T(8,128)(2,1)S(1)} %get-tuple-element.28.refs_0_, bf16[3584,512]{1,0:T(8,128)(2,1)S(1)} %get-tuple-element.29.refs_1_, bf16[2,2,40,1792]{3,2,1,0:T(8,128)(2,1)S(1)} %bitcast.33), custom_call_target="tpu_custom_call" | custom-call | tf_op jit(solution)/shard_map/pallas_call | solution.py:252
  42.0 2.3 %all-gather.2 = bf16[320,1024]{1,0:T(8,128)(2,1)S(1)} all-gather(bf16[160,1024]{1,0:T(8,128)(2,1)S(1)} %get-tuple-element.35), channel_id=4, replica_groups=mesh['rep'=2,'ep'=4,'node'=2,'sub'=2] {'sub'}, dimensions={0}, use_global_device_ids=true | all-gather | bytes 983040 | tf_op jit(solution)/shard_map/all_gather | solution.py:399
  44.3 0.1 shard_map.113.refs_0_
  44.5 1.3 %collective-permute-start.11 = (bf16[160,512]{1,0:T(8,128)(2,1)S(1)}, bf16[160,512]{1,0:T(8,128)(2,1)S(1)}, u32[]{:S(2)}, u32[]{:S(2)}) collective-permute-start(bf16[160,512]{1,0:T(8,128)(2,1)S(1)} %pad_maximum_fusion.3), channel_id=1, source_target_pairs={{0,2},{2,0},{1,3},{3,1},{4,6},{6,4},{5,7},{7,5},{8,10},{10,8},{9,1... | collective-permute-start | bytes 491528 | tf_op jit(solution)/shard_map/ppermute | solution.py:23
  45.7 5.4 %collective-permute-done.12.refs_3_ = bf16[2,40,1792]{2,1,0:T(8,128)(2,1)S(1)} collective-permute-done((bf16[2,40,1792]{2,1,0:T(8,128)(2,1)S(1)}, bf16[2,40,1792]{2,1,0:T(8,128)(2,1)S(1)}, u32[]{:S(2)}, u32[]{:S(2)}) %collective-permute-start.12) | collective-permute-done | bytes 286752 | tf_op jit(solution)/shard_map/ppermute | solution.py:23
  51.2 0.6 collective-permute-start.16
  51.8 0.8 %shard_map.114 = bf16[160,1792]{1,0:T(8,128)(2,1)S(1)} custom-call(bf16[160,512]{1,0:T(8,128)(2,1)S(1)} %shard_map.113.refs_0_, bf16[160,512]{1,0:T(8,128)(2,1)S(1)} %collective-permute-done.11.refs_1_, bf16[1024,1792]{1,0:T(8,128)(2,1)S(1)} %get-tuple-element.33.refs_2_, bf16[2,40,1792]{2,1,0:T(8,128)(2,1)S(1)} %collective-permute-done.12.refs_3_), custom_call_target="tpu_custom_call" | custom-call | tf_op jit(solution)/shard_map/pallas_call | solution.py:272
  52.7 3.6 %collective-permute-start.13 = (bf16[40,1792]{1,0:T(8,128)(2,1)S(1)}, bf16[40,1792]{1,0:T(8,128)(2,1)S(1)}, u32[]{:S(2)}, u32[]{:S(2)}) collective-permute-start(bf16[40,1792]{1,0:T(8,128)(2,1)S(1)} %get-tuple-element.42), channel_id=1, source_target_pairs={{0,12},{4,8},{8,4},{12,0},{1,13},{5,9},{9,5},{13,1},{2,14},{6,10},... | collective-permute-start | bytes 430088 | tf_op jit(solution)/shard_map/ppermute | solution.py:23
  56.2 0.2 collective-permute-start.14
  56.4 2.4 %collective-permute-start.15 = (bf16[40,1792]{1,0:T(8,128)(2,1)S(1)}, bf16[40,1792]{1,0:T(8,128)(2,1)S(1)}, u32[]{:S(2)}, u32[]{:S(2)}) collective-permute-start(bf16[40,1792]{1,0:T(8,128)(2,1)S(1)} %get-tuple-element.40), channel_id=1, source_target_pairs={{0,14},{2,12},{4,10},{6,8},{8,6},{10,4},{12,2},{14,0},{1,15},{3,13... | collective-permute-start | bytes 430088 | tf_op jit(solution)/shard_map/ppermute | solution.py:39
  58.9 2.4 %collective-permute-done.13.refs_0_ = bf16[40,1792]{1,0:T(8,128)(2,1)S(1)} collective-permute-done((bf16[40,1792]{1,0:T(8,128)(2,1)S(1)}, bf16[40,1792]{1,0:T(8,128)(2,1)S(1)}, u32[]{:S(2)}, u32[]{:S(2)}) %collective-permute-start.13) | collective-permute-done | bytes 143392 | tf_op jit(solution)/shard_map/ppermute | solution.py:23
  61.2 4.8 %collective-permute-done.14.refs_3_ = bf16[40,1792]{1,0:T(8,128)(2,1)S(1)} collective-permute-done((bf16[40,1792]{1,0:T(8,128)(2,1)S(1)}, bf16[40,1792]{1,0:T(8,128)(2,1)S(1)}, u32[]{:S(2)}, u32[]{:S(2)}) %collective-permute-start.14) | collective-permute-done | bytes 143392 | tf_op jit(solution)/shard_map/ppermute | solution.py:23
  66.0 1.5 %collective-permute-done.15.refs_4_ = bf16[40,1792]{1,0:T(8,128)(2,1)S(1)} collective-permute-done((bf16[40,1792]{1,0:T(8,128)(2,1)S(1)}, bf16[40,1792]{1,0:T(8,128)(2,1)S(1)}, u32[]{:S(2)}, u32[]{:S(2)}) %collective-permute-start.15) | collective-permute-done | bytes 143392 | tf_op jit(solution)/shard_map/ppermute | solution.py:39
  67.5 1.1 %shard_map.115 = (bf16[4,64,40]{2,1,0:T(8,128)(2,1)S(1)}, f32[64,1792]{1,0:T(8,128)S(1)}, f32[64,1792]{1,0:T(8,128)S(1)}) custom-call(f32[2,64,4]{2,1,0:T(8,128)S(1)} %shard_map.106.refs_2_.info_ref, bf16[40,1792]{1,0:T(8,128)(2,1)S(1)} %collective-permute-done.13.refs_0_, bf16[40,1792]{1,0:T(8,128)(2,1)S(1)} %get-tuple-element.44.refs_1_, ...), custom_call_target="tpu_custom_call" | custom-call | tf_op jit(solution)/shard_map/pallas_call | solution.py:305
  68.6 0.2 collective-permute-done.17.refs_2_
  68.8 1.0 %shard_map.116 = bf16[64,3584]{1,0:T(8,128)(2,1)} custom-call(bf16[4,64,40]{2,1,0:T(8,128)(2,1)S(1)} %get-tuple-element.36.given_ref, f32[64,1792]{1,0:T(8,128)S(1)} %get-tuple-element.37.refs_0_, f32[64,1792]{1,0:T(8,128)S(1)} %get-tuple-element.38.refs_1_, bf16[40,1792]{1,0:T(8,128)(2,1)S(1)} %collective-permute-done.17.refs_2_), custom_call_target="tpu_custom_call" | custom-call | tf_op jit(solution)/shard_map/pallas_call | solution.py:330
  (19 shorter events, 0.2 us)
Async XLA Ops:
  1.6 17.6 %collective-permute-start.1 = (bf16[40,3584]{1,0:T(8,128)(2,1)S(1)}, bf16[40,3584]{1,0:T(8,128)(2,1)S(1)}, u32[]{:S(2)}, u32[]{:S(2)}) collective-permute-start(bf16[40,3584]{1,0:T(8,128)(2,1)S(1)} %get-tuple-element.22.refs_8_), channel_id=1, source_target_pairs={{0,2},{2,0},{1,3},{3,1},{4,6},{6,4},{5,7},{7,5},{8,10},{10,8},{9,1... | collective-permute-start | bytes 860168 | tf_op jit(solution)/shard_map/ppermute | solution.py:23
  4.6 10.5 %collective-permute-start = (bf16[40,1792]{1,0:T(8,128)(2,1)S(1)}, bf16[40,1792]{1,0:T(8,128)(2,1)S(1)}, u32[]{:S(2)}, u32[]{:S(2)}) collective-permute-start(bf16[40,1792]{1,0:T(8,128)(2,1)S(1)} %get-tuple-element.24), channel_id=1, source_target_pairs={{0,8},{4,12},{8,0},{12,4},{1,9},{5,13},{9,1},{13,5},{2,10},{6,14},... | collective-permute-start | bytes 430088 | tf_op jit(solution)/shard_map/ppermute | solution.py:23
  7.2 15.2 %collective-permute-start.3 = (bf16[40,3584]{1,0:T(8,128)(2,1)S(1)}, bf16[40,3584]{1,0:T(8,128)(2,1)S(1)}, u32[]{:S(2)}, u32[]{:S(2)}) collective-permute-start(bf16[40,3584]{1,0:T(8,128)(2,1)S(1)} %get-tuple-element.27), channel_id=1, source_target_pairs={{0,4},{4,0},{8,12},{12,8},{1,5},{5,1},{9,13},{13,9},{2,6},{6,2},{1... | collective-permute-start | bytes 860168 | tf_op jit(solution)/shard_map/ppermute | solution.py:23
  8.8 13.7 %collective-permute-start.4 = (bf16[40,3584]{1,0:T(8,128)(2,1)S(1)}, bf16[40,3584]{1,0:T(8,128)(2,1)S(1)}, u32[]{:S(2)}, u32[]{:S(2)}) collective-permute-start(bf16[40,3584]{1,0:T(8,128)(2,1)S(1)} %get-tuple-element.27), channel_id=1, source_target_pairs={{0,2},{2,0},{1,3},{3,1},{4,6},{6,4},{5,7},{7,5},{8,10},{10,8},{9,1... | collective-permute-start | bytes 860168 | tf_op jit(solution)/shard_map/ppermute | solution.py:23
  9.3 9.8 %collective-permute-start.2 = (bf16[40,1792]{1,0:T(8,128)(2,1)S(1)}, bf16[40,1792]{1,0:T(8,128)(2,1)S(1)}, u32[]{:S(2)}, u32[]{:S(2)}) collective-permute-start(bf16[40,1792]{1,0:T(8,128)(2,1)S(1)} %get-tuple-element.26), channel_id=1, source_target_pairs={{0,8},{4,12},{8,0},{12,4},{1,9},{5,13},{9,1},{13,5},{2,10},{6,14},... | collective-permute-start | bytes 430088 | tf_op jit(solution)/shard_map/ppermute | solution.py:23
  15.0 8.4 %collective-permute-start.5 = (bf16[40,1792]{1,0:T(8,128)(2,1)S(1)}, bf16[40,1792]{1,0:T(8,128)(2,1)S(1)}, u32[]{:S(2)}, u32[]{:S(2)}) collective-permute-start(bf16[40,1792]{1,0:T(8,128)(2,1)S(1)} %shard_map.102.refs_0_), channel_id=1, source_target_pairs={{0,2},{2,0},{1,3},{3,1},{4,6},{6,4},{5,7},{7,5},{8,10},{10,8},{9,1... | collective-permute-start | bytes 430088 | tf_op jit(solution)/shard_map/ppermute | solution.py:23
  19.1 5.1 %collective-permute-start.6 = (bf16[40,1792]{1,0:T(8,128)(2,1)S(1)}, bf16[40,1792]{1,0:T(8,128)(2,1)S(1)}, u32[]{:S(2)}, u32[]{:S(2)}) collective-permute-start(bf16[40,1792]{1,0:T(8,128)(2,1)S(1)} %shard_map.104.refs_0_), channel_id=1, source_target_pairs={{0,2},{2,0},{1,3},{3,1},{4,6},{6,4},{5,7},{7,5},{8,10},{10,8},{9,1... | collective-permute-start | bytes 430088 | tf_op jit(solution)/shard_map/ppermute | solution.py:23
  19.7 11.5 %collective-permute-start.7 = (bf16[40,3584]{1,0:T(8,128)(2,1)S(1)}, bf16[40,3584]{1,0:T(8,128)(2,1)S(1)}, u32[]{:S(2)}, u32[]{:S(2)}) collective-permute-start(bf16[40,3584]{1,0:T(8,128)(2,1)S(1)} %shard_map.109), channel_id=1, source_target_pairs={{0,12},{4,8},{8,4},{12,0},{1,13},{5,9},{9,5},{13,1},{2,14},{6,10},... | collective-permute-start | bytes 860168 | tf_op jit(solution)/shard_map/ppermute | solution.py:23
  28.1 7.1 %collective-permute-start.10 = (bf16[160,512]{1,0:T(8,128)(2,1)S(1)}, bf16[160,512]{1,0:T(8,128)(2,1)S(1)}, u32[]{:S(2)}, u32[]{:S(2)}) collective-permute-start(bf16[160,512]{1,0:T(8,128)(2,1)S(1)} %pad_maximum_fusion.2), channel_id=1, source_target_pairs={{0,2},{2,0},{1,3},{3,1},{4,6},{6,4},{5,7},{7,5},{8,10},{10,8},{9,1... | collective-permute-start | bytes 491528 | tf_op jit(solution)/shard_map/ppermute | solution.py:23
  29.4 9.8 %collective-permute-start.9 = (bf16[40,3584]{1,0:T(8,128)(2,1)S(1)}, bf16[40,3584]{1,0:T(8,128)(2,1)S(1)}, u32[]{:S(2)}, u32[]{:S(2)}) collective-permute-start(bf16[40,3584]{1,0:T(8,128)(2,1)S(1)} %shard_map.105.refs_0_), channel_id=1, source_target_pairs={{0,4},{4,0},{8,12},{12,8},{1,5},{5,1},{9,13},{13,9},{2,6},{6,2},{1... | collective-permute-start | bytes 860168 | tf_op jit(solution)/shard_map/ppermute | solution.py:23
  31.1 9.4 %collective-permute-start.8 = (bf16[40,3584]{1,0:T(8,128)(2,1)S(1)}, bf16[40,3584]{1,0:T(8,128)(2,1)S(1)}, u32[]{:S(2)}, u32[]{:S(2)}) collective-permute-start(bf16[40,3584]{1,0:T(8,128)(2,1)S(1)} %shard_map.110), channel_id=1, source_target_pairs={{0,2},{2,0},{1,3},{3,1},{4,6},{6,4},{5,7},{7,5},{8,10},{10,8},{9,1... | collective-permute-start | bytes 860168 | tf_op jit(solution)/shard_map/ppermute | solution.py:23
  36.0 15.1 %collective-permute-start.12 = (bf16[2,40,1792]{2,1,0:T(8,128)(2,1)S(1)}, bf16[2,40,1792]{2,1,0:T(8,128)(2,1)S(1)}, u32[]{:S(2)}, u32[]{:S(2)}) collective-permute-start(bf16[2,40,1792]{2,1,0:T(8,128)(2,1)S(1)} %slice_bitcast_fusion), channel_id=1, source_target_pairs={{0,8},{4,12},{8,0},{12,4},{1,9},{5,13},{9,1},{13,5},{2,10},{6,14},... | collective-permute-start | bytes 860168 | tf_op jit(solution)/shard_map/ppermute | solution.py:23
  44.5 7.4 %collective-permute-start.11 = (bf16[160,512]{1,0:T(8,128)(2,1)S(1)}, bf16[160,512]{1,0:T(8,128)(2,1)S(1)}, u32[]{:S(2)}, u32[]{:S(2)}) collective-permute-start(bf16[160,512]{1,0:T(8,128)(2,1)S(1)} %pad_maximum_fusion.3), channel_id=1, source_target_pairs={{0,2},{2,0},{1,3},{3,1},{4,6},{6,4},{5,7},{7,5},{8,10},{10,8},{9,1... | collective-permute-start | bytes 491528 | tf_op jit(solution)/shard_map/ppermute | solution.py:23
  51.2 16.3 %collective-permute-start.16 = (bf16[2,40,1792]{2,1,0:T(8,128)(2,1)S(1)}, bf16[2,40,1792]{2,1,0:T(8,128)(2,1)S(1)}, u32[]{:S(2)}, u32[]{:S(2)}) collective-permute-start(bf16[2,40,1792]{2,1,0:T(8,128)(2,1)S(1)} %pad_maximum_fusion.1), channel_id=1, source_target_pairs={{0,2},{2,0},{1,3},{3,1},{4,6},{6,4},{5,7},{7,5},{8,10},{10,8},{9,1... | collective-permute-start | bytes 860168 | tf_op jit(solution)/shard_map/ppermute | solution.py:23
  52.7 8.6 %collective-permute-start.13 = (bf16[40,1792]{1,0:T(8,128)(2,1)S(1)}, bf16[40,1792]{1,0:T(8,128)(2,1)S(1)}, u32[]{:S(2)}, u32[]{:S(2)}) collective-permute-start(bf16[40,1792]{1,0:T(8,128)(2,1)S(1)} %get-tuple-element.42), channel_id=1, source_target_pairs={{0,12},{4,8},{8,4},{12,0},{1,13},{5,9},{9,5},{13,1},{2,14},{6,10},... | collective-permute-start | bytes 430088 | tf_op jit(solution)/shard_map/ppermute | solution.py:23
  56.2 9.8 %collective-permute-start.14 = (bf16[40,1792]{1,0:T(8,128)(2,1)S(1)}, bf16[40,1792]{1,0:T(8,128)(2,1)S(1)}, u32[]{:S(2)}, u32[]{:S(2)}) collective-permute-start(bf16[40,1792]{1,0:T(8,128)(2,1)S(1)} %get-tuple-element.41), channel_id=1, source_target_pairs={{0,4},{4,0},{8,12},{12,8},{1,5},{5,1},{9,13},{13,9},{2,6},{6,2},{1... | collective-permute-start | bytes 430088 | tf_op jit(solution)/shard_map/ppermute | solution.py:23
  56.4 11.1 %collective-permute-start.15 = (bf16[40,1792]{1,0:T(8,128)(2,1)S(1)}, bf16[40,1792]{1,0:T(8,128)(2,1)S(1)}, u32[]{:S(2)}, u32[]{:S(2)}) collective-permute-start(bf16[40,1792]{1,0:T(8,128)(2,1)S(1)} %get-tuple-element.40), channel_id=1, source_target_pairs={{0,14},{2,12},{4,10},{6,8},{8,6},{10,4},{12,2},{14,0},{1,15},{3,13... | collective-permute-start | bytes 430088 | tf_op jit(solution)/shard_map/ppermute | solution.py:39
  58.8 10.0 %collective-permute-start.17 = (bf16[40,1792]{1,0:T(8,128)(2,1)S(1)}, bf16[40,1792]{1,0:T(8,128)(2,1)S(1)}, u32[]{:S(2)}, u32[]{:S(2)}) collective-permute-start(bf16[40,1792]{1,0:T(8,128)(2,1)S(1)} %get-tuple-element.39), channel_id=1, source_target_pairs={{0,6},{2,4},{4,2},{6,0},{8,14},{10,12},{12,10},{14,8},{1,7},{3,5},... | collective-permute-start | bytes 430088 | tf_op jit(solution)/shard_map/ppermute | solution.py:39

commit v7 on v6

--- a/solution.py
+++ b/solution.py
@@ -298,7 +298,7 @@
             for ks, rows in part:
                 ref = rest.pop(0)
                 mine += [(k, ref[i] if rows.ndim == 3 else ref[...]) for i, k in enumerate(ks)]
-            out[...] = weighted_sum(given_ref, mine) + weighted_sum(low, mine)
+            out[...] = weighted_sum(given_ref, mine)
 
     shapes = [jax.ShapeDtypeStruct((count, tok_rows, cap), bf16)]
     shapes += [jax.ShapeDtypeStruct((tok_rows, width), f32)] * len(pieces)

time: 70 us -> 70 us (level)
  no operation moved by 1% of the time
where the time goes in v7:
time: 70 us; the launch traced here: 69.8 us
  starting transfers between devices  28 us (40%)
  waiting for transfers between devices  21.6 us (31%)
  Pallas kernels  13.5 us (19%)
  blocking collectives  6.32 us (9%)
    ppermute x16, starting transfers between devices, swap(): lax.ppermute(value, axis, [(i, partner(i, step)) for i in range(count)])  25.5 us
    ppermute x16, waiting for transfers between devices, swap(): lax.ppermute(value, axis, [(i, partner(i, step)) for i in range(count)])  19.4 us
    pallas_call x1, Pallas kernels, load_and_route(): call(kernel, shapes, specs, scratch)  4.74 us
    all_gather x2, blocking collectives, gate_up(): return activate(own, lax.all_gather(sent, 'sub'))  4.55 us
    pallas_call x2, Pallas kernels, dots(): return call(kernel, shapes, specs)(rows, *weights, *behind)  2.73 us
    ppermute x2, starting transfers between devices, send(): return lax.ppermute(value, ('ep', 'node'), pairs)  2.41 us
    ppermute x2, waiting for transfers between devices, send(): return lax.ppermute(value, ('ep', 'node'), pairs)  2.14 us
    all_gather x1, blocking collectives, body(): logits = lax.all_gather(hold([logits], firsts[:1])[0], 'sub')  1.77 us
  transfers between devices with their start and end apart: 18, of which 10 were waited for; matrix products, arithmetic and copies ran while one was open for 1% of the time, Pallas kernels for 16%

profile of v7, /device:TPU:0, one launch (start us, length us, event | category | flops | bytes accessed | tf_op | source)
XLA Modules:
  0.0 69.8 jit_solution(14061324114911142002)
XLA Ops:
  0.0 1.6 %shard_map.100 = (f32[4,64]{1,0:T(4,128)S(1)}, bf16[40,1792]{1,0:T(8,128)(2,1)S(1)}, bf16[40,1792]{1,0:T(8,128)(2,1)S(1)}, bf16[40,3584]{1,0:T(8,128)(2,1)S(1)},...) custom-call(s32[1,4]{1,0:T(1,128)} %bitcast.44, s32[2,64]{1,0:T(2,128)} %bitcast.42, bf16[64,3584]{1,0:T(8,128)(2,1)} %refs_3_.1), custom_call_target="tpu_custom_call" | custom-call | tf_op jit(solution)/shard_map/pallas_call | solution.py:124
  1.6 3.0 %collective-permute-start.1 = (bf16[40,3584]{1,0:T(8,128)(2,1)S(1)}, bf16[40,3584]{1,0:T(8,128)(2,1)S(1)}, u32[]{:S(2)}, u32[]{:S(2)}) collective-permute-start(bf16[40,3584]{1,0:T(8,128)(2,1)S(1)} %get-tuple-element.22.refs_8_), channel_id=1, source_target_pairs={{0,2},{2,0},{1,3},{3,1},{4,6},{6,4},{5,7},{7,5},{8,10},{10,8},{9,1... | collective-permute-start | bytes 860168 | tf_op jit(solution)/shard_map/ppermute | solution.py:23
  4.6 2.6 %collective-permute-start = (bf16[40,1792]{1,0:T(8,128)(2,1)S(1)}, bf16[40,1792]{1,0:T(8,128)(2,1)S(1)}, u32[]{:S(2)}, u32[]{:S(2)}) collective-permute-start(bf16[40,1792]{1,0:T(8,128)(2,1)S(1)} %get-tuple-element.24), channel_id=1, source_target_pairs={{0,8},{4,12},{8,0},{12,4},{1,9},{5,13},{9,1},{13,5},{2,10},{6,14},... | collective-permute-start | bytes 430088 | tf_op jit(solution)/shard_map/ppermute | solution.py:23
  7.2 1.6 %collective-permute-start.3 = (bf16[40,3584]{1,0:T(8,128)(2,1)S(1)}, bf16[40,3584]{1,0:T(8,128)(2,1)S(1)}, u32[]{:S(2)}, u32[]{:S(2)}) collective-permute-start(bf16[40,3584]{1,0:T(8,128)(2,1)S(1)} %get-tuple-element.27), channel_id=1, source_target_pairs={{0,4},{4,0},{8,12},{12,8},{1,5},{5,1},{9,13},{13,9},{2,6},{6,2},{1... | collective-permute-start | bytes 860168 | tf_op jit(solution)/shard_map/ppermute | solution.py:23
  8.8 0.5 collective-permute-start.4
  9.3 0.3 collective-permute-start.2
  9.6 4.7 %shard_map.101 = (bf16[3584,512]{1,0:T(8,128)(2,1)S(1)}, bf16[3584,512]{1,0:T(8,128)(2,1)S(1)}, bf16[1024,1792]{1,0:T(8,128)(2,1)S(1)}, f32[4,64]{1,0:T(4,128)S(1)}) custom-call(bf16[3584,512]{1,0:T(8,128)(2,1)} %bitcast.38, bf16[3584,512]{1,0:T(8,128)(2,1)} %bitcast.39, bf16[1024,1792]{1,0:T(8,128)(2,1)} %bitcast.40, bf16[64,3584]{1,0:T(8,128)(2,1)} %refs_3_.1, ...), custom_call_target="tpu_custom_call" | custom-call | tf_op jit(solution)/shard_map/pallas_call | solution.py:192
  14.4 0.7 collective-permute-done.refs_1_
  15.0 0.9 %collective-permute-start.5 = (bf16[40,1792]{1,0:T(8,128)(2,1)S(1)}, bf16[40,1792]{1,0:T(8,128)(2,1)S(1)}, u32[]{:S(2)}, u32[]{:S(2)}) collective-permute-start(bf16[40,1792]{1,0:T(8,128)(2,1)S(1)} %shard_map.102.refs_0_), channel_id=1, source_target_pairs={{0,2},{2,0},{1,3},{3,1},{4,6},{6,4},{5,7},{7,5},{8,10},{10,8},{9,1... | collective-permute-start | bytes 430088 | tf_op jit(solution)/shard_map/ppermute | solution.py:23
  16.0 1.8 %all-gather.3.refs_0_.parts_ref = f32[2,4,64]{2,1,0:T(4,128)S(1)} all-gather(f32[1,4,64]{2,1,0:T(4,128)S(1)} %bitcast.37), channel_id=2, replica_groups=mesh['rep'=2,'ep'=4,'node'=2,'sub'=2] {'sub'}, dimensions={0}, use_global_device_ids=true | all-gather | bytes 3072 | tf_op jit(solution)/shard_map/all_gather | solution.py:377
  17.7 1.4 %collective-permute-done.2.refs_2_ = bf16[40,1792]{1,0:T(8,128)(2,1)S(1)} collective-permute-done((bf16[40,1792]{1,0:T(8,128)(2,1)S(1)}, bf16[40,1792]{1,0:T(8,128)(2,1)S(1)}, u32[]{:S(2)}, u32[]{:S(2)}) %collective-permute-start.2) | collective-permute-done | bytes 143392 | tf_op jit(solution)/shard_map/ppermute | solution.py:23
  19.1 0.5 collective-permute-start.6
  19.7 2.7 %collective-permute-start.7 = (bf16[40,3584]{1,0:T(8,128)(2,1)S(1)}, bf16[40,3584]{1,0:T(8,128)(2,1)S(1)}, u32[]{:S(2)}, u32[]{:S(2)}) collective-permute-start(bf16[40,3584]{1,0:T(8,128)(2,1)S(1)} %shard_map.109), channel_id=1, source_target_pairs={{0,12},{4,8},{8,4},{12,0},{1,13},{5,9},{9,5},{13,1},{2,14},{6,10},... | collective-permute-start | bytes 860168 | tf_op jit(solution)/shard_map/ppermute | solution.py:23
  22.4 0.0 collective-permute-done.3.refs_1_
  22.4 0.0 collective-permute-done.4.refs_2_
  22.4 1.0 %shard_map.106.refs_2_.info_ref = f32[2,64,4]{2,1,0:T(8,128)S(1)} custom-call(f32[2,4,64]{2,1,0:T(4,128)S(1)} %all-gather.3.refs_0_.parts_ref, f32[4,64]{1,0:T(4,128)S(1)} %get-tuple-element.25.place_ref, s32[1,4]{1,0:T(1,128)} %bitcast.45, s32[2,64]{1,0:T(2,128)} %bitcast.43, bf16[40,3584]{1,0:T(8,128)(2,1)S(1)} %shard_map.105.refs_0_), custom_call_target="tpu_custom_call" | custom-call | tf_op jit(solution)/shard_map/pallas_call | solution.py:224
  23.5 0.0 collective-permute-done.5
  23.5 0.8 %collective-permute-done.6 = bf16[40,1792]{1,0:T(8,128)(2,1)S(1)} collective-permute-done((bf16[40,1792]{1,0:T(8,128)(2,1)S(1)}, bf16[40,1792]{1,0:T(8,128)(2,1)S(1)}, u32[]{:S(2)}, u32[]{:S(2)}) %collective-permute-start.6) | collective-permute-done | bytes 143392 | tf_op jit(solution)/shard_map/ppermute | solution.py:23
  24.2 0.1 maximum_maximum_fusion.rows_ref
  24.3 1.4 %shard_map.107 = (f32[160,1024]{1,0:T(8,128)S(1)}, bf16[160,1024]{1,0:T(8,128)(2,1)S(1)}) custom-call(bf16[160,3584]{1,0:T(8,128)(2,1)S(1)} %maximum_maximum_fusion.rows_ref, bf16[3584,512]{1,0:T(8,128)(2,1)S(1)} %get-tuple-element.28.refs_0_, bf16[3584,512]{1,0:T(8,128)(2,1)S(1)} %get-tuple-element.29.refs_1_, f32[2,64,4]{2,1,0:T(8,128)S(1)} %shard_map.106.refs_2_.info_ref), custom_call_target="tpu_custom_call" | custom-call | tf_op jit(solution)/shard_map/pallas_call | solution.py:252
  25.7 2.3 %all-gather.1 = bf16[320,1024]{1,0:T(8,128)(2,1)S(1)} all-gather(bf16[160,1024]{1,0:T(8,128)(2,1)S(1)} %get-tuple-element.31), channel_id=3, replica_groups=mesh['rep'=2,'ep'=4,'node'=2,'sub'=2] {'sub'}, dimensions={0}, use_global_device_ids=true | all-gather | bytes 983040 | tf_op jit(solution)/shard_map/all_gather | solution.py:399
  28.0 0.1 shard_map.108.refs_0_
  28.1 1.3 %collective-permute-start.10 = (bf16[160,512]{1,0:T(8,128)(2,1)S(1)}, bf16[160,512]{1,0:T(8,128)(2,1)S(1)}, u32[]{:S(2)}, u32[]{:S(2)}) collective-permute-start(bf16[160,512]{1,0:T(8,128)(2,1)S(1)} %pad_maximum_fusion.2), channel_id=1, source_target_pairs={{0,2},{2,0},{1,3},{3,1},{4,6},{6,4},{5,7},{7,5},{8,10},{10,8},{9,1... | collective-permute-start | bytes 491528 | tf_op jit(solution)/shard_map/ppermute | solution.py:23
  29.4 1.7 %collective-permute-start.9 = (bf16[40,3584]{1,0:T(8,128)(2,1)S(1)}, bf16[40,3584]{1,0:T(8,128)(2,1)S(1)}, u32[]{:S(2)}, u32[]{:S(2)}) collective-permute-start(bf16[40,3584]{1,0:T(8,128)(2,1)S(1)} %shard_map.105.refs_0_), channel_id=1, source_target_pairs={{0,4},{4,0},{8,12},{12,8},{1,5},{5,1},{9,13},{13,9},{2,6},{6,2},{1... | collective-permute-start | bytes 860168 | tf_op jit(solution)/shard_map/ppermute | solution.py:23
  31.1 0.0 collective-permute-done.7.refs_1_
  31.1 1.5 %collective-permute-start.8 = (bf16[40,3584]{1,0:T(8,128)(2,1)S(1)}, bf16[40,3584]{1,0:T(8,128)(2,1)S(1)}, u32[]{:S(2)}, u32[]{:S(2)}) collective-permute-start(bf16[40,3584]{1,0:T(8,128)(2,1)S(1)} %shard_map.110), channel_id=1, source_target_pairs={{0,2},{2,0},{1,3},{3,1},{4,6},{6,4},{5,7},{7,5},{8,10},{10,8},{9,1... | collective-permute-start | bytes 860168 | tf_op jit(solution)/shard_map/ppermute | solution.py:23
  32.6 2.6 %collective-permute-done.10.refs_1_ = bf16[160,512]{1,0:T(8,128)(2,1)S(1)} collective-permute-done((bf16[160,512]{1,0:T(8,128)(2,1)S(1)}, bf16[160,512]{1,0:T(8,128)(2,1)S(1)}, u32[]{:S(2)}, u32[]{:S(2)}) %collective-permute-start.10) | collective-permute-done | bytes 163872 | tf_op jit(solution)/shard_map/ppermute | solution.py:23
  35.2 0.8 %shard_map.111 = bf16[160,1792]{1,0:T(8,128)(2,1)S(1)} custom-call(bf16[160,512]{1,0:T(8,128)(2,1)S(1)} %shard_map.108.refs_0_, bf16[160,512]{1,0:T(8,128)(2,1)S(1)} %collective-permute-done.10.refs_1_, bf16[1024,1792]{1,0:T(8,128)(2,1)S(1)} %get-tuple-element.33.refs_2_), custom_call_target="tpu_custom_call" | custom-call | tf_op jit(solution)/shard_map/pallas_call | solution.py:272
  36.0 3.2 %collective-permute-start.12 = (bf16[2,40,1792]{2,1,0:T(8,128)(2,1)S(1)}, bf16[2,40,1792]{2,1,0:T(8,128)(2,1)S(1)}, u32[]{:S(2)}, u32[]{:S(2)}) collective-permute-start(bf16[2,40,1792]{2,1,0:T(8,128)(2,1)S(1)} %slice_bitcast_fusion), channel_id=1, source_target_pairs={{0,8},{4,12},{8,0},{12,4},{1,9},{5,13},{9,1},{13,5},{2,10},{6,14},... | collective-permute-start | bytes 860168 | tf_op jit(solution)/shard_map/ppermute | solution.py:23
  39.2 0.0 collective-permute-done.9
  39.2 1.3 %collective-permute-done.8 = bf16[40,3584]{1,0:T(8,128)(2,1)S(1)} collective-permute-done((bf16[40,3584]{1,0:T(8,128)(2,1)S(1)}, bf16[40,3584]{1,0:T(8,128)(2,1)S(1)}, u32[]{:S(2)}, u32[]{:S(2)}) %collective-permute-start.8) | collective-permute-done | bytes 286752 | tf_op jit(solution)/shard_map/ppermute | solution.py:23
  40.6 0.1 pad_maximum_fusion.rows_ref
  40.7 1.4 %shard_map.112 = (f32[160,1024]{1,0:T(8,128)S(1)}, bf16[160,1024]{1,0:T(8,128)(2,1)S(1)}) custom-call(bf16[160,3584]{1,0:T(8,128)(2,1)S(1)} %pad_maximum_fusion.rows_ref, bf16[3584,512]{1,0:T(8,128)(2,1)S(1)} %get-tuple-element.28.refs_0_, bf16[3584,512]{1,0:T(8,128)(2,1)S(1)} %get-tuple-element.29.refs_1_, bf16[2,2,40,1792]{3,2,1,0:T(8,128)(2,1)S(1)} %bitcast.33), custom_call_target="tpu_custom_call" | custom-call | tf_op jit(solution)/shard_map/pallas_call | solution.py:252
  42.0 2.3 %all-gather.2 = bf16[320,1024]{1,0:T(8,128)(2,1)S(1)} all-gather(bf16[160,1024]{1,0:T(8,128)(2,1)S(1)} %get-tuple-element.35), channel_id=4, replica_groups=mesh['rep'=2,'ep'=4,'node'=2,'sub'=2] {'sub'}, dimensions={0}, use_global_device_ids=true | all-gather | bytes 983040 | tf_op jit(solution)/shard_map/all_gather | solution.py:399
  44.3 0.1 shard_map.113.refs_0_
  44.5 1.3 %collective-permute-start.11 = (bf16[160,512]{1,0:T(8,128)(2,1)S(1)}, bf16[160,512]{1,0:T(8,128)(2,1)S(1)}, u32[]{:S(2)}, u32[]{:S(2)}) collective-permute-start(bf16[160,512]{1,0:T(8,128)(2,1)S(1)} %pad_maximum_fusion.3), channel_id=1, source_target_pairs={{0,2},{2,0},{1,3},{3,1},{4,6},{6,4},{5,7},{7,5},{8,10},{10,8},{9,1... | collective-permute-start | bytes 491528 | tf_op jit(solution)/shard_map/ppermute | solution.py:23
  45.7 5.4 %collective-permute-done.12.refs_3_ = bf16[2,40,1792]{2,1,0:T(8,128)(2,1)S(1)} collective-permute-done((bf16[2,40,1792]{2,1,0:T(8,128)(2,1)S(1)}, bf16[2,40,1792]{2,1,0:T(8,128)(2,1)S(1)}, u32[]{:S(2)}, u32[]{:S(2)}) %collective-permute-start.12) | collective-permute-done | bytes 286752 | tf_op jit(solution)/shard_map/ppermute | solution.py:23
  51.2 0.6 collective-permute-start.16
  51.8 0.8 %shard_map.114 = bf16[160,1792]{1,0:T(8,128)(2,1)S(1)} custom-call(bf16[160,512]{1,0:T(8,128)(2,1)S(1)} %shard_map.113.refs_0_, bf16[160,512]{1,0:T(8,128)(2,1)S(1)} %collective-permute-done.11.refs_1_, bf16[1024,1792]{1,0:T(8,128)(2,1)S(1)} %get-tuple-element.33.refs_2_, bf16[2,40,1792]{2,1,0:T(8,128)(2,1)S(1)} %collective-permute-done.12.refs_3_), custom_call_target="tpu_custom_call" | custom-call | tf_op jit(solution)/shard_map/pallas_call | solution.py:272
  52.7 3.6 %collective-permute-start.13 = (bf16[40,1792]{1,0:T(8,128)(2,1)S(1)}, bf16[40,1792]{1,0:T(8,128)(2,1)S(1)}, u32[]{:S(2)}, u32[]{:S(2)}) collective-permute-start(bf16[40,1792]{1,0:T(8,128)(2,1)S(1)} %get-tuple-element.42), channel_id=1, source_target_pairs={{0,12},{4,8},{8,4},{12,0},{1,13},{5,9},{9,5},{13,1},{2,14},{6,10},... | collective-permute-start | bytes 430088 | tf_op jit(solution)/shard_map/ppermute | solution.py:23
  56.2 0.2 collective-permute-start.14
  56.4 2.4 %collective-permute-start.15 = (bf16[40,1792]{1,0:T(8,128)(2,1)S(1)}, bf16[40,1792]{1,0:T(8,128)(2,1)S(1)}, u32[]{:S(2)}, u32[]{:S(2)}) collective-permute-start(bf16[40,1792]{1,0:T(8,128)(2,1)S(1)} %get-tuple-element.40), channel_id=1, source_target_pairs={{0,14},{2,12},{4,10},{6,8},{8,6},{10,4},{12,2},{14,0},{1,15},{3,13... | collective-permute-start | bytes 430088 | tf_op jit(solution)/shard_map/ppermute | solution.py:39
  58.9 2.4 %collective-permute-done.13.refs_0_ = bf16[40,1792]{1,0:T(8,128)(2,1)S(1)} collective-permute-done((bf16[40,1792]{1,0:T(8,128)(2,1)S(1)}, bf16[40,1792]{1,0:T(8,128)(2,1)S(1)}, u32[]{:S(2)}, u32[]{:S(2)}) %collective-permute-start.13) | collective-permute-done | bytes 143392 | tf_op jit(solution)/shard_map/ppermute | solution.py:23
  61.2 4.8 %collective-permute-done.14.refs_3_ = bf16[40,1792]{1,0:T(8,128)(2,1)S(1)} collective-permute-done((bf16[40,1792]{1,0:T(8,128)(2,1)S(1)}, bf16[40,1792]{1,0:T(8,128)(2,1)S(1)}, u32[]{:S(2)}, u32[]{:S(2)}) %collective-permute-start.14) | collective-permute-done | bytes 143392 | tf_op jit(solution)/shard_map/ppermute | solution.py:23
  66.0 1.5 %collective-permute-done.15.refs_4_ = bf16[40,1792]{1,0:T(8,128)(2,1)S(1)} collective-permute-done((bf16[40,1792]{1,0:T(8,128)(2,1)S(1)}, bf16[40,1792]{1,0:T(8,128)(2,1)S(1)}, u32[]{:S(2)}, u32[]{:S(2)}) %collective-permute-start.15) | collective-permute-done | bytes 143392 | tf_op jit(solution)/shard_map/ppermute | solution.py:39
  67.5 0.6 shard_map.115
  68.1 0.7 collective-permute-done.17.refs_2_
  68.8 1.0 %shard_map.116 = bf16[64,3584]{1,0:T(8,128)(2,1)} custom-call(bf16[4,64,40]{2,1,0:T(8,128)(2,1)S(1)} %get-tuple-element.36.given_ref, f32[64,1792]{1,0:T(8,128)S(1)} %get-tuple-element.37.refs_0_, f32[64,1792]{1,0:T(8,128)S(1)} %get-tuple-element.38.refs_1_, bf16[40,1792]{1,0:T(8,128)(2,1)S(1)} %collective-permute-done.17.refs_2_), custom_call_target="tpu_custom_call" | custom-call | tf_op jit(solution)/shard_map/pallas_call | solution.py:330
  (19 shorter events, 0.2 us)
Async XLA Ops:
  1.6 17.6 %collective-permute-start.1 = (bf16[40,3584]{1,0:T(8,128)(2,1)S(1)}, bf16[40,3584]{1,0:T(8,128)(2,1)S(1)}, u32[]{:S(2)}, u32[]{:S(2)}) collective-permute-start(bf16[40,3584]{1,0:T(8,128)(2,1)S(1)} %get-tuple-element.22.refs_8_), channel_id=1, source_target_pairs={{0,2},{2,0},{1,3},{3,1},{4,6},{6,4},{5,7},{7,5},{8,10},{10,8},{9,1... | collective-permute-start | bytes 860168 | tf_op jit(solution)/shard_map/ppermute | solution.py:23
  4.6 10.5 %collective-permute-start = (bf16[40,1792]{1,0:T(8,128)(2,1)S(1)}, bf16[40,1792]{1,0:T(8,128)(2,1)S(1)}, u32[]{:S(2)}, u32[]{:S(2)}) collective-permute-start(bf16[40,1792]{1,0:T(8,128)(2,1)S(1)} %get-tuple-element.24), channel_id=1, source_target_pairs={{0,8},{4,12},{8,0},{12,4},{1,9},{5,13},{9,1},{13,5},{2,10},{6,14},... | collective-permute-start | bytes 430088 | tf_op jit(solution)/shard_map/ppermute | solution.py:23
  7.2 15.2 %collective-permute-start.3 = (bf16[40,3584]{1,0:T(8,128)(2,1)S(1)}, bf16[40,3584]{1,0:T(8,128)(2,1)S(1)}, u32[]{:S(2)}, u32[]{:S(2)}) collective-permute-start(bf16[40,3584]{1,0:T(8,128)(2,1)S(1)} %get-tuple-element.27), channel_id=1, source_target_pairs={{0,4},{4,0},{8,12},{12,8},{1,5},{5,1},{9,13},{13,9},{2,6},{6,2},{1... | collective-permute-start | bytes 860168 | tf_op jit(solution)/shard_map/ppermute | solution.py:23
  8.8 13.7 %collective-permute-start.4 = (bf16[40,3584]{1,0:T(8,128)(2,1)S(1)}, bf16[40,3584]{1,0:T(8,128)(2,1)S(1)}, u32[]{:S(2)}, u32[]{:S(2)}) collective-permute-start(bf16[40,3584]{1,0:T(8,128)(2,1)S(1)} %get-tuple-element.27), channel_id=1, source_target_pairs={{0,2},{2,0},{1,3},{3,1},{4,6},{6,4},{5,7},{7,5},{8,10},{10,8},{9,1... | collective-permute-start | bytes 860168 | tf_op jit(solution)/shard_map/ppermute | solution.py:23
  9.3 9.8 %collective-permute-start.2 = (bf16[40,1792]{1,0:T(8,128)(2,1)S(1)}, bf16[40,1792]{1,0:T(8,128)(2,1)S(1)}, u32[]{:S(2)}, u32[]{:S(2)}) collective-permute-start(bf16[40,1792]{1,0:T(8,128)(2,1)S(1)} %get-tuple-element.26), channel_id=1, source_target_pairs={{0,8},{4,12},{8,0},{12,4},{1,9},{5,13},{9,1},{13,5},{2,10},{6,14},... | collective-permute-start | bytes 430088 | tf_op jit(solution)/shard_map/ppermute | solution.py:23
  15.0 8.4 %collective-permute-start.5 = (bf16[40,1792]{1,0:T(8,128)(2,1)S(1)}, bf16[40,1792]{1,0:T(8,128)(2,1)S(1)}, u32[]{:S(2)}, u32[]{:S(2)}) collective-permute-start(bf16[40,1792]{1,0:T(8,128)(2,1)S(1)} %shard_map.102.refs_0_), channel_id=1, source_target_pairs={{0,2},{2,0},{1,3},{3,1},{4,6},{6,4},{5,7},{7,5},{8,10},{10,8},{9,1... | collective-permute-start | bytes 430088 | tf_op jit(solution)/shard_map/ppermute | solution.py:23
  19.1 5.1 %collective-permute-start.6 = (bf16[40,1792]{1,0:T(8,128)(2,1)S(1)}, bf16[40,1792]{1,0:T(8,128)(2,1)S(1)}, u32[]{:S(2)}, u32[]{:S(2)}) collective-permute-start(bf16[40,1792]{1,0:T(8,128)(2,1)S(1)} %shard_map.104.refs_0_), channel_id=1, source_target_pairs={{0,2},{2,0},{1,3},{3,1},{4,6},{6,4},{5,7},{7,5},{8,10},{10,8},{9,1... | collective-permute-start | bytes 430088 | tf_op jit(solution)/shard_map/ppermute | solution.py:23
  19.7 11.5 %collective-permute-start.7 = (bf16[40,3584]{1,0:T(8,128)(2,1)S(1)}, bf16[40,3584]{1,0:T(8,128)(2,1)S(1)}, u32[]{:S(2)}, u32[]{:S(2)}) collective-permute-start(bf16[40,3584]{1,0:T(8,128)(2,1)S(1)} %shard_map.109), channel_id=1, source_target_pairs={{0,12},{4,8},{8,4},{12,0},{1,13},{5,9},{9,5},{13,1},{2,14},{6,10},... | collective-permute-start | bytes 860168 | tf_op jit(solution)/shard_map/ppermute | solution.py:23
  28.1 7.1 %collective-permute-start.10 = (bf16[160,512]{1,0:T(8,128)(2,1)S(1)}, bf16[160,512]{1,0:T(8,128)(2,1)S(1)}, u32[]{:S(2)}, u32[]{:S(2)}) collective-permute-start(bf16[160,512]{1,0:T(8,128)(2,1)S(1)} %pad_maximum_fusion.2), channel_id=1, source_target_pairs={{0,2},{2,0},{1,3},{3,1},{4,6},{6,4},{5,7},{7,5},{8,10},{10,8},{9,1... | collective-permute-start | bytes 491528 | tf_op jit(solution)/shard_map/ppermute | solution.py:23
  29.4 9.8 %collective-permute-start.9 = (bf16[40,3584]{1,0:T(8,128)(2,1)S(1)}, bf16[40,3584]{1,0:T(8,128)(2,1)S(1)}, u32[]{:S(2)}, u32[]{:S(2)}) collective-permute-start(bf16[40,3584]{1,0:T(8,128)(2,1)S(1)} %shard_map.105.refs_0_), channel_id=1, source_target_pairs={{0,4},{4,0},{8,12},{12,8},{1,5},{5,1},{9,13},{13,9},{2,6},{6,2},{1... | collective-permute-start | bytes 860168 | tf_op jit(solution)/shard_map/ppermute | solution.py:23
  31.1 9.4 %collective-permute-start.8 = (bf16[40,3584]{1,0:T(8,128)(2,1)S(1)}, bf16[40,3584]{1,0:T(8,128)(2,1)S(1)}, u32[]{:S(2)}, u32[]{:S(2)}) collective-permute-start(bf16[40,3584]{1,0:T(8,128)(2,1)S(1)} %shard_map.110), channel_id=1, source_target_pairs={{0,2},{2,0},{1,3},{3,1},{4,6},{6,4},{5,7},{7,5},{8,10},{10,8},{9,1... | collective-permute-start | bytes 860168 | tf_op jit(solution)/shard_map/ppermute | solution.py:23
  36.0 15.1 %collective-permute-start.12 = (bf16[2,40,1792]{2,1,0:T(8,128)(2,1)S(1)}, bf16[2,40,1792]{2,1,0:T(8,128)(2,1)S(1)}, u32[]{:S(2)}, u32[]{:S(2)}) collective-permute-start(bf16[2,40,1792]{2,1,0:T(8,128)(2,1)S(1)} %slice_bitcast_fusion), channel_id=1, source_target_pairs={{0,8},{4,12},{8,0},{12,4},{1,9},{5,13},{9,1},{13,5},{2,10},{6,14},... | collective-permute-start | bytes 860168 | tf_op jit(solution)/shard_map/ppermute | solution.py:23
  44.5 7.4 %collective-permute-start.11 = (bf16[160,512]{1,0:T(8,128)(2,1)S(1)}, bf16[160,512]{1,0:T(8,128)(2,1)S(1)}, u32[]{:S(2)}, u32[]{:S(2)}) collective-permute-start(bf16[160,512]{1,0:T(8,128)(2,1)S(1)} %pad_maximum_fusion.3), channel_id=1, source_target_pairs={{0,2},{2,0},{1,3},{3,1},{4,6},{6,4},{5,7},{7,5},{8,10},{10,8},{9,1... | collective-permute-start | bytes 491528 | tf_op jit(solution)/shard_map/ppermute | solution.py:23
  51.2 16.3 %collective-permute-start.16 = (bf16[2,40,1792]{2,1,0:T(8,128)(2,1)S(1)}, bf16[2,40,1792]{2,1,0:T(8,128)(2,1)S(1)}, u32[]{:S(2)}, u32[]{:S(2)}) collective-permute-start(bf16[2,40,1792]{2,1,0:T(8,128)(2,1)S(1)} %pad_maximum_fusion.1), channel_id=1, source_target_pairs={{0,2},{2,0},{1,3},{3,1},{4,6},{6,4},{5,7},{7,5},{8,10},{10,8},{9,1... | collective-permute-start | bytes 860168 | tf_op jit(solution)/shard_map/ppermute | solution.py:23
  52.7 8.6 %collective-permute-start.13 = (bf16[40,1792]{1,0:T(8,128)(2,1)S(1)}, bf16[40,1792]{1,0:T(8,128)(2,1)S(1)}, u32[]{:S(2)}, u32[]{:S(2)}) collective-permute-start(bf16[40,1792]{1,0:T(8,128)(2,1)S(1)} %get-tuple-element.42), channel_id=1, source_target_pairs={{0,12},{4,8},{8,4},{12,0},{1,13},{5,9},{9,5},{13,1},{2,14},{6,10},... | collective-permute-start | bytes 430088 | tf_op jit(solution)/shard_map/ppermute | solution.py:23
  56.2 9.8 %collective-permute-start.14 = (bf16[40,1792]{1,0:T(8,128)(2,1)S(1)}, bf16[40,1792]{1,0:T(8,128)(2,1)S(1)}, u32[]{:S(2)}, u32[]{:S(2)}) collective-permute-start(bf16[40,1792]{1,0:T(8,128)(2,1)S(1)} %get-tuple-element.41), channel_id=1, source_target_pairs={{0,4},{4,0},{8,12},{12,8},{1,5},{5,1},{9,13},{13,9},{2,6},{6,2},{1... | collective-permute-start | bytes 430088 | tf_op jit(solution)/shard_map/ppermute | solution.py:23
  56.4 11.1 %collective-permute-start.15 = (bf16[40,1792]{1,0:T(8,128)(2,1)S(1)}, bf16[40,1792]{1,0:T(8,128)(2,1)S(1)}, u32[]{:S(2)}, u32[]{:S(2)}) collective-permute-start(bf16[40,1792]{1,0:T(8,128)(2,1)S(1)} %get-tuple-element.40), channel_id=1, source_target_pairs={{0,14},{2,12},{4,10},{6,8},{8,6},{10,4},{12,2},{14,0},{1,15},{3,13... | collective-permute-start | bytes 430088 | tf_op jit(solution)/shard_map/ppermute | solution.py:39
  58.8 10.0 %collective-permute-start.17 = (bf16[40,1792]{1,0:T(8,128)(2,1)S(1)}, bf16[40,1792]{1,0:T(8,128)(2,1)S(1)}, u32[]{:S(2)}, u32[]{:S(2)}) collective-permute-start(bf16[40,1792]{1,0:T(8,128)(2,1)S(1)} %get-tuple-element.39), channel_id=1, source_target_pairs={{0,6},{2,4},{4,2},{6,0},{8,14},{10,12},{12,10},{14,8},{1,7},{3,5},... | collective-permute-start | bytes 430088 | tf_op jit(solution)/shard_map/ppermute | solution.py:39
